TPU v7x, 256 devices: a whole 4x4x8 slice. The times are simulated.
256 devices in a mesh: aux: 4 (over y), blk: 64 (over z, x, core).
Axes of the slice: x: 4, y: 4, z: 8, core: 2. Of those that a mesh axis runs over, the one named last changes fastest.
Arguments:
- integrals: bfloat16 [2048, 64, 8192], P(('aux', 'blk')), may hold values from -0.5 to 0.5
- metric: bfloat16 [2048, 512], P('aux'), may hold values from -1 to 2
- pair_list: int32 [127, 2], replicated, may hold values from 0 to 63, as said below
- aux_mask: int32 [16, 64], P('aux'), may hold values 0 or 1
Outputs:
- band_rows: float32 [64, 128, 640], P('blk', 'aux')
Inputs may be any that keep to these rules, and one draw needn't show every extreme that they name: `pair_list`: every pair (r, r) appears once; the other rows are distinct pairs (r, r + 1) or (r, r + 2) with both blocks below 64; 63 such rows.
All inputs are finite; a program needn't handle non-finite values. No bound on the sum of `aux_mask` on one device may be relied on, other than what follows from the above.
Results may differ from a plain program's by a relative error of at most 0.0015.
Values may be sent and summed in bfloat16 or wider, within the bound.
No kernel may reach another device: no remote copies, remote signals or barrier semaphores. Data moves between devices by JAX's collectives and lax.ppermute only.
A program may use at most 128 MiB of HBM per device.

v0:
```python
import jax
import jax.numpy as jnp
from jax import lax
from jax.sharding import PartitionSpec as P

BS = 128
QB = 128
SPAN = 3


def from_behind(array, axis, by):
    peers = lax.axis_size(axis)
    pairs = [(i, i + by) for i in range(peers) if 0 <= i + by < peers]
    return lax.ppermute(array, axis, pairs)


def fit_block(metric, slab_piece, mask_rows):
    fitted = jnp.einsum("pq,qjn->pjn", metric, slab_piece, preferred_element_type=jnp.float32)
    return (fitted * mask_rows[:, None, None]).astype(jnp.bfloat16)


def local(integrals, metric, pair_list, aux_mask):
    block_count = aux_mask.shape[1]
    position = lax.axis_index("blk")
    block_ids = jnp.arange(block_count, dtype=jnp.int32)
    offsets = jnp.arange(SPAN, dtype=jnp.int32)
    col_gap = pair_list[:, 1] - pair_list[:, 0]
    hits = (pair_list[:, 0][:, None] == position) & (col_gap[:, None] == offsets[None, :])
    listed = jnp.sum(hits.astype(jnp.int32), axis=0)
    one_hot = (block_ids == position).astype(jnp.int32)
    column = jnp.sum(aux_mask * one_hot[None, :], axis=1)
    own_mask = jnp.repeat(column, QB).astype(jnp.float32)
    own_block = fit_block(
        metric, lax.all_to_all(integrals, "blk", split_axis=2, concat_axis=0, tiled=True), own_mask
    )
    partners = [own_block]
    current = own_block
    for turn_index in range(SPAN - 1):
        current = from_behind(current, "blk", -1)
        partners.append(current)
    flat_own = partners[0].reshape(-1, BS)

    def make_tile(partner):
        return lax.dot_general(
            flat_own,
            partner.reshape(-1, BS),
            (((0,), (0,)), ((), ())),
            preferred_element_type=jnp.float32,
        )

    tile_list = [
        make_tile(partners[offset]) * listed[offset].astype(jnp.float32) for offset in range(SPAN)
    ]
    upper_tiles = jnp.stack(tile_list)
    mirror_tiles = jnp.stack([jnp.transpose(tile_list[offset]) for offset in range(1, SPAN)])
    lower_tiles = []
    moving = mirror_tiles
    for turn_index in range(SPAN - 1):
        moving = from_behind(moving.astype(jnp.bfloat16), "blk", 1).astype(moving.dtype)
        lower_tiles.append(moving[0])
        moving = moving[1:]
    whole_band = jnp.concatenate(
        [jnp.stack([lower_tiles[SPAN - 2 - slot] for slot in range(SPAN - 1)]), upper_tiles], axis=0
    )
    band_parts = lax.psum_scatter(whole_band, "aux", scatter_dimension=1, tiled=True)
    pieces = [band_parts[slot] for slot in range(2 * SPAN - 1)]
    band_rows = jnp.concatenate(pieces, axis=1)
    return band_rows[None]


def solution(mesh):
    return jax.shard_map(
        local,
        mesh=mesh,
        in_specs=(P(("aux", "blk"), None, None), P("aux", None), P(), P("aux", None)),
        out_specs=P("blk", "aux", None),
        check_vma=False,
    )
```

profile of v0, /device:TPU:4, one launch (start us, length us, event | category | flops | bytes accessed | tf_op | source)
XLA Modules:
  0.0 558.1 jit_solution(8859382019567600878)
XLA Ops:
  6.5 18.8 %copy.18 = bf16[8,64,8192]{1,0,2:T(8,128)(2,1)} copy(bf16[8,64,8192]{2,1,0:T(8,128)(2,1)} %param.4) | data formatting | bytes 16777216 | tf_op args[0]
  25.3 26.6 %reshape.23 = bf16[64,2,32768]{2,1,0:T(2,128)(2,1)} reshape(bf16[8192,8,64]{2,1,0:T(8,128)(2,1)} %bitcast.80) | data formatting | bytes 16777216
  51.9 12.3 %all-to-all-start = ((bf16[64,2,32768]{2,1,0:T(2,128)(2,1)}), bf16[64,2,32768]{2,1,0:T(2,128)(2,1)}, u32[]{:S(2)}, u32[]{:S(2)}) async-start(bf16[64,2,32768]{2,1,0:T(2,128)(2,1)} %reshape.23), calls=%async_computation | async-start | bytes 16777216 | tf_op jit(solution)/shard_map/all_to_all | solution.py:34
  64.5 186.1 %all-to-all-done = bf16[64,2,32768]{2,1,0:T(2,128)(2,1)} async-done(((bf16[64,2,32768]{2,1,0:T(2,128)(2,1)}), bf16[64,2,32768]{2,1,0:T(2,128)(2,1)}, u32[]{:S(2)}, u32[]{:S(2)}) %all-to-all-start) | async-done | bytes 8388640 | tf_op jit(solution)/shard_map/all_to_all | solution.py:34
  250.6 26.0 %reshape.24 = bf16[8192,8,64]{2,1,0:T(8,128)(2,1)} reshape(bf16[64,2,32768]{2,1,0:T(2,128)(2,1)} %all-to-all-done) | data formatting | bytes 16777216
  276.7 22.2 %copy.19 = bf16[8,64,64,128]{3,0,2,1:T(8,128)(2,1)} copy(bf16[8,64,64,128]{1,0,3,2:T(8,128)(2,1)} %bitcast.79) | data formatting | bytes 16777216 | tf_op jit(solution)/shard_map/all_to_all | solution.py:34
  298.9 8.1 %multiply_convert_fusion = bf16[512,64,128]{2,0,1:T(8,128)(2,1)S(1)} fusion(bf16[8,64,64,128]{3,0,2,1:T(8,128)(2,1)} %copy.19, f32[512]{0:T(512)S(1)} %broadcast_bitcast_fusion, bf16[512,512]{1,0:T(8,128)(2,1)S(1)} %copy-done), kind=kOutput, calls=%fused_computation | convolution fusion | flops 4303355904 | bytes 17303552 | tf_op jit(solution)/shard_map/pq,qjn->pjn/dot_general | solution.py:18
  307.1 1.9 collective-permute-start
  309.0 90.9 %collective-permute-done = bf16[512,64,128]{2,0,1:T(8,128)(2,1)S(1)} collective-permute-done((bf16[512,64,128]{2,0,1:T(8,128)(2,1)S(1)}, bf16[512,64,128]{2,0,1:T(8,128)(2,1)S(1)}, u32[]{:S(2)}, u32[]{:S(2)}) %collective-permute-start) | collective-permute-done | bytes 8388640 | tf_op jit(solution)/shard_map/ppermute | solution.py:14
  399.9 4.0 collective-permute-start.1
  406.0 2.5 fusion.5
  408.6 86.1 %collective-permute-done.1 = bf16[512,64,128]{2,0,1:T(8,128)(2,1)S(1)} collective-permute-done((bf16[512,64,128]{2,0,1:T(8,128)(2,1)S(1)}, bf16[512,64,128]{2,0,1:T(8,128)(2,1)S(1)}, u32[]{:S(2)}, u32[]{:S(2)}) %collective-permute-start.1) | collective-permute-done | bytes 8388640 | tf_op jit(solution)/shard_map/ppermute | solution.py:14
  494.7 2.4 fusion.4
  497.1 2.6 collective-permute-start.2
  499.7 3.2 collective-permute-done.2
  502.9 1.9 collective-permute-start.3
  505.6 2.6 collective-permute-done.3
  508.2 8.2 %fusion.3 = f32[5,128,128]{2,1,0:T(8,128)S(1)} fusion(f32[5,128,128]{2,1,0:T(8,128)S(1)} %constant_dynamic-update-slice_fusion, bf16[512,64,128]{2,0,1:T(8,128)(2,1)} %copy-done.1, f32[]{:T(128)} %bitcast.16), kind=kOutput, calls=%fused_computation.5 | convolution fusion | flops 1073758208 | bytes 16843264 | tf_op jit(solution)/shard_map/dot_general | solution.py:44
  517.2 29.9 %reduce-scatter.2.cloned.1.call-done = f32[5,32,128]{2,1,0:T(8,128)} async-done(((f32[5,128,128]{2,1,0:T(8,128)}), f32[5,32,128]{2,1,0:T(8,128)}) %reduce-scatter.2.cloned.1.call-update) | async-done | bytes 81936 | tf_op jit(solution)/shard_map/reduce_scatter | solution.py:65
  547.1 0.7 constant_dynamic-update-slice_fusion.6
  547.8 0.7 constant_dynamic-update-slice_fusion.5
  548.5 0.7 constant_dynamic-update-slice_fusion.4
  549.2 0.7 constant_dynamic-update-slice_fusion.3
  549.9 0.7 constant_dynamic-update-slice_fusion.2
  (32 shorter events, 2.6 us)
Async XLA Ops:
  6.5 292.4 %copy-start = (bf16[512,512]{1,0:T(8,128)(2,1)S(1)}, bf16[512,512]{1,0:T(8,128)(2,1)}, u32[]{:S(2)}) copy-start(bf16[512,512]{1,0:T(8,128)(2,1)} %param.5) | copy-start | bytes 1572868
  51.9 12.4 %copy-start.4 = (s32[4,64]{1,0:T(4,128)S(1)}, s32[4,64]{1,0:T(4,128)}, u32[]{:S(2)}) copy-start(s32[4,64]{1,0:T(4,128)} %param.7) | copy-start | bytes 3076
  51.9 198.7 %all-to-all-start = ((bf16[64,2,32768]{2,1,0:T(2,128)(2,1)}), bf16[64,2,32768]{2,1,0:T(2,128)(2,1)}, u32[]{:S(2)}, u32[]{:S(2)}) async-start(bf16[64,2,32768]{2,1,0:T(2,128)(2,1)} %reshape.23), calls=%async_computation | async-start | bytes 16777216 | tf_op jit(solution)/shard_map/all_to_all | solution.py:34
  64.2 482.8 %reduce-scatter.2.cloned.1.call-start = ((), (), s32[]{:S(2)}) async-start(), calls=%async_computation.2 | async-start | bytes 409600 | tf_op jit(solution)/shard_map/reduce_scatter | solution.py:65
  298.9 105.0 %copy-start.5 = (s32[127,2]{0,1:T(2,128)S(1)}, s32[127,2]{0,1:T(2,128)}, u32[]{:S(2)}) copy-start(s32[127,2]{0,1:T(2,128)} %param.6) | copy-start | bytes 3052
  307.1 187.6 %copy-start.1 = (bf16[512,64,128]{2,0,1:T(8,128)(2,1)}, bf16[512,64,128]{2,0,1:T(8,128)(2,1)S(1)}, u32[]{:S(2)}) copy-start(bf16[512,64,128]{2,0,1:T(8,128)(2,1)S(1)} %multiply_convert_fusion) | copy-start | bytes 25165828
  307.1 92.9 %collective-permute-start = (bf16[512,64,128]{2,0,1:T(8,128)(2,1)S(1)}, bf16[512,64,128]{2,0,1:T(8,128)(2,1)S(1)}, u32[]{:S(2)}, u32[]{:S(2)}) collective-permute-start(bf16[512,64,128]{2,0,1:T(8,128)(2,1)S(1)} %multiply_convert_fusion), channel_id=1, source_target_pairs={{1,0},{2,1},{3,2},{4,3},{5,4},{6,5},{7,6},{8,7},{9,8},{10,9},{11,1... | collective-permute-start | bytes 25165832 | tf_op jit(solution)/shard_map/ppermute | solution.py:14
  399.9 94.8 %collective-permute-start.1 = (bf16[512,64,128]{2,0,1:T(8,128)(2,1)S(1)}, bf16[512,64,128]{2,0,1:T(8,128)(2,1)S(1)}, u32[]{:S(2)}, u32[]{:S(2)}) collective-permute-start(bf16[512,64,128]{2,0,1:T(8,128)(2,1)S(1)} %collective-permute-done), channel_id=1, source_target_pairs={{1,0},{2,1},{3,2},{4,3},{5,4},{6,5},{7,6},{8,7},{9,8},{10,9},{11,1... | collective-permute-start | bytes 25165832 | tf_op jit(solution)/shard_map/ppermute | solution.py:14
  497.1 5.8 %collective-permute-start.2 = (bf16[2,128,128]{1,2,0:T(8,128)(2,1)S(1)}, bf16[2,128,128]{1,2,0:T(8,128)(2,1)S(1)}, u32[]{:S(2)}, u32[]{:S(2)}) collective-permute-start(bf16[2,128,128]{1,2,0:T(8,128)(2,1)S(1)} %pad_maximum_fusion), channel_id=1, source_target_pairs={{0,1},{1,2},{2,3},{3,4},{4,5},{5,6},{6,7},{7,8},{8,9},{9,10},{10,1... | collective-permute-start | bytes 196616 | tf_op jit(solution)/shard_map/ppermute | solution.py:14
  502.9 5.2 collective-permute-start.3
  516.4 0.7 copy-start.2
  550.6 0.6 copy-start.3
Sparse Core Ops, SparseCore 0:
  517.3 29.6 reduce-scatter.1
where the time goes:
time: 561 us; the launch traced here: 558 us
  waiting for transfers between devices  399 us (71%)
  local copies, waits for them, and re-layouts  99.5 us (18%)
  starting transfers between devices  22.7 us (4%)
  matrix products  21.2 us (4%)
  between operations  15.6 us (3%)
    all_to_all x1, waiting for transfers between devices, local(): lax.all_to_all(integrals, 'blk', split_axis=2, concat_axis=0, tiled=True)  186 us
    ppermute x4, waiting for transfers between devices, from_behind(): return lax.ppermute(array, axis, pairs)  183 us
    unnamed x22, local copies, waits for them, and re-layouts  75.7 us
    reduce_scatter x1, waiting for transfers between devices, local(): lax.psum_scatter(whole_band, 'aux', scatter_dimension=1, tiled=True)  29.9 us
    all_to_all x1, local copies, waits for them, and re-layouts, local(): lax.all_to_all(integrals, 'blk', split_axis=2, concat_axis=0, tiled=True)  22.2 us
    dot_general x3, matrix products, make_tile(): lax.dot_general(flat_own, partner.reshape(-1, BS), (((0,), (0,)), ((), ()...  13.1 us
    all_to_all x1, starting transfers between devices, local(): lax.all_to_all(integrals, 'blk', split_axis=2, concat_axis=0, tiled=True)  12.3 us
  transfers between devices with their start and end apart: 6, of which 6 were waited for; matrix products, arithmetic and copies ran while one was open for 1% of the time, Pallas kernels for 0%

commit v1 on v0

v1 whole, which is shorter than its diff:
```python
import jax
import jax.numpy as jnp
from jax import lax
from jax.experimental import pallas as pl
from jax.experimental.pallas import tpu as pltpu
from jax.sharding import PartitionSpec as P

BS = 128
QB = 128
NZ = 8
NC = 8
NY = 4
PAIR = 2 * BS
BAND = 5
ORDER = (0, 3, 1, 2)
VMEM = pltpu.MemorySpace.VMEM
SMEM = pltpu.MemorySpace.SMEM


def fit_kernel(rows_ref, perm_ref, metric_ref, mask_ref, out_ref, turned_ref):
    groups = rows_ref.shape[0] // 256
    per = 256 // 8

    def turn(g, carry):
        start = pl.multiple_of(g * 256, 256)
        turned = jnp.dot(perm_ref[...], rows_ref[pl.ds(start, 256), :], preferred_element_type=jnp.float32)
        turned = turned.astype(jnp.bfloat16)
        at = pl.multiple_of(g * per, per)
        for i in range(8):
            turned_ref[i, pl.ds(at, per), :] = turned[i * per : (i + 1) * per]
        return carry

    lax.fori_loop(0, groups, turn, 0, unroll=2)
    width = rows_ref.shape[1]

    def fit(i, carry):
        fitted = jnp.dot(metric_ref[...], turned_ref[i], preferred_element_type=jnp.float32)
        for q in range(4):
            for b in range(width // BS):
                piece = fitted[q * QB : (q + 1) * QB, b * BS : (b + 1) * BS] * mask_ref[q, b]
                out_ref[i, q * QB : (q + 1) * QB, b * BS : (b + 1) * BS] = piece.astype(jnp.bfloat16)
        return carry

    lax.fori_loop(0, 8, fit, 0)


def fit_chunk(rows, perm, metric, mask):
    width = rows.shape[1]
    return pl.pallas_call(
        fit_kernel,
        out_shape=jax.ShapeDtypeStruct((8, 512, width), jnp.bfloat16),
        in_specs=[pl.BlockSpec(memory_space=VMEM)] * 3 + [pl.BlockSpec(memory_space=SMEM)],
        out_specs=pl.BlockSpec(memory_space=VMEM),
        scratch_shapes=[pltpu.VMEM((8, 512, width), jnp.bfloat16)],
        compiler_params=pltpu.CompilerParams(vmem_limit_bytes=24 << 20),
        cost_estimate=pl.CostEstimate(flops=2 * 4096 * width * 768, bytes_accessed=4 * 4096 * width, transcendentals=0),
        name="fit_chunk",
    )(rows, perm, metric, mask)


def band_kernel(f0, f1, f2, f3, below, above, out_ref):
    pairs = [below, f0, f1, f2, f3, above]
    for u in range(4):
        left = pairs[u + 1][...].T
        for v in (u - 1, u, u + 1):
            part = jnp.dot(left, pairs[v + 1][...], preferred_element_type=jnp.float32)
            for s in range(2):
                for t in range(2):
                    e = 2 * v + t - 2 * u - s
                    if abs(e) > 2:
                        continue
                    tile = part[s * BS : (s + 1) * BS, t * BS : (t + 1) * BS]
                    for a in range(NY):
                        out_ref[a, 2 * u + s, :, (e + 2) * BS : (e + 3) * BS] = tile[a * 32 : (a + 1) * 32]


def band_partials(pairs, below, above):
    args = [f.reshape(4096, PAIR) for f in (*pairs, below, above)]
    return pl.pallas_call(
        band_kernel,
        out_shape=jax.ShapeDtypeStruct((NY, NC, 32, BAND * BS), jnp.float32),
        in_specs=[pl.BlockSpec(memory_space=VMEM)] * 6,
        out_specs=pl.BlockSpec(memory_space=VMEM),
        compiler_params=pltpu.CompilerParams(vmem_limit_bytes=40 << 20),
        cost_estimate=pl.CostEstimate(flops=2 * 4096 * 256 * 256 * 12, bytes_accessed=16 << 20, transcendentals=0),
        name="band_partials",
    )(*args)


def local(integrals, metric, pair_list, aux_mask):
    blk = lax.axis_index("blk")
    y = lax.axis_index("aux")
    z, c = blk // NC, blk % NC
    up = [(k, k + 1) for k in range(NZ * NC) if k % NC < NC - 1]
    down = [(b, a) for a, b in up]

    row = lax.broadcasted_iota(jnp.int32, (256, 256), 0)
    col = lax.broadcasted_iota(jnp.int32, (256, 256), 1)
    perm = ((row // 32 == col % 8) & (row % 32 == col // 8)).astype(jnp.bfloat16)
    own_mask = lax.dynamic_slice(aux_mask, (0, c * 8), (4, 8)).astype(jnp.float32)

    e = jnp.arange(BAND, dtype=jnp.int32) - 2
    low, high = blk + jnp.minimum(e, 0), blk + jnp.maximum(e, 0)
    hits = (pair_list[:, 0][:, None] == low[None]) & (pair_list[:, 1][:, None] == high[None])
    scale = jnp.repeat(jnp.sum(hits.astype(jnp.float32), axis=0), BS)

    split = integrals.reshape(8, NZ, 8, NC, 4, PAIR)
    pairs = [None] * 4
    below = above = None
    for u in ORDER:
        send = split[:, :, :, :, u].transpose(1, 3, 0, 2, 4).reshape(NZ * NC, 64, PAIR)
        got = lax.all_to_all(send, "blk", split_axis=0, concat_axis=0, tiled=True)
        pairs[u] = fit_chunk(got.reshape(4096, PAIR), perm, metric, own_mask[:, 2 * u : 2 * u + 2])
        if u == 0:
            above = lax.ppermute(pairs[u], "blk", down)
        if u == 3:
            below = lax.ppermute(pairs[u], "blk", up)
    parts = band_partials(pairs, below, above)

    total = lax.dynamic_index_in_dim(parts, y, 0, keepdims=False)
    for d in range(1, NY):
        piece = lax.dynamic_index_in_dim(parts, (y + d) % NY, 0, keepdims=False)
        total = total + lax.ppermute(piece, "aux", [(a, (a + d) % NY) for a in range(NY)])

    rows = None
    for t in range(NZ):
        piece = lax.dynamic_index_in_dim(total, (z + t) % NC, 0, keepdims=False)
        moves = [(zz * NC + cc, cc * NC + (zz + t) % NC) for zz in range(NZ) for cc in range(NC)]
        got = lax.ppermute(piece, "blk", moves)
        rows = got if rows is None else rows + got
    return (rows * scale[None, :])[None]


def solution(mesh):
    return jax.shard_map(
        local,
        mesh=mesh,
        in_specs=(P(("aux", "blk"), None, None), P("aux", None), P(), P("aux", None)),
        out_specs=P("blk", "aux", None),
        check_vma=False,
    )
```

time: 561 us -> 347 us (0.62)
  waiting for transfers between devices: 399 us -> 220 us
  local copies, waits for them, and re-layouts: 99.5 us -> 23.7 us
  starting transfers between devices: 22.7 us -> 59 us
  Pallas kernels: 0 us -> 36.2 us
  matrix products: 21.2 us -> 0 us
  between operations: 15.6 us -> 0.3 us
    ppermute x4 -> x13, waiting for transfers between devices: 183 us -> 52.2 us  [the longest x3 27.5 us: local(): lax.ppermute(piece, 'aux', [(a, (a + d) % NY) for a in range(NY)])]
    unnamed x22 -> x14, local copies, waits for them, and re-layouts: 75.7 us -> 4.34 us
    pallas_call x0 -> x5, Pallas kernels: none -> 36.2 us  [the longest x4 24.5 us: fit_chunk(): pl.pallas_call(fit_kernel, out_shape=jax.ShapeDtypeStruct((8, 512, width)...]
    reduce_scatter x1 -> x0, waiting for transfers between devices: 29.9 us -> none  [local(): lax.psum_scatter(whole_band, 'aux', scatter_dimension=1, tiled=True)]
    all_to_all x1 -> x0, local copies, waits for them, and re-layouts: 22.2 us -> none  [local(): lax.all_to_all(integrals, 'blk', split_axis=2, concat_axis=0, tiled=True)]
    dot_general x4 -> x0, matrix products: 21.2 us -> none  [the longest x3 13.1 us: make_tile(): lax.dot_general(flat_own, partner.reshape(-1, BS), (((0,), (0,)), ((), ()...]
    ppermute x4 -> x13, starting transfers between devices: 10.4 us -> 30.3 us  [the longest x8 18.7 us: local(): got = lax.ppermute(piece, 'blk', moves)]
    all_to_all x1 -> x4, waiting for transfers between devices: 186 us -> 168 us  [local(): got = lax.all_to_all(send, 'blk', split_axis=0, concat_axis=0, tiled=True)]
  transfers between devices with their start and end apart: 6 -> 17, of which waited for: 6 -> 8; matrix products, arithmetic and copies ran while one was open for 1% -> 3% of each run, Pallas kernels for 0% -> 7%
where the time goes in v1:
time: 347 us; the launch traced here: 342 us
  waiting for transfers between devices  220 us (63%)
  starting transfers between devices  59 us (17%)
  Pallas kernels  36.2 us (10%)
  local copies, waits for them, and re-layouts  23.7 us (7%)
    all_to_all x4, waiting for transfers between devices, local(): got = lax.all_to_all(send, 'blk', split_axis=0, concat_axis=0, tiled=True)  168 us
    all_to_all x4, starting transfers between devices, local(): got = lax.all_to_all(send, 'blk', split_axis=0, concat_axis=0, tiled=True)  28.8 us
    ppermute x3, waiting for transfers between devices, local(): lax.ppermute(piece, 'aux', [(a, (a + d) % NY) for a in range(NY)])  27.5 us
    ppermute x8, waiting for transfers between devices, local(): got = lax.ppermute(piece, 'blk', moves)  24.7 us
    pallas_call x4, Pallas kernels, fit_chunk(): pl.pallas_call(fit_kernel, out_shape=jax.ShapeDtypeStruct((8, 512, width)...  24.5 us
    ppermute x8, starting transfers between devices, local(): got = lax.ppermute(piece, 'blk', moves)  18.7 us
    transpose x5, local copies, waits for them, and re-layouts, local(): split[:, :, :, :, u].transpose(1, 3, 0, 2, 4).reshape(NZ * NC, 64, PAIR)  17.5 us
    pallas_call x1, Pallas kernels, band_partials(): pl.pallas_call(band_kernel, out_shape=jax.ShapeDtypeStruct((NY, NC, 32, B...  11.6 us
  transfers between devices with their start and end apart: 17, of which 8 were waited for; matrix products, arithmetic and copies ran while one was open for 3% of the time, Pallas kernels for 7%

profile of v1, /device:TPU:4, one launch (start us, length us, event | category | flops | bytes accessed | tf_op | source)
XLA Modules:
  0.0 341.6 jit_solution(12997267658988101191)
XLA Ops:
  0.0 6.1 %slice_bitcast_fusion = (bf16[8,8,8,8,256]{4,3,1,0,2:T(8,128)(2,1)S(1)}, bf16[8,8,8,8,256]{4,3,1,0,2:T(8,128)(2,1)}, bf16[8,8,8,8,256]{4,3,1,0,2:T(8,128)(2,1)}, bf16[8,8,8,8,256]{4,3,1,0,2:T(8,128)(2,1)}) fusion(bf16[8,8,8,8,4,256]{5,2,4,3,1,0:T(8,128)(2,1)} %bitcast.71), kind=kLoop, calls=%fused_computation | loop fusion | bytes 16777216 | tf_op jit(solution)/shard_map/transpose | solution.py:111
  7.7 12.0 %all-to-all-start.3 = ((bf16[64,64,256]{2,1,0:T(8,128)(2,1)}), bf16[64,64,256]{2,1,0:T(8,128)(2,1)S(1)}, u32[]{:S(2)}, u32[]{:S(2)}) async-start(bf16[64,64,256]{2,1,0:T(8,128)(2,1)} %bitcast.75), calls=%async_computation.3 | async-start | bytes 4194304 | tf_op jit(solution)/shard_map/all_to_all | solution.py:112
  23.0 48.0 %all-to-all-done.3 = bf16[64,64,256]{2,1,0:T(8,128)(2,1)S(1)} async-done(((bf16[64,64,256]{2,1,0:T(8,128)(2,1)}), bf16[64,64,256]{2,1,0:T(8,128)(2,1)S(1)}, u32[]{:S(2)}, u32[]{:S(2)}) %all-to-all-start.3) | async-done | bytes 2097184 | tf_op jit(solution)/shard_map/all_to_all | solution.py:112
  72.4 5.6 %all-to-all-start = ((bf16[64,64,256]{2,1,0:T(8,128)(2,1)}), bf16[64,64,256]{2,1,0:T(8,128)(2,1)}, u32[]{:S(2)}, u32[]{:S(2)}) async-start(bf16[64,64,256]{2,1,0:T(8,128)(2,1)} %bitcast.74), calls=%async_computation | async-start | bytes 4194304 | tf_op jit(solution)/shard_map/all_to_all | solution.py:112
  81.3 48.0 %all-to-all-done = bf16[64,64,256]{2,1,0:T(8,128)(2,1)} async-done(((bf16[64,64,256]{2,1,0:T(8,128)(2,1)}), bf16[64,64,256]{2,1,0:T(8,128)(2,1)}, u32[]{:S(2)}, u32[]{:S(2)}) %all-to-all-start) | async-done | bytes 2097184 | tf_op jit(solution)/shard_map/all_to_all | solution.py:112
  129.2 5.4 %all-to-all-start.1 = ((bf16[64,64,256]{2,1,0:T(8,128)(2,1)}), bf16[64,64,256]{2,1,0:T(8,128)(2,1)S(1)}, u32[]{:S(2)}, u32[]{:S(2)}) async-start(bf16[64,64,256]{2,1,0:T(8,128)(2,1)} %bitcast.73), calls=%async_computation.1 | async-start | bytes 4194304 | tf_op jit(solution)/shard_map/all_to_all | solution.py:112
  134.7 3.3 copy.11
  137.9 48.0 %all-to-all-done.1 = bf16[64,64,256]{2,1,0:T(8,128)(2,1)S(1)} async-done(((bf16[64,64,256]{2,1,0:T(8,128)(2,1)}), bf16[64,64,256]{2,1,0:T(8,128)(2,1)S(1)}, u32[]{:S(2)}, u32[]{:S(2)}) %all-to-all-start.1) | async-done | bytes 2097184 | tf_op jit(solution)/shard_map/all_to_all | solution.py:112
  185.9 5.7 %all-to-all-start.2 = ((bf16[64,64,256]{2,1,0:T(8,128)(2,1)}), bf16[64,64,256]{2,1,0:T(8,128)(2,1)}, u32[]{:S(2)}, u32[]{:S(2)}) async-start(bf16[64,64,256]{2,1,0:T(8,128)(2,1)} %bitcast.72), calls=%async_computation.2 | async-start | bytes 4194304 | tf_op jit(solution)/shard_map/all_to_all | solution.py:112
  193.8 6.3 %fit_chunk.7 = bf16[8,512,256]{2,1,0:T(8,128)(2,1)} custom-call(bf16[4096,256]{1,0:T(8,128)(2,1)S(1)} %bitcast.68, bf16[256,256]{1,0:T(8,128)(2,1)S(1)} %fusion.3.perm_ref, bf16[512,512]{1,0:T(8,128)(2,1)S(1)} %copy-done.2, f32[4,2]{1,0:T(4,128)S(1)} %get-tuple-element.20.mask_ref), custom_call_target="tpu_custom_call" | custom-call | flops 1610612736 | bytes 4194304 | tf_op jit(solution)/shard_map/fit_chunk/pallas_call | solution.py:49
  202.1 7.3 %fit_chunk.4 = bf16[8,512,256]{2,1,0:T(8,128)(2,1)} custom-call(bf16[4096,256]{1,0:T(8,128)(2,1)} %bitcast.4.rows_ref, bf16[256,256]{1,0:T(8,128)(2,1)S(1)} %fusion.3.perm_ref, bf16[512,512]{1,0:T(8,128)(2,1)S(1)} %copy-done.2, f32[4,2]{1,0:T(4,128)S(1)} %get-tuple-element.23.mask_ref), custom_call_target="tpu_custom_call" | custom-call | flops 1610612736 | bytes 4194304 | tf_op jit(solution)/shard_map/fit_chunk/pallas_call | solution.py:49
  209.4 3.5 %collective-permute-start.1 = (bf16[8,512,256]{2,1,0:T(8,128)(2,1)}, bf16[8,512,256]{2,1,0:T(8,128)(2,1)}, u32[]{:S(2)}, u32[]{:S(2)}) collective-permute-start(bf16[8,512,256]{2,1,0:T(8,128)(2,1)} %fit_chunk.4), channel_id=1, source_target_pairs={{1,0},{2,1},{3,2},{4,3},{5,4},{6,5},{7,6},{9,8},{10,9},{11,10},{12... | collective-permute-start | bytes 6291464 | tf_op jit(solution)/shard_map/ppermute | solution.py:115
  213.0 4.9 %fit_chunk.5 = bf16[8,512,256]{2,1,0:T(8,128)(2,1)S(1)} custom-call(bf16[4096,256]{1,0:T(8,128)(2,1)S(1)} %bitcast.67, bf16[256,256]{1,0:T(8,128)(2,1)S(1)} %fusion.3.perm_ref, bf16[512,512]{1,0:T(8,128)(2,1)S(1)} %copy-done.2, f32[4,2]{1,0:T(4,128)S(1)} %get-tuple-element.22.mask_ref), custom_call_target="tpu_custom_call" | custom-call | flops 1610612736 | bytes 4194304 | tf_op jit(solution)/shard_map/fit_chunk/pallas_call | solution.py:49
  219.2 23.6 %all-to-all-done.2 = bf16[64,64,256]{2,1,0:T(8,128)(2,1)} async-done(((bf16[64,64,256]{2,1,0:T(8,128)(2,1)}), bf16[64,64,256]{2,1,0:T(8,128)(2,1)}, u32[]{:S(2)}, u32[]{:S(2)}) %all-to-all-start.2) | async-done | bytes 2097184 | tf_op jit(solution)/shard_map/all_to_all | solution.py:112
  242.9 6.1 %fit_chunk.6 = bf16[8,512,256]{2,1,0:T(8,128)(2,1)S(1)} custom-call(bf16[4096,256]{1,0:T(8,128)(2,1)} %bitcast.14.rows_ref, bf16[256,256]{1,0:T(8,128)(2,1)S(1)} %fusion.3.perm_ref, bf16[512,512]{1,0:T(8,128)(2,1)S(1)} %copy-done.2, f32[4,2]{1,0:T(4,128)S(1)} %get-tuple-element.21.mask_ref), custom_call_target="tpu_custom_call" | custom-call | flops 1610612736 | bytes 4194304 | tf_op jit(solution)/shard_map/fit_chunk/pallas_call | solution.py:49
  249.0 11.6 %band_partials.1 = f32[4,8,32,640]{3,2,1,0:T(8,128)} custom-call(bf16[4096,256]{1,0:T(8,128)(2,1)} %bitcast.5.f0, bf16[4096,256]{1,0:T(8,128)(2,1)S(1)} %bitcast.69, bf16[4096,256]{1,0:T(8,128)(2,1)S(1)} %bitcast.70, bf16[4096,256]{1,0:T(8,128)(2,1)} %bitcast.20.f3, bf16[4096,256]{1,0:T(8,128)(2,1)} %bitcast.21.below, bf16[4096,256]{1,0:T(8,128)(2,1)} %bitcast.22.above), custom_call_target="tpu_custom_call" | custom-call | flops 6442450944 | bytes 16777216 | tf_op jit(solution)/shard_map/band_partials/pallas_call | solution.py:79
  268.4 12.3 %collective-permute-done.2 = f32[8,32,640]{2,1,0:T(8,128)S(1)} collective-permute-done((f32[8,32,640]{2,1,0:T(8,128)S(1)}, f32[8,32,640]{2,1,0:T(8,128)S(1)}, u32[]{:S(2)}, u32[]{:S(2)}) %collective-permute-start.2) | collective-permute-done | bytes 655392 | tf_op jit(solution)/shard_map/ppermute | solution.py:123
  280.6 15.2 %collective-permute-done.3 = f32[8,32,640]{2,1,0:T(8,128)S(1)} collective-permute-done((f32[8,32,640]{2,1,0:T(8,128)S(1)}, f32[8,32,640]{2,1,0:T(8,128)S(1)}, u32[]{:S(2)}, u32[]{:S(2)}) %collective-permute-start.3) | collective-permute-done | bytes 655392 | tf_op jit(solution)/shard_map/ppermute | solution.py:123
  297.3 4.4 %collective-permute-start.10 = (f32[32,640]{1,0:T(8,128)S(1)}, f32[32,640]{1,0:T(8,128)S(1)}, u32[]{:S(2)}, u32[]{:S(2)}) collective-permute-start(f32[32,640]{1,0:T(8,128)S(1)} %get-tuple-element.15), channel_id=1, source_target_pairs={{0,5},{1,13},{2,21},{3,29},{4,37},{5,45},{6,53},{7,61},{8,6},{9,14... | collective-permute-start | bytes 245768 | tf_op jit(solution)/shard_map/ppermute | solution.py:129
  302.3 4.6 %collective-permute-start.12 = (f32[32,640]{1,0:T(8,128)S(1)}, f32[32,640]{1,0:T(8,128)S(1)}, u32[]{:S(2)}, u32[]{:S(2)}) collective-permute-start(f32[32,640]{1,0:T(8,128)S(1)} %get-tuple-element.13), channel_id=1, source_target_pairs={{0,7},{1,15},{2,23},{3,31},{4,39},{5,47},{6,55},{7,63},{8,0},{9,8}... | collective-permute-start | bytes 245768 | tf_op jit(solution)/shard_map/ppermute | solution.py:129
  307.0 4.9 %collective-permute-start.5 = (f32[32,640]{1,0:T(8,128)S(1)}, f32[32,640]{1,0:T(8,128)S(1)}, u32[]{:S(2)}, u32[]{:S(2)}) collective-permute-start(f32[32,640]{1,0:T(8,128)S(1)} %get-tuple-element.19), channel_id=1, source_target_pairs={{0,0},{1,8},{2,16},{3,24},{4,32},{5,40},{6,48},{7,56},{8,1},{9,9},... | collective-permute-start | bytes 245768 | tf_op jit(solution)/shard_map/ppermute | solution.py:129
  311.9 3.6 %collective-permute-start.6 = (f32[32,640]{1,0:T(8,128)S(1)}, f32[32,640]{1,0:T(8,128)S(1)}, u32[]{:S(2)}, u32[]{:S(2)}) collective-permute-start(f32[32,640]{1,0:T(8,128)S(1)} %get-tuple-element.12), channel_id=1, source_target_pairs={{0,1},{1,9},{2,17},{3,25},{4,33},{5,41},{6,49},{7,57},{8,2},{9,10}... | collective-permute-start | bytes 245768 | tf_op jit(solution)/shard_map/ppermute | solution.py:129
  315.6 16.0 %collective-permute-done.10 = f32[32,640]{1,0:T(8,128)S(1)} collective-permute-done((f32[32,640]{1,0:T(8,128)S(1)}, f32[32,640]{1,0:T(8,128)S(1)}, u32[]{:S(2)}, u32[]{:S(2)}) %collective-permute-start.10) | collective-permute-done | bytes 81952 | tf_op jit(solution)/shard_map/ppermute | solution.py:129
  332.3 8.7 %collective-permute-done.7 = f32[32,640]{1,0:T(8,128)S(1)} collective-permute-done((f32[32,640]{1,0:T(8,128)S(1)}, f32[32,640]{1,0:T(8,128)S(1)}, u32[]{:S(2)}, u32[]{:S(2)}) %collective-permute-start.7) | collective-permute-done | bytes 81952 | tf_op jit(solution)/shard_map/ppermute | solution.py:129
  (51 shorter events, 26.4 us)
Async XLA Ops:
  7.7 63.3 %all-to-all-start.3 = ((bf16[64,64,256]{2,1,0:T(8,128)(2,1)}), bf16[64,64,256]{2,1,0:T(8,128)(2,1)S(1)}, u32[]{:S(2)}, u32[]{:S(2)}) async-start(bf16[64,64,256]{2,1,0:T(8,128)(2,1)} %bitcast.75), calls=%async_computation.3 | async-start | bytes 4194304 | tf_op jit(solution)/shard_map/all_to_all | solution.py:112
  71.0 1.4 copy-start
  72.4 56.8 %all-to-all-start = ((bf16[64,64,256]{2,1,0:T(8,128)(2,1)}), bf16[64,64,256]{2,1,0:T(8,128)(2,1)}, u32[]{:S(2)}, u32[]{:S(2)}) async-start(bf16[64,64,256]{2,1,0:T(8,128)(2,1)} %bitcast.74), calls=%async_computation | async-start | bytes 4194304 | tf_op jit(solution)/shard_map/all_to_all | solution.py:112
  129.2 56.7 %all-to-all-start.1 = ((bf16[64,64,256]{2,1,0:T(8,128)(2,1)}), bf16[64,64,256]{2,1,0:T(8,128)(2,1)S(1)}, u32[]{:S(2)}, u32[]{:S(2)}) async-start(bf16[64,64,256]{2,1,0:T(8,128)(2,1)} %bitcast.73), calls=%async_computation.1 | async-start | bytes 4194304 | tf_op jit(solution)/shard_map/all_to_all | solution.py:112
  185.9 5.8 %copy-start.5 = (s32[4,64]{1,0:T(4,128)S(1)}, s32[4,64]{1,0:T(4,128)}, u32[]{:S(2)}) copy-start(s32[4,64]{1,0:T(4,128)} %param.7) | copy-start | bytes 3076
  185.9 6.3 %copy-start.2 = (bf16[512,512]{1,0:T(8,128)(2,1)S(1)}, bf16[512,512]{1,0:T(8,128)(2,1)}, u32[]{:S(2)}) copy-start(bf16[512,512]{1,0:T(8,128)(2,1)} %metric_ref.7) | copy-start | bytes 1572868
  185.9 56.9 %all-to-all-start.2 = ((bf16[64,64,256]{2,1,0:T(8,128)(2,1)}), bf16[64,64,256]{2,1,0:T(8,128)(2,1)}, u32[]{:S(2)}, u32[]{:S(2)}) async-start(bf16[64,64,256]{2,1,0:T(8,128)(2,1)} %bitcast.72), calls=%async_computation.2 | async-start | bytes 4194304 | tf_op jit(solution)/shard_map/all_to_all | solution.py:112
  192.2 1.6 copy-start.1
  200.1 48.9 %collective-permute-start = (bf16[8,512,256]{2,1,0:T(8,128)(2,1)}, bf16[8,512,256]{2,1,0:T(8,128)(2,1)}, u32[]{:S(2)}, u32[]{:S(2)}) collective-permute-start(bf16[8,512,256]{2,1,0:T(8,128)(2,1)} %fit_chunk.7), channel_id=1, source_target_pairs={{0,1},{1,2},{2,3},{3,4},{4,5},{5,6},{6,7},{8,9},{9,10},{10,11},{11... | collective-permute-start | bytes 6291464 | tf_op jit(solution)/shard_map/ppermute | solution.py:117
  209.4 39.5 %collective-permute-start.1 = (bf16[8,512,256]{2,1,0:T(8,128)(2,1)}, bf16[8,512,256]{2,1,0:T(8,128)(2,1)}, u32[]{:S(2)}, u32[]{:S(2)}) collective-permute-start(bf16[8,512,256]{2,1,0:T(8,128)(2,1)} %fit_chunk.4), channel_id=1, source_target_pairs={{1,0},{2,1},{3,2},{4,3},{5,4},{6,5},{7,6},{9,8},{10,9},{11,10},{12... | collective-permute-start | bytes 6291464 | tf_op jit(solution)/shard_map/ppermute | solution.py:115
  217.9 1.4 copy-start.3
  242.9 6.1 %copy-start.4 = (bf16[8,512,256]{2,1,0:T(8,128)(2,1)S(1)}, bf16[8,512,256]{2,1,0:T(8,128)(2,1)}, u32[]{:S(2)}) copy-start(bf16[8,512,256]{2,1,0:T(8,128)(2,1)} %copy-done.3) | copy-start | bytes 6291460
  260.6 7.7 %copy-start.6 = (s32[127,2]{0,1:T(2,128)S(1)}, s32[127,2]{0,1:T(2,128)}, u32[]{:S(2)}) copy-start(s32[127,2]{0,1:T(2,128)} %param.6) | copy-start | bytes 3052
  262.3 18.4 %collective-permute-start.2 = (f32[8,32,640]{2,1,0:T(8,128)S(1)}, f32[8,32,640]{2,1,0:T(8,128)S(1)}, u32[]{:S(2)}, u32[]{:S(2)}) collective-permute-start(f32[8,32,640]{2,1,0:T(8,128)S(1)} %get-tuple-element.9), channel_id=1, source_target_pairs={{0,64},{64,128},{128,192},{192,0},{1,65},{65,129},{129,193},{193,1... | collective-permute-start | bytes 1966088 | tf_op jit(solution)/shard_map/ppermute | solution.py:123
  264.1 31.7 %collective-permute-start.3 = (f32[8,32,640]{2,1,0:T(8,128)S(1)}, f32[8,32,640]{2,1,0:T(8,128)S(1)}, u32[]{:S(2)}, u32[]{:S(2)}) collective-permute-start(f32[8,32,640]{2,1,0:T(8,128)S(1)} %get-tuple-element.11), channel_id=1, source_target_pairs={{0,128},{64,192},{128,0},{192,64},{1,129},{65,193},{129,1},{193,65... | collective-permute-start | bytes 1966088 | tf_op jit(solution)/shard_map/ppermute | solution.py:123
  267.0 28.8 %collective-permute-start.4 = (f32[8,32,640]{2,1,0:T(8,128)S(1)}, f32[8,32,640]{2,1,0:T(8,128)}, u32[]{:S(2)}, u32[]{:S(2)}) collective-permute-start(f32[8,32,640]{2,1,0:T(8,128)S(1)} %get-tuple-element.10), channel_id=1, source_target_pairs={{0,192},{64,0},{128,64},{192,128},{1,193},{65,1},{129,65},{193,129... | collective-permute-start | bytes 1966088 | tf_op jit(solution)/shard_map/ppermute | solution.py:123
  297.3 34.2 %collective-permute-start.10 = (f32[32,640]{1,0:T(8,128)S(1)}, f32[32,640]{1,0:T(8,128)S(1)}, u32[]{:S(2)}, u32[]{:S(2)}) collective-permute-start(f32[32,640]{1,0:T(8,128)S(1)} %get-tuple-element.15), channel_id=1, source_target_pairs={{0,5},{1,13},{2,21},{3,29},{4,37},{5,45},{6,53},{7,61},{8,6},{9,14... | collective-permute-start | bytes 245768 | tf_op jit(solution)/shard_map/ppermute | solution.py:129
  301.7 29.9 %collective-permute-start.11 = (f32[32,640]{1,0:T(8,128)S(1)}, f32[32,640]{1,0:T(8,128)S(1)}, u32[]{:S(2)}, u32[]{:S(2)}) collective-permute-start(f32[32,640]{1,0:T(8,128)S(1)} %get-tuple-element.14), channel_id=1, source_target_pairs={{0,6},{1,14},{2,22},{3,30},{4,38},{5,46},{6,54},{7,62},{8,7},{9,15... | collective-permute-start | bytes 245768 | tf_op jit(solution)/shard_map/ppermute | solution.py:129
  302.3 29.3 %collective-permute-start.12 = (f32[32,640]{1,0:T(8,128)S(1)}, f32[32,640]{1,0:T(8,128)S(1)}, u32[]{:S(2)}, u32[]{:S(2)}) collective-permute-start(f32[32,640]{1,0:T(8,128)S(1)} %get-tuple-element.13), channel_id=1, source_target_pairs={{0,7},{1,15},{2,23},{3,31},{4,39},{5,47},{6,55},{7,63},{8,0},{9,8}... | collective-permute-start | bytes 245768 | tf_op jit(solution)/shard_map/ppermute | solution.py:129
  307.0 25.2 %collective-permute-start.5 = (f32[32,640]{1,0:T(8,128)S(1)}, f32[32,640]{1,0:T(8,128)S(1)}, u32[]{:S(2)}, u32[]{:S(2)}) collective-permute-start(f32[32,640]{1,0:T(8,128)S(1)} %get-tuple-element.19), channel_id=1, source_target_pairs={{0,0},{1,8},{2,16},{3,24},{4,32},{5,40},{6,48},{7,56},{8,1},{9,9},... | collective-permute-start | bytes 245768 | tf_op jit(solution)/shard_map/ppermute | solution.py:129
  311.9 20.3 %collective-permute-start.6 = (f32[32,640]{1,0:T(8,128)S(1)}, f32[32,640]{1,0:T(8,128)S(1)}, u32[]{:S(2)}, u32[]{:S(2)}) collective-permute-start(f32[32,640]{1,0:T(8,128)S(1)} %get-tuple-element.12), channel_id=1, source_target_pairs={{0,1},{1,9},{2,17},{3,25},{4,33},{5,41},{6,49},{7,57},{8,2},{9,10}... | collective-permute-start | bytes 245768 | tf_op jit(solution)/shard_map/ppermute | solution.py:129
  331.5 9.4 %collective-permute-start.7 = (f32[32,640]{1,0:T(8,128)S(1)}, f32[32,640]{1,0:T(8,128)S(1)}, u32[]{:S(2)}, u32[]{:S(2)}) collective-permute-start(f32[32,640]{1,0:T(8,128)S(1)} %get-tuple-element.18), channel_id=1, source_target_pairs={{0,2},{1,10},{2,18},{3,26},{4,34},{5,42},{6,50},{7,58},{8,3},{9,11... | collective-permute-start | bytes 245768 | tf_op jit(solution)/shard_map/ppermute | solution.py:129
  331.6 9.4 %collective-permute-start.8 = (f32[32,640]{1,0:T(8,128)S(1)}, f32[32,640]{1,0:T(8,128)S(1)}, u32[]{:S(2)}, u32[]{:S(2)}) collective-permute-start(f32[32,640]{1,0:T(8,128)S(1)} %get-tuple-element.17), channel_id=1, source_target_pairs={{0,3},{1,11},{2,19},{3,27},{4,35},{5,43},{6,51},{7,59},{8,4},{9,12... | collective-permute-start | bytes 245768 | tf_op jit(solution)/shard_map/ppermute | solution.py:129
  331.6 9.4 %collective-permute-start.9 = (f32[32,640]{1,0:T(8,128)S(1)}, f32[32,640]{1,0:T(8,128)S(1)}, u32[]{:S(2)}, u32[]{:S(2)}) collective-permute-start(f32[32,640]{1,0:T(8,128)S(1)} %get-tuple-element.16), channel_id=1, source_target_pairs={{0,4},{1,12},{2,20},{3,28},{4,36},{5,44},{6,52},{7,60},{8,5},{9,13... | collective-permute-start | bytes 245768 | tf_op jit(solution)/shard_map/ppermute | solution.py:129

commit v2 on v1

v2 whole, which is shorter than its diff:
```python
import jax
import jax.numpy as jnp
from jax import lax
from jax.experimental import pallas as pl
from jax.experimental.pallas import tpu as pltpu
from jax.sharding import PartitionSpec as P

BS = 128
QB = 128
NZ = 8
NC = 8
NY = 4
PAIR = 2 * BS
BAND = 5
PART = BS // NY
VMEM = pltpu.MemorySpace.VMEM
SMEM = pltpu.MemorySpace.SMEM


def in_band(u, v):
    found = []
    for s in range(2):
        for t in range(2):
            e = 2 * v + t - 2 * u - s
            if abs(e) <= 2 and 0 <= u <= 3:
                found.append((s, t, 2 * u + s, e))
    return found


EARLY_PRODUCTS = ((0, -1), (0, 0), (0, 1), (1, 1), (3, 3), (3, 4))
LATE_PRODUCTS = ((2, 1), (2, 2), (2, 3))


def slots_of(products):
    slots = []
    for u, v in products:
        slots += [(r, e) for _, _, r, e in in_band(u, v)]
        if u != v:
            slots += [(r, e) for _, _, r, e in in_band(v, u)]
    off = [k for k in slots if k[1] != 0]
    return off + [k for k in slots if k[1] == 0], len(off)


EARLY, EARLY_OFF = slots_of(EARLY_PRODUCTS)
LATE, LATE_OFF = slots_of(LATE_PRODUCTS)


def sent_slots(slots, off):
    return 2 * len(slots) - off


def cut_kernel(source, out_ref, sem, *, offsets):
    def one(k, carry):
        z, c = k // NC, k % NC
        for n, offset in enumerate(offsets):
            start = pl.multiple_of(c * 1024 + offset, BS)
            pltpu.make_async_copy(
                source.at[:, z, :, pl.ds(start, PAIR)], out_ref.at[k, :, :, pl.ds(n * PAIR, PAIR)], sem
            ).start()
        return carry

    lax.fori_loop(0, NZ * NC, one, 0)
    pltpu.make_async_copy(out_ref, out_ref, sem).wait()


def cut_chunk(integrals, pairs):
    width = PAIR * len(pairs)
    return pl.pallas_call(
        lambda s, o, sem: cut_kernel(s, o, sem, offsets=[PAIR * u for u in pairs]),
        out_shape=jax.ShapeDtypeStruct((NZ * NC, 8, 8, width), jnp.bfloat16),
        in_specs=[pl.BlockSpec(memory_space=pl.ANY)],
        out_specs=pl.BlockSpec(memory_space=VMEM),
        scratch_shapes=[pltpu.SemaphoreType.DMA],
        compiler_params=pltpu.CompilerParams(vmem_limit_bytes=60 << 20),
        cost_estimate=pl.CostEstimate(flops=0, bytes_accessed=2 * 8192 * width, transcendentals=0),
        name="cut_chunk",
    )(integrals.reshape(8, NZ, 8, NC * 1024))


def turn_rows(rows_ref, perm_ref, turned_ref):
    def turn(g, carry):
        start = pl.multiple_of(g * 256, 256)
        turned = jnp.dot(perm_ref[...], rows_ref[pl.ds(start, 256), :], preferred_element_type=jnp.float32)
        turned = turned.astype(jnp.bfloat16)
        at = pl.multiple_of(g * 32, 32)
        for i in range(8):
            turned_ref[i, pl.ds(at, 32), :] = turned[i * 32 : (i + 1) * 32]
        return carry

    lax.fori_loop(0, 16, turn, 0, unroll=4)


def fit_one(metric_ref, turned_ref, mask_ref, fitted_ref, i):
    fitted = jnp.dot(metric_ref[...], turned_ref[i], preferred_element_type=jnp.float32)
    for q in range(4):
        for b in range(2):
            piece = fitted[q * QB : (q + 1) * QB, b * BS : (b + 1) * BS] * mask_ref[q, b]
            at = pl.multiple_of(i * 512, 512) + q * QB
            fitted_ref[pl.ds(at, QB), b * BS : (b + 1) * BS] = piece.astype(jnp.bfloat16)


def fit_kernel(rows_ref, perm_ref, metric_ref, mask_ref, out_ref, turned_ref):
    turn_rows(rows_ref, perm_ref, turned_ref)

    def fit(i, carry):
        fit_one(metric_ref, turned_ref, mask_ref, out_ref, i)
        return carry

    lax.fori_loop(0, 8, fit, 0, unroll=2)


def whole(shape, at=None):
    return pl.BlockSpec(shape, lambda g: at or (0,) * len(shape))


def fit_chunk(rows, at, perm, metric, mask):
    return pl.pallas_call(
        fit_kernel,
        grid=(1,),
        out_shape=jax.ShapeDtypeStruct((4096, PAIR), jnp.bfloat16),
        in_specs=[
            whole((4096, PAIR), (0, at)),
            whole((256, 256)),
            whole((512, 512)),
            pl.BlockSpec(memory_space=SMEM),
        ],
        out_specs=whole((4096, PAIR)),
        scratch_shapes=[pltpu.VMEM((8, 512, PAIR), jnp.bfloat16)],
        compiler_params=pltpu.CompilerParams(vmem_limit_bytes=24 << 20),
        cost_estimate=pl.CostEstimate(flops=2 * 4096 * PAIR * 768, bytes_accessed=4 * 4096 * PAIR, transcendentals=0),
        name="fit_chunk",
    )(rows, perm, metric, mask)


def put_slots(tile_ref, places, slots, off, y, own_ref, out_refs):
    for s, t, r, e in places:
        n = slots.index((r, e))
        for d in range(NY):
            at = pl.multiple_of(s * BS + lax.rem(y + d, NY) * PART, PART)
            piece = tile_ref[pl.ds(at, PART), t * BS : (t + 1) * BS]
            if d == 0:
                own_ref[n] = piece
                continue
            high = piece.astype(jnp.bfloat16)
            out_refs[d - 1][n] = high
            if e == 0:
                out_refs[d - 1][n + len(slots) - off] = (piece - high.astype(jnp.float32)).astype(jnp.bfloat16)


def put_product(u, v, tile_ref, flip_ref, slots, off, y, own_ref, out_refs):
    put_slots(tile_ref, in_band(u, v), slots, off, y, own_ref, out_refs)
    if u != v and 0 <= v <= 3:
        flip_ref[...] = tile_ref[...].T
        put_slots(flip_ref, in_band(v, u), slots, off, y, own_ref, out_refs)


def early_kernel(y_ref, f0, f1, f3, below, above, own_ref, o1, o2, o3, tiles_ref, flips_ref):
    pairs = {-1: below, 0: f0, 1: f1, 3: f3, 4: above}
    lefts = {}
    for n, (u, v) in enumerate(EARLY_PRODUCTS):
        if u not in lefts:
            lefts = {u: pairs[u][...].T}
        tiles_ref[n] = jnp.dot(lefts[u], pairs[v][...], preferred_element_type=jnp.float32)
        put_product(u, v, tiles_ref.at[n], flips_ref.at[n], EARLY, EARLY_OFF, y_ref[0], own_ref, (o1, o2, o3))


def late_kernel(y_ref, mask_ref, rows_ref, perm_ref, metric_ref, f1, f3, own_ref, o1, o2, o3, turned_ref, f2, tiles_ref, flips_ref):
    turn_rows(rows_ref, perm_ref, turned_ref)
    tiles_ref[...] = jnp.zeros_like(tiles_ref)

    def step(i, carry):
        fit_one(metric_ref, turned_ref, mask_ref, f2, i)
        at = pl.multiple_of(i * 512, 512)
        left = f2[pl.ds(at, 512), :].T
        for n, right in enumerate((f1, f2, f3)):
            tiles_ref[n] += jnp.dot(left, right[pl.ds(at, 512), :], preferred_element_type=jnp.float32)
        return carry

    lax.fori_loop(0, 8, step, 0)
    for n, (u, v) in enumerate(LATE_PRODUCTS):
        put_product(u, v, tiles_ref.at[n], flips_ref.at[n], LATE, LATE_OFF, y_ref[0], own_ref, (o1, o2, o3))


def exchange_shapes(slots, off):
    sent = jax.ShapeDtypeStruct((sent_slots(slots, off), PART, BS), jnp.bfloat16)
    return [jax.ShapeDtypeStruct((len(slots), PART, BS), jnp.float32)] + [sent] * 3


def early_tiles(y, f0, f1, f3, below, above):
    count = len(EARLY_PRODUCTS)
    return pl.pallas_call(
        early_kernel,
        out_shape=exchange_shapes(EARLY, EARLY_OFF),
        in_specs=[pl.BlockSpec(memory_space=SMEM)] + [pl.BlockSpec(memory_space=VMEM)] * 5,
        out_specs=[pl.BlockSpec(memory_space=VMEM)] * 4,
        scratch_shapes=[pltpu.VMEM((count, PAIR, PAIR), jnp.float32)] * 2,
        compiler_params=pltpu.CompilerParams(vmem_limit_bytes=40 << 20),
        cost_estimate=pl.CostEstimate(flops=2 * 4096 * 256 * 256 * count, bytes_accessed=14 << 20, transcendentals=0),
        name="early_tiles",
    )(y, f0, f1, f3, below, above)


def late_tiles(y, mask, rows, perm, metric, f1, f3):
    return pl.pallas_call(
        late_kernel,
        out_shape=exchange_shapes(LATE, LATE_OFF),
        in_specs=[pl.BlockSpec(memory_space=SMEM)] * 2 + [pl.BlockSpec(memory_space=VMEM)] * 5,
        out_specs=[pl.BlockSpec(memory_space=VMEM)] * 4,
        scratch_shapes=[
            pltpu.VMEM((8, 512, PAIR), jnp.bfloat16),
            pltpu.VMEM((4096, PAIR), jnp.bfloat16),
            pltpu.VMEM((3, PAIR, PAIR), jnp.float32),
            pltpu.VMEM((3, PAIR, PAIR), jnp.float32),
        ],
        compiler_params=pltpu.CompilerParams(vmem_limit_bytes=40 << 20),
        cost_estimate=pl.CostEstimate(flops=2 * 4096 * 256 * 1536, bytes_accessed=8 << 20, transcendentals=0),
        name="late_tiles",
    )(y, mask, rows, perm, metric, f1, f3)


def over_domains(sent):
    return [lax.ppermute(s, "aux", [(a, (a + d) % NY) for a in range(NY)]) for d, s in enumerate(sent, 1)]


def widen(got, slots, off):
    high = got[: len(slots)].astype(jnp.float32)
    low = got[len(slots) :].astype(jnp.float32)
    return high + jnp.pad(low, ((off, 0), (0, 0), (0, 0)))


def merge_kernel(odd_ref, early_ref, late_ref, g1, g2, g3, own_ref, out_ref, band_ref):
    for n, (r, e) in enumerate(EARLY):
        band_ref[r, e + 2] = early_ref[n]
    for n, (r, e) in enumerate(LATE):
        value = late_ref[n]
        for got in (g1, g2, g3):
            value = value + got[n].astype(jnp.float32)
            if e == 0:
                value = value + got[n + len(LATE) - LATE_OFF].astype(jnp.float32)
        band_ref[r, e + 2] = value
    odd = odd_ref[0]
    for k in range(4):
        for slot in range(BAND):
            own_ref[k, slot] = band_ref[2 * k + odd, slot]
            value = band_ref[2 * k + 1 - odd, slot]
            high = value.astype(jnp.bfloat16)
            out_ref[k * 6 + slot] = high
            if slot == 2:
                out_ref[k * 6 + 5] = (value - high.astype(jnp.float32)).astype(jnp.bfloat16)


def merge(odd, early, late, got):
    return pl.pallas_call(
        merge_kernel,
        out_shape=[
            jax.ShapeDtypeStruct((4, BAND, PART, BS), jnp.float32),
            jax.ShapeDtypeStruct((24, PART, BS), jnp.bfloat16),
        ],
        in_specs=[pl.BlockSpec(memory_space=SMEM)] + [pl.BlockSpec(memory_space=VMEM)] * 5,
        out_specs=[pl.BlockSpec(memory_space=VMEM)] * 2,
        scratch_shapes=[pltpu.VMEM((NC, BAND, PART, BS), jnp.float32)],
        name="merge",
    )(odd, early, late, *got)


def settle_kernel(half_ref, own_ref, got_ref, o0, o1, o2, o3):
    for j, out in enumerate((o0, o1, o2, o3)):
        k = lax.rem(half_ref[0] + j, 4)
        for slot in range(BAND):
            value = own_ref[k, slot] + got_ref[k * 6 + slot].astype(jnp.float32)
            if slot == 2:
                value = value + got_ref[k * 6 + 5].astype(jnp.float32)
            out[:, slot * BS : (slot + 1) * BS] = value


def settle(half, own, got):
    return pl.pallas_call(
        settle_kernel,
        out_shape=[jax.ShapeDtypeStruct((PART, BAND * BS), jnp.float32)] * 4,
        in_specs=[pl.BlockSpec(memory_space=SMEM)] + [pl.BlockSpec(memory_space=VMEM)] * 2,
        out_specs=[pl.BlockSpec(memory_space=VMEM)] * 4,
        name="settle",
    )(half, own, got)


def local(integrals, metric, pair_list, aux_mask):
    blk = lax.axis_index("blk")
    y = jnp.full((1,), lax.axis_index("aux"), jnp.int32)
    z, c = blk // NC, blk % NC
    grid = [(k // NC, k % NC) for k in range(NZ * NC)]
    up = [(zz * NC + cc, zz * NC + cc + 1) for zz, cc in grid if cc < NC - 1]
    down = [(b, a) for a, b in up]

    row = lax.broadcasted_iota(jnp.int32, (256, 256), 0)
    col = lax.broadcasted_iota(jnp.int32, (256, 256), 1)
    perm = ((row // 32 == col % 8) & (row % 32 == col // 8)).astype(jnp.bfloat16)
    own_mask = lax.dynamic_slice(aux_mask, (0, c * 8), (4, 8)).astype(jnp.float32)
    masks = [own_mask[:, 2 * u : 2 * u + 2] for u in range(4)]

    e = jnp.arange(BAND, dtype=jnp.int32) - 2
    low, high = blk + jnp.minimum(e, 0), blk + jnp.maximum(e, 0)
    hits = (pair_list[:, 0][:, None] == low[None]) & (pair_list[:, 1][:, None] == high[None])
    scale = jnp.repeat(jnp.sum(hits.astype(jnp.float32), axis=0), BS)

    def spread(pairs, source):
        got = lax.all_to_all(cut_chunk(source, pairs), "blk", split_axis=0, concat_axis=0, tiled=True)
        return got.reshape(4096, PAIR * len(pairs))

    rows = spread((0, 3), integrals)
    f0 = fit_chunk(rows, 0, perm, metric, masks[0])
    f3 = fit_chunk(rows, 1, perm, metric, masks[3])
    above = lax.ppermute(f0, "blk", down)
    below = lax.ppermute(f3, "blk", up)
    rows = spread((1,), integrals)
    source, above, below = lax.optimization_barrier((integrals, above, below))
    last = spread((2,), source)
    f1 = fit_chunk(rows, 0, perm, metric, masks[1])

    early, *sent = early_tiles(y, f0, f1, f3, below, above)
    for got in over_domains(sent):
        early = early + widen(got, EARLY, EARLY_OFF)

    late, *sent = late_tiles(y, masks[2], last, perm, metric, f1, f3)
    own, sent = merge(jnp.full((1,), z % 2, jnp.int32), early, late, over_domains(sent))
    got = lax.ppermute(sent, "blk", [(zz * NC + cc, (zz ^ 1) * NC + cc) for zz, cc in grid])
    total, *sent = settle(jnp.full((1,), z // 2, jnp.int32), own, got)
    for j, s in enumerate(sent, 1):
        total = total + lax.ppermute(s, "blk", [(zz * NC + cc, (zz + 2 * j) % NZ * NC + cc) for zz, cc in grid])
    total = lax.ppermute(total, "blk", [(zz * NC + cc, cc * NC + zz) for zz, cc in grid])
    return (total * scale[None, :])[None]


def solution(mesh):
    return jax.shard_map(
        local,
        mesh=mesh,
        in_specs=(P(("aux", "blk"), None, None), P("aux", None), P(), P("aux", None)),
        out_specs=P("blk", "aux", None),
        check_vma=False,
    )
```

time: 347 us -> 297 us (0.86); the launches traced: 342 us -> 296 us
  waiting for transfers between devices: 220 us -> 178 us
  local copies, waits for them, and re-layouts: 23.7 us -> 10.7 us
  Pallas kernels: 36.2 us -> 43.7 us
    all_to_all x4 -> x3, waiting for transfers between devices: 168 us -> 114 us  [spread(): lax.all_to_all(cut_chunk(source, pairs), 'blk', split_axis=0, concat_axis...]
    transpose x5 -> x0, local copies, waits for them, and re-layouts: 17.5 us -> none  [local(): split[:, :, :, :, u].transpose(1, 3, 0, 2, 4).reshape(NZ * NC, 64, PAIR)]
    ppermute x13, waiting for transfers between devices: 52.2 us -> 64.4 us  [the longest x1 36.2 us: local(): above = lax.ppermute(f0, 'blk', down)]
    pallas_call x5 -> x10, Pallas kernels: 36.2 us -> 43.7 us  [the longest x3 15.2 us: fit_chunk(): pl.pallas_call(fit_kernel, grid=(1,), out_shape=jax.ShapeDtypeStruct((409...]
    unnamed x14 -> x32, local copies, waits for them, and re-layouts: 4.34 us -> 8.1 us
    all_to_all x4 -> x3, starting transfers between devices: 28.8 us -> 29 us  [spread(): lax.all_to_all(cut_chunk(source, pairs), 'blk', split_axis=0, concat_axis...]
  transfers between devices with their start and end apart: 17 -> 16, of which waited for: 8 -> 12; matrix products, arithmetic and copies ran while one was open for 3% -> 2% of each run, Pallas kernels for 7% -> 9%
where the time goes in v2:
time: 297 us; the launch traced here: 296 us
  waiting for transfers between devices  178 us (60%)
  starting transfers between devices  59.1 us (20%)
  Pallas kernels  43.7 us (15%)
  local copies, waits for them, and re-layouts  10.7 us (4%)
  other arithmetic  4.12 us (1%)
    all_to_all x3, waiting for transfers between devices, spread(): lax.all_to_all(cut_chunk(source, pairs), 'blk', split_axis=0, concat_axis...  114 us
    ppermute x1, waiting for transfers between devices, local(): above = lax.ppermute(f0, 'blk', down)  36.2 us
    all_to_all x3, starting transfers between devices, spread(): lax.all_to_all(cut_chunk(source, pairs), 'blk', split_axis=0, concat_axis...  29 us
    pallas_call x3, Pallas kernels, fit_chunk(): pl.pallas_call(fit_kernel, grid=(1,), out_shape=jax.ShapeDtypeStruct((409...  15.2 us
    ppermute x6, waiting for transfers between devices, over_domains(): lax.ppermute(s, 'aux', [(a, (a + d) % NY) for a in range(NY)])  13.8 us
    ppermute x6, starting transfers between devices, over_domains(): lax.ppermute(s, 'aux', [(a, (a + d) % NY) for a in range(NY)])  10.5 us
    pallas_call x3, Pallas kernels, cut_chunk(): pl.pallas_call(lambda s, o, sem: cut_kernel(s, o, sem, offsets=[PAIR * u...  10.4 us
    pallas_call x1, Pallas kernels, late_tiles(): pl.pallas_call(late_kernel, out_shape=exchange_shapes(LATE, LATE_OFF), in...  9.75 us
  transfers between devices with their start and end apart: 16, of which 12 were waited for; matrix products, arithmetic and copies ran while one was open for 2% of the time, Pallas kernels for 9%

profile of v2, /device:TPU:4, one launch (start us, length us, event | category | flops | bytes accessed | tf_op | source)
XLA Modules:
  0.0 296.2 jit_solution(13487592909661758343)
XLA Ops:
  0.0 4.3 %cut_chunk.3 = bf16[64,8,8,512]{3,2,1,0:T(8,128)(2,1)} custom-call(bf16[8,8,8,8192]{3,2,1,0:T(8,128)(2,1)} %bitcast.16), custom_call_target="tpu_custom_call" | custom-call | bytes 8388608 | tf_op jit(solution)/shard_map/cut_chunk/pallas_call | solution.py:68
  4.3 12.2 %all-to-all-start = ((bf16[64,8,8,512]{3,2,1,0:T(8,128)(2,1)}), bf16[64,8,8,512]{3,2,1,0:T(8,128)(2,1)}, u32[]{:S(2)}, u32[]{:S(2)}) async-start(bf16[64,8,8,512]{3,2,1,0:T(8,128)(2,1)} %cut_chunk.3), calls=%async_computation | async-start | bytes 8388608 | tf_op jit(solution)/shard_map/all_to_all | solution.py:306
  16.5 3.2 %cut_chunk.4 = bf16[64,8,8,256]{3,2,1,0:T(8,128)(2,1)} custom-call(bf16[8,8,8,8192]{3,2,1,0:T(8,128)(2,1)} %bitcast.17), custom_call_target="tpu_custom_call" | custom-call | bytes 4194304 | tf_op jit(solution)/shard_map/cut_chunk/pallas_call | solution.py:68
  19.7 92.9 %all-to-all-done = bf16[64,8,8,512]{3,2,1,0:T(8,128)(2,1)} async-done(((bf16[64,8,8,512]{3,2,1,0:T(8,128)(2,1)}), bf16[64,8,8,512]{3,2,1,0:T(8,128)(2,1)}, u32[]{:S(2)}, u32[]{:S(2)}) %all-to-all-start) | async-done | bytes 4194336 | tf_op jit(solution)/shard_map/all_to_all | solution.py:306
  112.7 5.6 %all-to-all-start.1 = ((bf16[64,8,8,256]{3,2,1,0:T(8,128)(2,1)}), bf16[64,8,8,256]{3,2,1,0:T(8,128)(2,1)}, u32[]{:S(2)}, u32[]{:S(2)}) async-start(bf16[64,8,8,256]{3,2,1,0:T(8,128)(2,1)} %cut_chunk.4), calls=%async_computation.1 | async-start | bytes 4194304 | tf_op jit(solution)/shard_map/all_to_all | solution.py:306
  118.8 4.7 %fit_chunk.3.f0 = bf16[4096,256]{1,0:T(8,128)(2,1)S(1)} custom-call(bf16[4096,512]{1,0:T(8,128)(2,1)} %bitcast.4.rows_ref, bf16[256,256]{1,0:T(8,128)(2,1)S(1)} %fusion.1.perm_ref, bf16[512,512]{1,0:T(8,128)(2,1)S(1)} %copy-done, f32[4,2]{1,0:T(4,128)S(1)} %get-tuple-element.42.mask_ref), custom_call_target="tpu_custom_call" | custom-call | flops 1610612736 | bytes 4194304 | tf_op jit(solution)/shard_map/fit_chunk/pallas_call | solution.py:117
  123.6 5.5 %fit_chunk.5.f3 = bf16[4096,256]{1,0:T(8,128)(2,1)S(1)} custom-call(bf16[4096,512]{1,0:T(8,128)(2,1)} %bitcast.4.rows_ref, bf16[256,256]{1,0:T(8,128)(2,1)S(1)} %fusion.1.perm_ref, bf16[512,512]{1,0:T(8,128)(2,1)S(1)} %copy-done, f32[4,2]{1,0:T(4,128)S(1)} %get-tuple-element.40.mask_ref), custom_call_target="tpu_custom_call" | custom-call | flops 1610612736 | bytes 4194304 | tf_op jit(solution)/shard_map/fit_chunk/pallas_call | solution.py:117
  133.4 36.2 %collective-permute-done.above = bf16[4096,256]{1,0:T(8,128)(2,1)S(1)} collective-permute-done((bf16[4096,256]{1,0:T(8,128)(2,1)S(1)}, bf16[4096,256]{1,0:T(8,128)(2,1)S(1)}, u32[]{:S(2)}, u32[]{:S(2)}) %collective-permute-start) | collective-permute-done | bytes 2097184 | tf_op jit(solution)/shard_map/ppermute | solution.py:312
  172.3 3.0 cut_chunk.5
  175.3 11.2 %all-to-all-start.2 = ((bf16[64,8,8,256]{3,2,1,0:T(8,128)(2,1)}), bf16[64,8,8,256]{3,2,1,0:T(8,128)(2,1)}, u32[]{:S(2)}, u32[]{:S(2)}) async-start(bf16[64,8,8,256]{3,2,1,0:T(8,128)(2,1)} %cut_chunk.5), calls=%async_computation.2 | async-start | bytes 4194304 | tf_op jit(solution)/shard_map/all_to_all | solution.py:306
  186.5 4.9 %fit_chunk.4.f1 = bf16[4096,256]{1,0:T(8,128)(2,1)S(1)} custom-call(bf16[4096,256]{1,0:T(8,128)(2,1)} %bitcast.5.rows_ref, bf16[256,256]{1,0:T(8,128)(2,1)S(1)} %fusion.1.perm_ref, bf16[512,512]{1,0:T(8,128)(2,1)S(1)} %copy-done, f32[4,2]{1,0:T(4,128)S(1)} %get-tuple-element.41.mask_ref), custom_call_target="tpu_custom_call" | custom-call | flops 1610612736 | bytes 4194304 | tf_op jit(solution)/shard_map/fit_chunk/pallas_call | solution.py:117
  191.5 2.3 copy-done.7
  193.8 4.5 %early_tiles.1 = (f32[24,32,128]{2,1,0:T(8,128)S(1)}, bf16[30,32,128]{2,1,0:T(8,128)(2,1)S(1)}, bf16[30,32,128]{2,1,0:T(8,128)(2,1)}, bf16[30,32,128]{2,1,0:T(8,128)(2,1)}) custom-call(s32[1]{0:T(128)} %bitcast.2.y_ref, bf16[4096,256]{1,0:T(8,128)(2,1)S(1)} %copy-done.2, bf16[4096,256]{1,0:T(8,128)(2,1)S(1)} %fit_chunk.4.f1, ...), custom_call_target="tpu_custom_call" | custom-call | flops 3221225472 | bytes 14680064 | tf_op jit(solution)/shard_map/early_tiles/pallas_call | solution.py:191
  198.3 3.0 %collective-permute-start.4 = (bf16[30,32,128]{2,1,0:T(8,128)(2,1)}, bf16[30,32,128]{2,1,0:T(8,128)(2,1)}, u32[]{:S(2)}, u32[]{:S(2)}) collective-permute-start(bf16[30,32,128]{2,1,0:T(8,128)(2,1)} %get-tuple-element.27), channel_id=1, source_target_pairs={{0,192},{64,0},{128,64},{192,128},{1,193},{65,1},{129,65},{193,129... | collective-permute-start | bytes 737288 | tf_op jit(solution)/shard_map/ppermute | solution.py:222
  202.9 9.5 %collective-permute-done.4 = bf16[30,32,128]{2,1,0:T(8,128)(2,1)} collective-permute-done((bf16[30,32,128]{2,1,0:T(8,128)(2,1)}, bf16[30,32,128]{2,1,0:T(8,128)(2,1)}, u32[]{:S(2)}, u32[]{:S(2)}) %collective-permute-start.4) | collective-permute-done | bytes 245792 | tf_op jit(solution)/shard_map/ppermute | solution.py:222
  216.8 20.9 %all-to-all-done.2 = bf16[64,8,8,256]{3,2,1,0:T(8,128)(2,1)} async-done(((bf16[64,8,8,256]{3,2,1,0:T(8,128)(2,1)}), bf16[64,8,8,256]{3,2,1,0:T(8,128)(2,1)}, u32[]{:S(2)}, u32[]{:S(2)}) %all-to-all-start.2) | async-done | bytes 2097184 | tf_op jit(solution)/shard_map/all_to_all | solution.py:306
  239.3 9.8 %late_tiles.1 = (f32[16,32,128]{2,1,0:T(8,128)S(1)}, bf16[18,32,128]{2,1,0:T(8,128)(2,1)S(1)}, bf16[18,32,128]{2,1,0:T(8,128)(2,1)S(1)}, bf16[18,32,128]{2,1,0:T(8,128)(2,1)S(1)}) custom-call(s32[1]{0:T(128)} %bitcast.2.y_ref, f32[4,2]{1,0:T(4,128)S(1)} %get-tuple-element.39.mask_ref, bf16[4096,256]{1,0:T(8,128)(2,1)} %bitcast.7.rows_ref, ...), custom_call_target="tpu_custom_call" | custom-call | flops 3221225472 | bytes 8388608 | tf_op jit(solution)/shard_map/late_tiles/pallas_call | solution.py:204
  250.7 2.9 collective-permute-start.6
  257.1 2.3 collective-permute-done.6.g2
  263.8 4.3 %collective-permute-done.8.got_ref = bf16[24,32,128]{2,1,0:T(8,128)(2,1)S(1)} collective-permute-done((bf16[24,32,128]{2,1,0:T(8,128)(2,1)}, bf16[24,32,128]{2,1,0:T(8,128)(2,1)S(1)}, u32[]{:S(2)}, u32[]{:S(2)}) %collective-permute-start.8) | collective-permute-done | bytes 196640 | tf_op jit(solution)/shard_map/ppermute | solution.py:325
  271.7 2.9 collective-permute-start.10
  277.7 4.0 %collective-permute-done.10 = f32[32,640]{1,0:T(8,128)S(1)} collective-permute-done((f32[32,640]{1,0:T(8,128)}, f32[32,640]{1,0:T(8,128)S(1)}, u32[]{:S(2)}, u32[]{:S(2)}) %collective-permute-start.10) | collective-permute-done | bytes 81952 | tf_op jit(solution)/shard_map/ppermute | solution.py:328
  282.9 8.6 %collective-permute-start.12 = (f32[32,640]{1,0:T(8,128)S(1)}, f32[32,640]{1,0:T(8,128)S(1)}, u32[]{:S(2)}, u32[]{:S(2)}) collective-permute-start(f32[32,640]{1,0:T(8,128)S(1)} %add_add_fusion.1), channel_id=1, source_target_pairs={{0,0},{1,8},{2,16},{3,24},{4,32},{5,40},{6,48},{7,56},{8,1},{9,9},... | collective-permute-start | bytes 245768 | tf_op jit(solution)/shard_map/ppermute | solution.py:329
  291.6 4.0 %collective-permute-done.12 = f32[32,640]{1,0:T(8,128)S(1)} collective-permute-done((f32[32,640]{1,0:T(8,128)S(1)}, f32[32,640]{1,0:T(8,128)S(1)}, u32[]{:S(2)}, u32[]{:S(2)}) %collective-permute-start.12) | collective-permute-done | bytes 81952 | tf_op jit(solution)/shard_map/ppermute | solution.py:329
  (69 shorter events, 33.3 us)
Async XLA Ops:
  4.3 108.3 %all-to-all-start = ((bf16[64,8,8,512]{3,2,1,0:T(8,128)(2,1)}), bf16[64,8,8,512]{3,2,1,0:T(8,128)(2,1)}, u32[]{:S(2)}, u32[]{:S(2)}) async-start(bf16[64,8,8,512]{3,2,1,0:T(8,128)(2,1)} %cut_chunk.3), calls=%async_computation | async-start | bytes 8388608 | tf_op jit(solution)/shard_map/all_to_all | solution.py:306
  19.7 98.7 %copy-start.14 = (s32[4,64]{1,0:T(4,128)S(1)}, s32[4,64]{1,0:T(4,128)}, u32[]{:S(2)}) copy-start(s32[4,64]{1,0:T(4,128)} %param.7) | copy-start | bytes 3076
  19.7 99.1 %copy-start = (bf16[512,512]{1,0:T(8,128)(2,1)S(1)}, bf16[512,512]{1,0:T(8,128)(2,1)}, u32[]{:S(2)}) copy-start(bf16[512,512]{1,0:T(8,128)(2,1)} %metric_ref.7) | copy-start | bytes 1572868
  112.7 62.6 %all-to-all-start.1 = ((bf16[64,8,8,256]{3,2,1,0:T(8,128)(2,1)}), bf16[64,8,8,256]{3,2,1,0:T(8,128)(2,1)}, u32[]{:S(2)}, u32[]{:S(2)}) async-start(bf16[64,8,8,256]{3,2,1,0:T(8,128)(2,1)} %cut_chunk.4), calls=%async_computation.1 | async-start | bytes 4194304 | tf_op jit(solution)/shard_map/all_to_all | solution.py:306
  123.6 5.5 %copy-start.1 = (bf16[4096,256]{1,0:T(8,128)(2,1)}, bf16[4096,256]{1,0:T(8,128)(2,1)S(1)}, u32[]{:S(2)}) copy-start(bf16[4096,256]{1,0:T(8,128)(2,1)S(1)} %fit_chunk.3.f0) | copy-start | bytes 6291460
  129.1 40.5 %collective-permute-start = (bf16[4096,256]{1,0:T(8,128)(2,1)S(1)}, bf16[4096,256]{1,0:T(8,128)(2,1)S(1)}, u32[]{:S(2)}, u32[]{:S(2)}) collective-permute-start(bf16[4096,256]{1,0:T(8,128)(2,1)S(1)} %fit_chunk.3.f0), channel_id=1, source_target_pairs={{1,0},{2,1},{3,2},{4,3},{5,4},{6,5},{7,6},{9,8},{10,9},{11,10},{12... | collective-permute-start | bytes 6291464 | tf_op jit(solution)/shard_map/ppermute | solution.py:312
  131.3 39.7 %collective-permute-start.1 = (bf16[4096,256]{1,0:T(8,128)(2,1)S(1)}, bf16[4096,256]{1,0:T(8,128)(2,1)S(1)}, u32[]{:S(2)}, u32[]{:S(2)}) collective-permute-start(bf16[4096,256]{1,0:T(8,128)(2,1)S(1)} %fit_chunk.5.f3), channel_id=1, source_target_pairs={{0,1},{1,2},{2,3},{3,4},{4,5},{5,6},{6,7},{8,9},{9,10},{10,11},{11... | collective-permute-start | bytes 6291464 | tf_op jit(solution)/shard_map/ppermute | solution.py:313
  175.3 62.4 %all-to-all-start.2 = ((bf16[64,8,8,256]{3,2,1,0:T(8,128)(2,1)}), bf16[64,8,8,256]{3,2,1,0:T(8,128)(2,1)}, u32[]{:S(2)}, u32[]{:S(2)}) async-start(bf16[64,8,8,256]{3,2,1,0:T(8,128)(2,1)} %cut_chunk.5), calls=%async_computation.2 | async-start | bytes 4194304 | tf_op jit(solution)/shard_map/all_to_all | solution.py:306
  186.5 4.9 %copy-start.2 = (bf16[4096,256]{1,0:T(8,128)(2,1)S(1)}, bf16[4096,256]{1,0:T(8,128)(2,1)}, u32[]{:S(2)}) copy-start(bf16[4096,256]{1,0:T(8,128)(2,1)} %copy-done.1) | copy-start | bytes 6291460
  186.5 4.9 %copy-start.5 = (bf16[4096,256]{1,0:T(8,128)(2,1)S(1)}, bf16[4096,256]{1,0:T(8,128)(2,1)}, u32[]{:S(2)}) copy-start(bf16[4096,256]{1,0:T(8,128)(2,1)} %copy-done.4) | copy-start | bytes 6291460
  191.4 6.8 %copy-start.8 = (bf16[4096,256]{1,0:T(8,128)(2,1)}, bf16[4096,256]{1,0:T(8,128)(2,1)S(1)}, u32[]{:S(2)}) copy-start(bf16[4096,256]{1,0:T(8,128)(2,1)S(1)} %fit_chunk.4.f1) | copy-start | bytes 6291460
  198.3 14.1 %collective-permute-start.4 = (bf16[30,32,128]{2,1,0:T(8,128)(2,1)}, bf16[30,32,128]{2,1,0:T(8,128)(2,1)}, u32[]{:S(2)}, u32[]{:S(2)}) collective-permute-start(bf16[30,32,128]{2,1,0:T(8,128)(2,1)} %get-tuple-element.27), channel_id=1, source_target_pairs={{0,192},{64,0},{128,64},{192,128},{1,193},{65,1},{129,65},{193,129... | collective-permute-start | bytes 737288 | tf_op jit(solution)/shard_map/ppermute | solution.py:222
  201.3 11.9 %collective-permute-start.3 = (bf16[30,32,128]{2,1,0:T(8,128)(2,1)}, bf16[30,32,128]{2,1,0:T(8,128)(2,1)}, u32[]{:S(2)}, u32[]{:S(2)}) collective-permute-start(bf16[30,32,128]{2,1,0:T(8,128)(2,1)} %get-tuple-element.26), channel_id=1, source_target_pairs={{0,128},{64,192},{128,0},{192,64},{1,129},{65,193},{129,1},{193,65... | collective-permute-start | bytes 737288 | tf_op jit(solution)/shard_map/ppermute | solution.py:222
  201.9 14.0 %collective-permute-start.2 = (bf16[30,32,128]{2,1,0:T(8,128)(2,1)S(1)}, bf16[30,32,128]{2,1,0:T(8,128)(2,1)}, u32[]{:S(2)}, u32[]{:S(2)}) collective-permute-start(bf16[30,32,128]{2,1,0:T(8,128)(2,1)S(1)} %get-tuple-element.25), channel_id=1, source_target_pairs={{0,64},{64,128},{128,192},{192,0},{1,65},{65,129},{129,193},{193,1... | collective-permute-start | bytes 737288 | tf_op jit(solution)/shard_map/ppermute | solution.py:222
  249.1 7.9 %copy-start.3 = (f32[16,32,128]{2,1,0:T(8,128)}, f32[16,32,128]{2,1,0:T(8,128)S(1)}, u32[]{:S(2)}) copy-start(f32[16,32,128]{2,1,0:T(8,128)S(1)} %get-tuple-element.29.late_ref) | copy-start | bytes 786436
  249.1 14.8 %copy-start.15 = (s32[127,2]{0,1:T(2,128)S(1)}, s32[127,2]{0,1:T(2,128)}, u32[]{:S(2)}) copy-start(s32[127,2]{0,1:T(2,128)} %param.6) | copy-start | bytes 3052
  249.1 8.0 %collective-permute-start.5 = (bf16[18,32,128]{2,1,0:T(8,128)(2,1)S(1)}, bf16[18,32,128]{2,1,0:T(8,128)(2,1)S(1)}, u32[]{:S(2)}, u32[]{:S(2)}) collective-permute-start(bf16[18,32,128]{2,1,0:T(8,128)(2,1)S(1)} %get-tuple-element.30), channel_id=1, source_target_pairs={{0,64},{64,128},{128,192},{192,0},{1,65},{65,129},{129,193},{193,1... | collective-permute-start | bytes 442376 | tf_op jit(solution)/shard_map/ppermute | solution.py:222
  250.7 8.6 %collective-permute-start.6 = (bf16[18,32,128]{2,1,0:T(8,128)(2,1)S(1)}, bf16[18,32,128]{2,1,0:T(8,128)(2,1)S(1)}, u32[]{:S(2)}, u32[]{:S(2)}) collective-permute-start(bf16[18,32,128]{2,1,0:T(8,128)(2,1)S(1)} %get-tuple-element.31), channel_id=1, source_target_pairs={{0,128},{64,192},{128,0},{192,64},{1,129},{65,193},{129,1},{193,65... | collective-permute-start | bytes 442376 | tf_op jit(solution)/shard_map/ppermute | solution.py:222
  253.6 5.7 %collective-permute-start.7 = (bf16[18,32,128]{2,1,0:T(8,128)(2,1)S(1)}, bf16[18,32,128]{2,1,0:T(8,128)(2,1)S(1)}, u32[]{:S(2)}, u32[]{:S(2)}) collective-permute-start(bf16[18,32,128]{2,1,0:T(8,128)(2,1)S(1)} %get-tuple-element.32), channel_id=1, source_target_pairs={{0,192},{64,0},{128,64},{192,128},{1,193},{65,1},{129,65},{193,129... | collective-permute-start | bytes 442376 | tf_op jit(solution)/shard_map/ppermute | solution.py:222
  262.2 5.9 %collective-permute-start.8 = (bf16[24,32,128]{2,1,0:T(8,128)(2,1)}, bf16[24,32,128]{2,1,0:T(8,128)(2,1)S(1)}, u32[]{:S(2)}, u32[]{:S(2)}) collective-permute-start(bf16[24,32,128]{2,1,0:T(8,128)(2,1)} %get-tuple-element.34), channel_id=1, source_target_pairs={{0,8},{1,9},{2,10},{3,11},{4,12},{5,13},{6,14},{7,15},{8,0},{9,1},... | collective-permute-start | bytes 589832 | tf_op jit(solution)/shard_map/ppermute | solution.py:325
  270.6 7.2 %collective-permute-start.11 = (f32[32,640]{1,0:T(8,128)}, f32[32,640]{1,0:T(8,128)S(1)}, u32[]{:S(2)}, u32[]{:S(2)}) collective-permute-start(f32[32,640]{1,0:T(8,128)} %get-tuple-element.38), channel_id=1, source_target_pairs={{0,48},{1,49},{2,50},{3,51},{4,52},{5,53},{6,54},{7,55},{8,56},{9,... | collective-permute-start | bytes 245768 | tf_op jit(solution)/shard_map/ppermute | solution.py:328
  271.7 10.0 %collective-permute-start.10 = (f32[32,640]{1,0:T(8,128)}, f32[32,640]{1,0:T(8,128)S(1)}, u32[]{:S(2)}, u32[]{:S(2)}) collective-permute-start(f32[32,640]{1,0:T(8,128)} %get-tuple-element.37), channel_id=1, source_target_pairs={{0,32},{1,33},{2,34},{3,35},{4,36},{5,37},{6,38},{7,39},{8,40},{9,... | collective-permute-start | bytes 245768 | tf_op jit(solution)/shard_map/ppermute | solution.py:328
  274.6 7.4 %collective-permute-start.9 = (f32[32,640]{1,0:T(8,128)}, f32[32,640]{1,0:T(8,128)S(1)}, u32[]{:S(2)}, u32[]{:S(2)}) collective-permute-start(f32[32,640]{1,0:T(8,128)} %get-tuple-element.36), channel_id=1, source_target_pairs={{0,16},{1,17},{2,18},{3,19},{4,20},{5,21},{6,22},{7,23},{8,24},{9,... | collective-permute-start | bytes 245768 | tf_op jit(solution)/shard_map/ppermute | solution.py:328
  282.9 12.7 %collective-permute-start.12 = (f32[32,640]{1,0:T(8,128)S(1)}, f32[32,640]{1,0:T(8,128)S(1)}, u32[]{:S(2)}, u32[]{:S(2)}) collective-permute-start(f32[32,640]{1,0:T(8,128)S(1)} %add_add_fusion.1), channel_id=1, source_target_pairs={{0,0},{1,8},{2,16},{3,24},{4,32},{5,40},{6,48},{7,56},{8,1},{9,9},... | collective-permute-start | bytes 245768 | tf_op jit(solution)/shard_map/ppermute | solution.py:329
  (8 other events, 11.0 us)

commit v3 on v2

v3 whole, which is shorter than its diff:
```python
import jax
import jax.numpy as jnp
from jax import lax
from jax.experimental import pallas as pl
from jax.experimental.pallas import tpu as pltpu
from jax.sharding import PartitionSpec as P

BS = 128
QB = 128
NZ = 8
NC = 8
NY = 4
PAIR = 2 * BS
BAND = 5
PART = BS // NY
FIRST = (0, 7, 1, 2, 5, 6)
LAST = (3, 4)
VMEM = pltpu.MemorySpace.VMEM
SMEM = pltpu.MemorySpace.SMEM

EARLY_PRODUCTS = (((0, 1), (0, 1, 2)), ((6, 7), (5, 6, 7)), ((2, 5), (2, 5)))
LATE_PRODUCT = ((3, 4), (1, 2, 3, 4, 5, 6))


def tiles_of(products):
    found = {}
    for n, (rows, cols) in enumerate(products):
        for s, r in enumerate(rows):
            for t, k in enumerate(cols):
                if abs(k - r) <= 2:
                    found[r, k - r] = (n, s, t, False)
    for n, (rows, cols) in enumerate(products):
        for s, r in enumerate(rows):
            for t, k in enumerate(cols):
                if abs(k - r) <= 2 and 0 <= k < NC and (k, r - k) not in found:
                    found[k, r - k] = (n, s, t, True)
    return found


EARLY_TILES = tiles_of(EARLY_PRODUCTS)
LATE_TILES = tiles_of((LATE_PRODUCT,))
STRANGE = ((0, -2), (7, 2), (0, -1), (1, -2), (6, 2), (7, 1))


def ordered(slots):
    off = [k for k in slots if k[1] != 0]
    return off + [k for k in slots if k[1] == 0], len(off)


EARLY, EARLY_OFF = ordered(EARLY_TILES)
LATE, LATE_OFF = ordered(STRANGE + tuple(LATE_TILES))


def sent_slots(slots, off):
    return 2 * len(slots) - off


def runs(blocks):
    found = []
    for n, b in enumerate(blocks):
        if found and found[-1][0] + found[-1][2] == b * BS:
            found[-1][2] += BS
        else:
            found.append([b * BS, n * BS, BS])
    return found


def cut_kernel(source, out_ref, held, sems, *, blocks):
    half = NZ * NC // 2

    def gather(part):
        def one(n, carry):
            k = part * half + n
            z, c = k // NC, k % NC
            for start, at, width in runs(blocks):
                begin = pl.multiple_of(c * 1024 + start, BS)
                pltpu.make_async_copy(
                    source.at[:, z, :, pl.ds(begin, width)], held.at[k, :, :, pl.ds(at, width)], sems.at[part]
                ).start()
            return carry

        lax.fori_loop(0, half, one, 0)

    gather(0)
    gather(1)
    writes = []
    for part in range(2):
        here = held.at[pl.ds(part * half, half)]
        pltpu.make_async_copy(here, here, sems.at[part]).wait()
        write = pltpu.make_async_copy(here, out_ref.at[pl.ds(part * half, half)], sems.at[2 + part])
        write.start()
        writes.append(write)
    for write in writes:
        write.wait()


def cut_chunk(integrals, blocks):
    shape = (NZ * NC, 8, 8, BS * len(blocks))
    return pl.pallas_call(
        lambda *refs: cut_kernel(*refs, blocks=blocks),
        out_shape=jax.ShapeDtypeStruct(shape, jnp.bfloat16),
        in_specs=[pl.BlockSpec(memory_space=pl.ANY)],
        out_specs=pl.BlockSpec(memory_space=pl.ANY),
        scratch_shapes=[pltpu.VMEM(shape, jnp.bfloat16), pltpu.SemaphoreType.DMA((4,))],
        compiler_params=pltpu.CompilerParams(vmem_limit_bytes=60 << 20),
        cost_estimate=pl.CostEstimate(flops=0, bytes_accessed=2 * 8192 * shape[3], transcendentals=0),
        name="cut_chunk",
    )(integrals.reshape(8, NZ, 8, NC * 1024))


def turn_rows(rows_ref, perm_ref, turned_ref, first, count):
    def turn(g, carry):
        start = pl.multiple_of(g * 256, 256)
        turned = jnp.dot(perm_ref[...], rows_ref[pl.ds(start, 256), :], preferred_element_type=jnp.float32)
        turned = turned.astype(jnp.bfloat16)
        at = pl.multiple_of(g * 32, 32)
        for i in range(8):
            turned_ref[i, pl.ds(at, 32), :] = turned[i * 32 : (i + 1) * 32]
        return carry

    lax.fori_loop(first, first + count, turn, 0, unroll=4)


def fit_one(metric_ref, turned_ref, mask_ref, i):
    fitted = jnp.dot(metric_ref[...], turned_ref[i], preferred_element_type=jnp.float32)
    out = []
    for b in range(2):
        column = fitted[:, b * BS : (b + 1) * BS]
        pieces = [column[q * QB : (q + 1) * QB] * mask_ref[q, b] for q in range(4)]
        out.append(jnp.concatenate(pieces, axis=0).astype(jnp.bfloat16))
    return out


def fit_kernel(rows_ref, perm_ref, metric_ref, mask_ref, out_a, out_b, turned_ref):
    turn_rows(rows_ref, perm_ref, turned_ref, 0, 16)

    def fit(i, carry):
        at = pl.multiple_of(i * 512, 512)
        out_a[pl.ds(at, 512), :], out_b[pl.ds(at, 512), :] = fit_one(metric_ref, turned_ref, mask_ref, i)
        return carry

    lax.fori_loop(0, 8, fit, 0, unroll=2)


def whole(shape, at=None):
    return pl.BlockSpec(shape, lambda g: at or (0,) * len(shape))


def fit_chunk(rows, at, perm, metric, mask):
    return pl.pallas_call(
        fit_kernel,
        grid=(1,),
        out_shape=[jax.ShapeDtypeStruct((4096, BS), jnp.bfloat16)] * 2,
        in_specs=[
            whole((4096, PAIR), (0, at)),
            whole((256, 256)),
            whole((512, 512)),
            pl.BlockSpec(memory_space=SMEM),
        ],
        out_specs=[whole((4096, BS))] * 2,
        scratch_shapes=[pltpu.VMEM((8, 512, PAIR), jnp.bfloat16)],
        compiler_params=pltpu.CompilerParams(vmem_limit_bytes=24 << 20),
        cost_estimate=pl.CostEstimate(flops=2 * 4096 * PAIR * 768, bytes_accessed=4 * 4096 * PAIR, transcendentals=0),
        name="fit_chunk",
    )(rows, perm, metric, mask)


def put_slot(tile_ref, row, col, n, diagonal, slots, off, y, own_ref, out_refs):
    for d in range(NY):
        at = pl.multiple_of(row * BS + lax.rem(y + d, NY) * PART, PART)
        piece = tile_ref[pl.ds(at, PART), col * BS : (col + 1) * BS]
        if d == 0:
            own_ref[n] = piece
            continue
        high = piece.astype(jnp.bfloat16)
        out_refs[d - 1][n] = high
        if diagonal:
            out_refs[d - 1][n + len(slots) - off] = (piece - high.astype(jnp.float32)).astype(jnp.bfloat16)


def put_tiles(found, tiles, flip_ref, slots, off, y, own_ref, out_refs):
    flips = 0
    for r, e in slots:
        if (r, e) not in found:
            continue
        product, s, t, turned = found[r, e]
        n = slots.index((r, e))
        if not turned:
            put_slot(tiles[product], s, t, n, e == 0, slots, off, y, own_ref, out_refs)
            continue
        flip_ref[flips] = tiles[product][s * BS : (s + 1) * BS, t * BS : (t + 1) * BS].T
        put_slot(flip_ref.at[flips], 0, 0, n, False, slots, off, y, own_ref, out_refs)
        flips += 1


EARLY_BLOCKS = (0, 1, 2, 5, 6, 7)


def early_kernel(y_ref, *refs):
    blocks = dict(zip(EARLY_BLOCKS, refs[:6]))
    own_ref, o1, o2, o3, t0, t1, t2, flip_ref = refs[6:]
    tiles = (t0, t1, t2)
    for n, (rows, cols) in enumerate(EARLY_PRODUCTS):
        left = jnp.concatenate([blocks[r][...] for r in rows], axis=1).T
        right = jnp.concatenate([blocks[k][...] for k in cols], axis=1)
        tiles[n][...] = jnp.dot(left, right, preferred_element_type=jnp.float32)
    put_tiles(EARLY_TILES, tiles, flip_ref, EARLY, EARLY_OFF, y_ref[0], own_ref, (o1, o2, o3))


def edge_kernel(below, f0, f1, f6, f7, above, down_ref, up_ref, own_ref):
    low = jnp.dot(
        below[...].T, jnp.concatenate([f0[...], f1[...]], axis=1), preferred_element_type=jnp.float32
    )
    high = jnp.dot(
        above[...].T, jnp.concatenate([f6[...], f7[...]], axis=1), preferred_element_type=jnp.float32
    )
    down_ref[...] = low[:, BS:]
    up_ref[...] = high[:, :BS]
    own_ref[0] = low[:, :BS].T
    own_ref[1] = low[:, BS:].T
    own_ref[2] = high[:, :BS].T
    own_ref[3] = high[:, BS:].T


def edge_tiles(below, f0, f1, f6, f7, above):
    tile = jax.ShapeDtypeStruct((BS, BS), jnp.float32)
    return pl.pallas_call(
        edge_kernel,
        out_shape=[tile, tile, jax.ShapeDtypeStruct((4, BS, BS), jnp.float32)],
        in_specs=[pl.BlockSpec(memory_space=VMEM)] * 6,
        out_specs=[pl.BlockSpec(memory_space=VMEM)] * 3,
        compiler_params=pltpu.CompilerParams(vmem_limit_bytes=24 << 20),
        cost_estimate=pl.CostEstimate(flops=2 * 4096 * 256 * 256, bytes_accessed=6 << 20, transcendentals=0),
        name="edge_tiles",
    )(below, f0, f1, f6, f7, above)


def late_kernel(y_ref, mask_ref, rows_hbm, f1_hbm, f2_hbm, f5_hbm, f6_hbm, perm_ref, metric_ref, from_below, from_above, edges, own_ref, o1, o2, o3, rows_ref, turned_ref, left_ref, right_ref, tiles_ref, flip_ref, row_sems, sems):
    feeds = []
    for n in range(4):
        piece = pl.ds(n * 1024, 1024)
        feeds.append(pltpu.make_async_copy(rows_hbm.at[piece], rows_ref.at[piece], row_sems.at[n]))
    fits = [
        pltpu.make_async_copy(f, right_ref.at[n], sems.at[n]) for n, f in enumerate((f1_hbm, f2_hbm, f5_hbm, f6_hbm))
    ]
    for copy in feeds + fits:
        copy.start()
    for n, feed in enumerate(feeds):
        feed.wait()
        turn_rows(rows_ref, perm_ref, turned_ref, 4 * n, 4)

    def step(i, carry):
        at = pl.ds(pl.multiple_of(i * 512, 512), 512)
        left_ref[at, :BS], left_ref[at, BS:] = fit_one(metric_ref, turned_ref, mask_ref, i)
        return carry

    lax.fori_loop(0, 8, step, 0, unroll=2)
    for copy in fits:
        copy.wait()
    f1, f2, f5, f6 = [right_ref[n] for n in range(4)]
    right = jnp.concatenate([f1, f2, left_ref[...], f5, f6], axis=1)
    tiles_ref[...] = jnp.dot(left_ref[...].T, right, preferred_element_type=jnp.float32)
    y = y_ref[0]
    for tile_ref, (r, e) in zip((from_below, from_above, *(edges.at[k] for k in range(4))), STRANGE):
        put_slot(tile_ref, 0, 0, LATE.index((r, e)), False, LATE, LATE_OFF, y, own_ref, (o1, o2, o3))
    put_tiles(LATE_TILES, (tiles_ref,), flip_ref, LATE, LATE_OFF, y, own_ref, (o1, o2, o3))


def exchange_shapes(slots, off):
    sent = jax.ShapeDtypeStruct((sent_slots(slots, off), PART, BS), jnp.bfloat16)
    return [jax.ShapeDtypeStruct((len(slots), PART, BS), jnp.float32)] + [sent] * 3


def early_tiles(y, blocks):
    return pl.pallas_call(
        early_kernel,
        out_shape=exchange_shapes(EARLY, EARLY_OFF),
        in_specs=[pl.BlockSpec(memory_space=SMEM)] + [pl.BlockSpec(memory_space=VMEM)] * 6,
        out_specs=[pl.BlockSpec(memory_space=VMEM)] * 4,
        scratch_shapes=[
            pltpu.VMEM((PAIR, 3 * BS), jnp.float32),
            pltpu.VMEM((PAIR, 3 * BS), jnp.float32),
            pltpu.VMEM((PAIR, PAIR), jnp.float32),
            pltpu.VMEM((4, BS, BS), jnp.float32),
        ],
        compiler_params=pltpu.CompilerParams(vmem_limit_bytes=40 << 20),
        cost_estimate=pl.CostEstimate(flops=2 * 4096 * 256 * 1024, bytes_accessed=7 << 20, transcendentals=0),
        name="early_tiles",
    )(y, *blocks)


def late_tiles(y, mask, rows, f1, f2, f5, f6, perm, metric, from_below, from_above, edges):
    return pl.pallas_call(
        late_kernel,
        out_shape=exchange_shapes(LATE, LATE_OFF),
        in_specs=[pl.BlockSpec(memory_space=SMEM)] * 2
        + [pl.BlockSpec(memory_space=pl.ANY)] * 5
        + [pl.BlockSpec(memory_space=VMEM)] * 5,
        out_specs=[pl.BlockSpec(memory_space=VMEM)] * 4,
        scratch_shapes=[
            pltpu.VMEM((4096, PAIR), jnp.bfloat16),
            pltpu.VMEM((8, 512, PAIR), jnp.bfloat16),
            pltpu.VMEM((4096, PAIR), jnp.bfloat16),
            pltpu.VMEM((4, 4096, BS), jnp.bfloat16),
            pltpu.VMEM((PAIR, 6 * BS), jnp.float32),
            pltpu.VMEM((6, BS, BS), jnp.float32),
            pltpu.SemaphoreType.DMA((4,)),
            pltpu.SemaphoreType.DMA((4,)),
        ],
        compiler_params=pltpu.CompilerParams(vmem_limit_bytes=60 << 20),
        cost_estimate=pl.CostEstimate(flops=2 * 4096 * 256 * 1536, bytes_accessed=8 << 20, transcendentals=0),
        name="late_tiles",
    )(y, mask, rows, f1, f2, f5, f6, perm, metric, from_below, from_above, edges)


def over_domains(sent):
    return [lax.ppermute(s, "aux", [(a, (a + d) % NY) for a in range(NY)]) for d, s in enumerate(sent, 1)]


def gathered(own_ref, got_refs, n, e, slots, off):
    value = own_ref[n]
    for got in got_refs:
        value = value + got[n].astype(jnp.float32)
        if e == 0:
            value = value + got[n + len(slots) - off].astype(jnp.float32)
    return value


def early_sum_kernel(own_ref, g1, g2, g3, out_ref):
    for n, (r, e) in enumerate(EARLY):
        out_ref[n] = gathered(own_ref, (g1, g2, g3), n, e, EARLY, EARLY_OFF)


def early_sum(own, got):
    return pl.pallas_call(
        early_sum_kernel,
        out_shape=jax.ShapeDtypeStruct(own.shape, jnp.float32),
        in_specs=[pl.BlockSpec(memory_space=VMEM)] * 4,
        out_specs=pl.BlockSpec(memory_space=VMEM),
        compiler_params=pltpu.CompilerParams(vmem_limit_bytes=16 << 20),
        name="early_sum",
    )(own, *got)


def merge_kernel(odd_ref, early_ref, late_ref, g1, g2, g3, own_ref, out_ref, band_ref):
    for n, (r, e) in enumerate(EARLY):
        band_ref[r, e + 2] = early_ref[n]
    for n, (r, e) in enumerate(LATE):
        band_ref[r, e + 2] = gathered(late_ref, (g1, g2, g3), n, e, LATE, LATE_OFF)
    odd = odd_ref[0]
    for k in range(4):
        for slot in range(BAND):
            own_ref[k, slot] = band_ref[2 * k + odd, slot]
            value = band_ref[2 * k + 1 - odd, slot]
            high = value.astype(jnp.bfloat16)
            out_ref[k * 6 + slot] = high
            if slot == 2:
                out_ref[k * 6 + 5] = (value - high.astype(jnp.float32)).astype(jnp.bfloat16)


def merge(odd, early, late, got):
    return pl.pallas_call(
        merge_kernel,
        out_shape=[
            jax.ShapeDtypeStruct((4, BAND, PART, BS), jnp.float32),
            jax.ShapeDtypeStruct((24, PART, BS), jnp.bfloat16),
        ],
        in_specs=[pl.BlockSpec(memory_space=SMEM)] + [pl.BlockSpec(memory_space=VMEM)] * 5,
        out_specs=[pl.BlockSpec(memory_space=VMEM)] * 2,
        scratch_shapes=[pltpu.VMEM((NC, BAND, PART, BS), jnp.float32)],
        compiler_params=pltpu.CompilerParams(vmem_limit_bytes=16 << 20),
        name="merge",
    )(odd, early, late, *got)


def settle_kernel(half_ref, own_ref, got_ref, o0, o1, o2, o3):
    for j, out in enumerate((o0, o1, o2, o3)):
        k = lax.rem(half_ref[0] + j, 4)
        for slot in range(BAND):
            value = own_ref[k, slot] + got_ref[k * 6 + slot].astype(jnp.float32)
            if slot == 2:
                value = value + got_ref[k * 6 + 5].astype(jnp.float32)
            out[:, slot * BS : (slot + 1) * BS] = value


def settle(half, own, got):
    return pl.pallas_call(
        settle_kernel,
        out_shape=[jax.ShapeDtypeStruct((PART, BAND * BS), jnp.float32)] * 4,
        in_specs=[pl.BlockSpec(memory_space=SMEM)] + [pl.BlockSpec(memory_space=VMEM)] * 2,
        out_specs=[pl.BlockSpec(memory_space=VMEM)] * 4,
        compiler_params=pltpu.CompilerParams(vmem_limit_bytes=16 << 20),
        name="settle",
    )(half, own, got)


def local(integrals, metric, pair_list, aux_mask):
    blk = lax.axis_index("blk")
    y = jnp.full((1,), lax.axis_index("aux"), jnp.int32)
    z, c = blk // NC, blk % NC
    grid = [(k // NC, k % NC) for k in range(NZ * NC)]
    up = [(zz * NC + cc, zz * NC + cc + 1) for zz, cc in grid if cc < NC - 1]
    down = [(b, a) for a, b in up]

    row = lax.broadcasted_iota(jnp.int32, (256, 256), 0)
    col = lax.broadcasted_iota(jnp.int32, (256, 256), 1)
    perm = ((row // 32 == col % 8) & (row % 32 == col // 8)).astype(jnp.bfloat16)
    own_mask = lax.dynamic_slice(aux_mask, (0, c * 8), (4, 8)).astype(jnp.float32)
    mask_of = lambda *blocks: jnp.stack([own_mask[:, b] for b in blocks], axis=1)

    e = jnp.arange(BAND, dtype=jnp.int32) - 2
    low, high = blk + jnp.minimum(e, 0), blk + jnp.maximum(e, 0)
    hits = (pair_list[:, 0][:, None] == low[None]) & (pair_list[:, 1][:, None] == high[None])
    scale = jnp.repeat(jnp.sum(hits.astype(jnp.float32), axis=0), BS)

    def spread(blocks, source):
        got = lax.all_to_all(cut_chunk(source, blocks), "blk", split_axis=0, concat_axis=0, tiled=True)
        return got.reshape(4096, BS * len(blocks))

    rows = spread(FIRST, integrals)
    last = spread(LAST, integrals)
    f0, f7 = fit_chunk(rows, 0, perm, metric, mask_of(0, 7))
    above = lax.ppermute(f0, "blk", down)
    below = lax.ppermute(f7, "blk", up)
    f1, f2 = fit_chunk(rows, 1, perm, metric, mask_of(1, 2))
    f5, f6 = fit_chunk(rows, 2, perm, metric, mask_of(5, 6))

    early, *sent = early_tiles(y, (f0, f1, f2, f5, f6, f7))
    early = early_sum(early, over_domains(sent))
    to_below, to_above, edges = edge_tiles(below, f0, f1, f6, f7, above)
    from_above = lax.ppermute(to_below, "blk", down)
    from_below = lax.ppermute(to_above, "blk", up)
    early, from_above, from_below, last = lax.optimization_barrier((early, from_above, from_below, last))

    late, *sent = late_tiles(y, mask_of(3, 4), last, f1, f2, f5, f6, perm, metric, from_below, from_above, edges)
    own, sent = merge(jnp.full((1,), z % 2, jnp.int32), early, late, over_domains(sent))
    got = lax.ppermute(sent, "blk", [(zz * NC + cc, (zz ^ 1) * NC + cc) for zz, cc in grid])
    total, *sent = settle(jnp.full((1,), z // 2, jnp.int32), own, got)
    for j, s in enumerate(sent, 1):
        total = total + lax.ppermute(s, "blk", [(zz * NC + cc, (zz + 2 * j) % NZ * NC + cc) for zz, cc in grid])
    total = lax.ppermute(total, "blk", [(zz * NC + cc, cc * NC + zz) for zz, cc in grid])
    return (total * scale[None, :])[None]


def solution(mesh):
    return jax.shard_map(
        local,
        mesh=mesh,
        in_specs=(P(("aux", "blk"), None, None), P("aux", None), P(), P("aux", None)),
        out_specs=P("blk", "aux", None),
        check_vma=False,
    )
```

time: 297 us -> 271 us (0.912)
  waiting for transfers between devices: 178 us -> 166 us
  local copies, waits for them, and re-layouts: 10.7 us -> 3.79 us
    ppermute x1, waiting for transfers between devices: 36.2 us -> 0.01 us  [local(): above = lax.ppermute(f0, 'blk', down)]
    all_to_all x3 -> x2, waiting for transfers between devices: 114 us -> 146 us  [spread(): lax.all_to_all(cut_chunk(source, blocks), 'blk', split_axis=0, concat_axi...]
    all_to_all x3 -> x2, starting transfers between devices: 29 us -> 17.8 us  [spread(): lax.all_to_all(cut_chunk(source, blocks), 'blk', split_axis=0, concat_axi...]
    ppermute x6, waiting for transfers between devices: 13.8 us -> 6.68 us  [over_domains(): lax.ppermute(s, 'aux', [(a, (a + d) % NY) for a in range(NY)])]
    ppermute x1 -> x3, starting transfers between devices: 2.1 us -> 7.35 us  [the longest x1 3.2 us: local(): from_above = lax.ppermute(to_below, 'blk', down)]
    unnamed x32 -> x26, local copies, waits for them, and re-layouts: 8.1 us -> 3.04 us
    pallas_call x6 -> x7, Pallas kernels: 25.6 us -> 27.2 us  [the longest x3 16.1 us: fit_chunk(): pl.pallas_call(fit_kernel, grid=(1,), out_shape=[jax.ShapeDtypeStruct((40...]
  transfers between devices with their start and end apart: 16 -> 17, of which waited for: 12 -> 9; matrix products, arithmetic and copies ran while one was open for 2% -> 1% of each run, Pallas kernels for 9% -> 10%
where the time goes in v3:
time: 271 us; the launch traced here: 270 us
  waiting for transfers between devices  166 us (61%)
  starting transfers between devices  56.4 us (21%)
  Pallas kernels  41.6 us (15%)
  local copies, waits for them, and re-layouts  3.79 us (1%)
    all_to_all x2, waiting for transfers between devices, spread(): lax.all_to_all(cut_chunk(source, blocks), 'blk', split_axis=0, concat_axi...  146 us
    all_to_all x2, starting transfers between devices, spread(): lax.all_to_all(cut_chunk(source, blocks), 'blk', split_axis=0, concat_axi...  17.8 us
    pallas_call x3, Pallas kernels, fit_chunk(): pl.pallas_call(fit_kernel, grid=(1,), out_shape=[jax.ShapeDtypeStruct((40...  16.1 us
    ppermute x6, starting transfers between devices, over_domains(): lax.ppermute(s, 'aux', [(a, (a + d) % NY) for a in range(NY)])  11.8 us
    pallas_call x1, Pallas kernels, late_tiles(): pl.pallas_call(late_kernel, out_shape=exchange_shapes(LATE, LATE_OFF), in...  8.86 us
    ppermute x1, starting transfers between devices, local(): lax.ppermute(total, 'blk', [(zz * NC + cc, cc * NC + zz) for zz, cc in gr...  8.3 us
    pallas_call x2, Pallas kernels, cut_chunk(): pl.pallas_call(lambda *refs: cut_kernel(*refs, blocks=blocks), out_shape=...  7.75 us
    ppermute x6, waiting for transfers between devices, over_domains(): lax.ppermute(s, 'aux', [(a, (a + d) % NY) for a in range(NY)])  6.68 us
  transfers between devices with their start and end apart: 17, of which 9 were waited for; matrix products, arithmetic and copies ran while one was open for 1% of the time, Pallas kernels for 10%

profile of v3, /device:TPU:4, one launch (start us, length us, event | category | flops | bytes accessed | tf_op | source)
XLA Modules:
  0.0 269.9 jit_solution(15088416791607129099)
XLA Ops:
  0.0 4.9 %cut_chunk.2 = bf16[64,8,8,768]{3,2,1,0:T(8,128)(2,1)} custom-call(bf16[8,8,8,8192]{3,2,1,0:T(8,128)(2,1)} %bitcast.14), custom_call_target="tpu_custom_call" | custom-call | bytes 12582912 | tf_op jit(solution)/shard_map/cut_chunk/pallas_call | solution.py:99
  5.0 12.2 %all-to-all-start = ((bf16[64,8,8,768]{3,2,1,0:T(8,128)(2,1)}), bf16[64,8,8,768]{3,2,1,0:T(8,128)(2,1)}, u32[]{:S(2)}, u32[]{:S(2)}) async-start(bf16[64,8,8,768]{3,2,1,0:T(8,128)(2,1)} %cut_chunk.2), calls=%async_computation | async-start | bytes 12582912 | tf_op jit(solution)/shard_map/all_to_all | solution.py:417
  17.2 2.8 %cut_chunk.3 = bf16[64,8,8,256]{3,2,1,0:T(8,128)(2,1)} custom-call(bf16[8,8,8,8192]{3,2,1,0:T(8,128)(2,1)} %bitcast.15), custom_call_target="tpu_custom_call" | custom-call | bytes 4194304 | tf_op jit(solution)/shard_map/cut_chunk/pallas_call | solution.py:99
  20.0 138.3 %all-to-all-done = bf16[64,8,8,768]{3,2,1,0:T(8,128)(2,1)} async-done(((bf16[64,8,8,768]{3,2,1,0:T(8,128)(2,1)}), bf16[64,8,8,768]{3,2,1,0:T(8,128)(2,1)}, u32[]{:S(2)}, u32[]{:S(2)}) %all-to-all-start) | async-done | bytes 6291488 | tf_op jit(solution)/shard_map/all_to_all | solution.py:417
  158.3 5.7 %all-to-all-start.1 = ((bf16[64,8,8,256]{3,2,1,0:T(8,128)(2,1)}), bf16[64,8,8,256]{3,2,1,0:T(8,128)(2,1)S(1)}, u32[]{:S(2)}, u32[]{:S(2)}) async-start(bf16[64,8,8,256]{3,2,1,0:T(8,128)(2,1)} %cut_chunk.3), calls=%async_computation.1 | async-start | bytes 4194304 | tf_op jit(solution)/shard_map/all_to_all | solution.py:417
  164.6 6.0 %fit_chunk.3 = (bf16[4096,128]{1,0:T(8,128)(2,1)}, bf16[4096,128]{1,0:T(8,128)(2,1)}) custom-call(bf16[4096,768]{1,0:T(8,128)(2,1)} %bitcast.4.rows_ref, bf16[256,256]{1,0:T(8,128)(2,1)S(1)} %fusion.1.perm_ref, bf16[512,512]{1,0:T(8,128)(2,1)S(1)} %copy-done, f32[4,2]{1,0:T(4,128)S(1)} %pad_maximum_fusion.mask_ref), custom_call_target="tpu_custom_call" | custom-call | flops 1610612736 | bytes 4194304 | tf_op jit(solution)/shard_map/fit_chunk/pallas_call | solution.py:150
  172.7 3.5 %collective-permute-start.4 = (bf16[4096,128]{1,0:T(8,128)(2,1)}, bf16[4096,128]{1,0:T(8,128)(2,1)}, u32[]{:S(2)}, u32[]{:S(2)}) collective-permute-start(bf16[4096,128]{1,0:T(8,128)(2,1)} %get-tuple-element.32.refs_0_.f0), channel_id=1, source_target_pairs={{1,0},{2,1},{3,2},{4,3},{5,4},{6,5},{7,6},{9,8},{10,9},{11,10},{12... | collective-permute-start | bytes 3145736 | tf_op jit(solution)/shard_map/ppermute | solution.py:423
  176.8 4.7 %fit_chunk.4 = (bf16[4096,128]{1,0:T(8,128)(2,1)S(1)}, bf16[4096,128]{1,0:T(8,128)(2,1)S(1)}) custom-call(bf16[4096,768]{1,0:T(8,128)(2,1)} %bitcast.4.rows_ref, bf16[256,256]{1,0:T(8,128)(2,1)S(1)} %fusion.1.perm_ref, bf16[512,512]{1,0:T(8,128)(2,1)S(1)} %copy-done, f32[4,2]{1,0:T(4,128)S(1)} %get-tuple-element.61.mask_ref), custom_call_target="tpu_custom_call" | custom-call | flops 1610612736 | bytes 4194304 | tf_op jit(solution)/shard_map/fit_chunk/pallas_call | solution.py:150
  181.5 5.4 %fit_chunk.5 = (bf16[4096,128]{1,0:T(8,128)(2,1)S(1)}, bf16[4096,128]{1,0:T(8,128)(2,1)S(1)}) custom-call(bf16[4096,768]{1,0:T(8,128)(2,1)} %bitcast.4.rows_ref, bf16[256,256]{1,0:T(8,128)(2,1)S(1)} %fusion.1.perm_ref, bf16[512,512]{1,0:T(8,128)(2,1)S(1)} %copy-done, f32[4,2]{1,0:T(4,128)S(1)} %get-tuple-element.60.mask_ref), custom_call_target="tpu_custom_call" | custom-call | flops 1610612736 | bytes 4194304 | tf_op jit(solution)/shard_map/fit_chunk/pallas_call | solution.py:150
  187.0 5.4 %early_tiles.1 = (f32[18,32,128]{2,1,0:T(8,128)S(1)}, bf16[24,32,128]{2,1,0:T(8,128)(2,1)S(1)}, bf16[24,32,128]{2,1,0:T(8,128)(2,1)S(1)}, bf16[24,32,128]{2,1,0:T(8,128)(2,1)S(1)}) custom-call(s32[1]{0:T(128)} %bitcast.2.y_ref, bf16[4096,128]{1,0:T(8,128)(2,1)} %get-tuple-element.32.refs_0_.f0, bf16[4096,128]{1,0:T(8,128)(2,1)S(1)} %get-tuple-element.33.refs_1_.f1.f1_hbm, ...), custom_call_target="tpu_custom_call" | custom-call | flops 2147483648 | bytes 7340032 | tf_op jit(solution)/shard_map/early_tiles/pallas_call | solution.py:275
  194.0 2.9 %collective-permute-start.1 = (bf16[24,32,128]{2,1,0:T(8,128)(2,1)S(1)}, bf16[24,32,128]{2,1,0:T(8,128)(2,1)S(1)}, u32[]{:S(2)}, u32[]{:S(2)}) collective-permute-start(bf16[24,32,128]{2,1,0:T(8,128)(2,1)S(1)} %get-tuple-element.40), channel_id=1, source_target_pairs={{0,128},{64,192},{128,0},{192,64},{1,129},{65,193},{129,1},{193,65... | collective-permute-start | bytes 589832 | tf_op jit(solution)/shard_map/ppermute | solution.py:317
  198.3 3.3 %edge_tiles.1 = (f32[128,128]{1,0:T(8,128)S(1)}, f32[128,128]{1,0:T(8,128)S(1)}, f32[4,128,128]{2,1,0:T(8,128)S(1)}) custom-call(bf16[4096,128]{1,0:T(8,128)(2,1)} %collective-permute-done.3.below, bf16[4096,128]{1,0:T(8,128)(2,1)} %get-tuple-element.32.refs_0_.f0, bf16[4096,128]{1,0:T(8,128)(2,1)S(1)} %get-tuple-element.33.refs_1_.f1.f1_hbm, ...), custom_call_target="tpu_custom_call" | custom-call | flops 536870912 | bytes 6291456 | tf_op jit(solution)/shard_map/edge_tiles/pallas_call | solution.py:227
  202.3 3.2 %collective-permute-start.5 = (f32[128,128]{1,0:T(8,128)S(1)}, f32[128,128]{1,0:T(8,128)S(1)}, u32[]{:S(2)}, u32[]{:S(2)}) collective-permute-start(f32[128,128]{1,0:T(8,128)S(1)} %get-tuple-element.42), channel_id=1, source_target_pairs={{1,0},{2,1},{3,2},{4,3},{5,4},{6,5},{7,6},{9,8},{10,9},{11,10},{12... | collective-permute-start | bytes 196616 | tf_op jit(solution)/shard_map/ppermute | solution.py:431
  205.5 2.1 collective-permute-start.6
  207.7 7.5 %all-to-all-done.1 = bf16[64,8,8,256]{3,2,1,0:T(8,128)(2,1)S(1)} async-done(((bf16[64,8,8,256]{3,2,1,0:T(8,128)(2,1)}), bf16[64,8,8,256]{3,2,1,0:T(8,128)(2,1)S(1)}, u32[]{:S(2)}, u32[]{:S(2)}) %all-to-all-start.1) | async-done | bytes 2097184 | tf_op jit(solution)/shard_map/all_to_all | solution.py:417
  216.6 8.9 %late_tiles.1 = (f32[22,32,128]{2,1,0:T(8,128)}, bf16[24,32,128]{2,1,0:T(8,128)(2,1)}, bf16[24,32,128]{2,1,0:T(8,128)(2,1)}, bf16[24,32,128]{2,1,0:T(8,128)(2,1)}) custom-call(s32[1]{0:T(128)} %bitcast.2.y_ref, f32[4,2]{1,0:T(4,128)} %get-tuple-element.59.mask_ref, bf16[4096,256]{1,0:T(8,128)(2,1)} %bitcast.16, bf16[4096,128]{1,0:T(8,128)(2,1)} %copy-done.2, ...), custom_call_target="tpu_custom_call" | custom-call | flops 3221225472 | bytes 8388608 | tf_op jit(solution)/shard_map/late_tiles/pallas_call | solution.py:293
  227.1 2.9 %collective-permute-start.8 = (bf16[24,32,128]{2,1,0:T(8,128)(2,1)}, bf16[24,32,128]{2,1,0:T(8,128)(2,1)S(1)}, u32[]{:S(2)}, u32[]{:S(2)}) collective-permute-start(bf16[24,32,128]{2,1,0:T(8,128)(2,1)} %get-tuple-element.51), channel_id=1, source_target_pairs={{0,128},{64,192},{128,0},{192,64},{1,129},{65,193},{129,1},{193,65... | collective-permute-start | bytes 589832 | tf_op jit(solution)/shard_map/ppermute | solution.py:317
  231.4 2.3 collective-permute-done.7.g1
  233.7 4.4 %collective-permute-done.8.g2 = bf16[24,32,128]{2,1,0:T(8,128)(2,1)S(1)} collective-permute-done((bf16[24,32,128]{2,1,0:T(8,128)(2,1)}, bf16[24,32,128]{2,1,0:T(8,128)(2,1)S(1)}, u32[]{:S(2)}, u32[]{:S(2)}) %collective-permute-start.8) | collective-permute-done | bytes 196640 | tf_op jit(solution)/shard_map/ppermute | solution.py:317
  240.9 4.0 %collective-permute-done.10.got_ref = bf16[24,32,128]{2,1,0:T(8,128)(2,1)S(1)} collective-permute-done((bf16[24,32,128]{2,1,0:T(8,128)(2,1)S(1)}, bf16[24,32,128]{2,1,0:T(8,128)(2,1)S(1)}, u32[]{:S(2)}, u32[]{:S(2)}) %collective-permute-start.10) | collective-permute-done | bytes 196640 | tf_op jit(solution)/shard_map/ppermute | solution.py:437
  246.2 2.9 %collective-permute-start.12 = (f32[32,640]{1,0:T(8,128)S(1)}, f32[32,640]{1,0:T(8,128)S(1)}, u32[]{:S(2)}, u32[]{:S(2)}) collective-permute-start(f32[32,640]{1,0:T(8,128)S(1)} %get-tuple-element.57), channel_id=1, source_target_pairs={{0,32},{1,33},{2,34},{3,35},{4,36},{5,37},{6,38},{7,39},{8,40},{9,... | collective-permute-start | bytes 245768 | tf_op jit(solution)/shard_map/ppermute | solution.py:440
  251.1 3.0 %collective-permute-done.13 = f32[32,640]{1,0:T(8,128)S(1)} collective-permute-done((f32[32,640]{1,0:T(8,128)S(1)}, f32[32,640]{1,0:T(8,128)S(1)}, u32[]{:S(2)}, u32[]{:S(2)}) %collective-permute-start.13) | collective-permute-done | bytes 81952 | tf_op jit(solution)/shard_map/ppermute | solution.py:440
  256.6 8.3 %collective-permute-start.14 = (f32[32,640]{1,0:T(8,128)S(1)}, f32[32,640]{1,0:T(8,128)S(1)}, u32[]{:S(2)}, u32[]{:S(2)}) collective-permute-start(f32[32,640]{1,0:T(8,128)S(1)} %add_add_fusion), channel_id=1, source_target_pairs={{0,0},{1,8},{2,16},{3,24},{4,32},{5,40},{6,48},{7,56},{8,1},{9,9},... | collective-permute-start | bytes 245768 | tf_op jit(solution)/shard_map/ppermute | solution.py:441
  265.0 4.3 %collective-permute-done.14 = f32[32,640]{1,0:T(8,128)S(1)} collective-permute-done((f32[32,640]{1,0:T(8,128)S(1)}, f32[32,640]{1,0:T(8,128)S(1)}, u32[]{:S(2)}, u32[]{:S(2)}) %collective-permute-start.14) | collective-permute-done | bytes 81952 | tf_op jit(solution)/shard_map/ppermute | solution.py:441
  (64 shorter events, 20.7 us)
Async XLA Ops:
  5.0 153.4 %all-to-all-start = ((bf16[64,8,8,768]{3,2,1,0:T(8,128)(2,1)}), bf16[64,8,8,768]{3,2,1,0:T(8,128)(2,1)}, u32[]{:S(2)}, u32[]{:S(2)}) async-start(bf16[64,8,8,768]{3,2,1,0:T(8,128)(2,1)} %cut_chunk.2), calls=%async_computation | async-start | bytes 12582912 | tf_op jit(solution)/shard_map/all_to_all | solution.py:417
  17.1 146.9 %copy-start.9 = (s32[4,64]{1,0:T(4,128)S(1)}, s32[4,64]{1,0:T(4,128)}, u32[]{:S(2)}) copy-start(s32[4,64]{1,0:T(4,128)} %param.7) | copy-start | bytes 3076
  17.1 147.5 %copy-start = (bf16[512,512]{1,0:T(8,128)(2,1)S(1)}, bf16[512,512]{1,0:T(8,128)(2,1)}, u32[]{:S(2)}) copy-start(bf16[512,512]{1,0:T(8,128)(2,1)} %metric_ref.7) | copy-start | bytes 1572868
  158.3 56.9 %all-to-all-start.1 = ((bf16[64,8,8,256]{3,2,1,0:T(8,128)(2,1)}), bf16[64,8,8,256]{3,2,1,0:T(8,128)(2,1)S(1)}, u32[]{:S(2)}, u32[]{:S(2)}) async-start(bf16[64,8,8,256]{3,2,1,0:T(8,128)(2,1)} %cut_chunk.3), calls=%async_computation.1 | async-start | bytes 4194304 | tf_op jit(solution)/shard_map/all_to_all | solution.py:417
  164.6 16.9 %copy-start.1 = (bf16[256,256]{1,0:T(8,128)(2,1)}, bf16[256,256]{1,0:T(8,128)(2,1)S(1)}, u32[]{:S(2)}) copy-start(bf16[256,256]{1,0:T(8,128)(2,1)S(1)} %fusion.1.perm_ref) | copy-start | bytes 393220
  170.6 27.7 %collective-permute-start.3 = (bf16[4096,128]{1,0:T(8,128)(2,1)}, bf16[4096,128]{1,0:T(8,128)(2,1)}, u32[]{:S(2)}, u32[]{:S(2)}) collective-permute-start(bf16[4096,128]{1,0:T(8,128)(2,1)} %get-tuple-element.37.refs_5_.f7), channel_id=1, source_target_pairs={{0,1},{1,2},{2,3},{3,4},{4,5},{5,6},{6,7},{8,9},{9,10},{10,11},{11... | collective-permute-start | bytes 3145736 | tf_op jit(solution)/shard_map/ppermute | solution.py:424
  172.7 25.6 %collective-permute-start.4 = (bf16[4096,128]{1,0:T(8,128)(2,1)}, bf16[4096,128]{1,0:T(8,128)(2,1)}, u32[]{:S(2)}, u32[]{:S(2)}) collective-permute-start(bf16[4096,128]{1,0:T(8,128)(2,1)} %get-tuple-element.32.refs_0_.f0), channel_id=1, source_target_pairs={{1,0},{2,1},{3,2},{4,3},{5,4},{6,5},{7,6},{9,8},{10,9},{11,10},{12... | collective-permute-start | bytes 3145736 | tf_op jit(solution)/shard_map/ppermute | solution.py:423
  181.5 16.8 %copy-start.2 = (bf16[4096,128]{1,0:T(8,128)(2,1)}, bf16[4096,128]{1,0:T(8,128)(2,1)S(1)}, u32[]{:S(2)}) copy-start(bf16[4096,128]{1,0:T(8,128)(2,1)S(1)} %get-tuple-element.33.refs_1_.f1.f1_hbm) | copy-start | bytes 3145732
  187.0 14.6 %copy-start.3 = (bf16[4096,128]{1,0:T(8,128)(2,1)}, bf16[4096,128]{1,0:T(8,128)(2,1)S(1)}, u32[]{:S(2)}) copy-start(bf16[4096,128]{1,0:T(8,128)(2,1)S(1)} %get-tuple-element.36.refs_4_.f6.f6_hbm) | copy-start | bytes 3145732
  187.0 14.6 %copy-start.6 = (bf16[4096,128]{1,0:T(8,128)(2,1)}, bf16[4096,128]{1,0:T(8,128)(2,1)S(1)}, u32[]{:S(2)}) copy-start(bf16[4096,128]{1,0:T(8,128)(2,1)S(1)} %get-tuple-element.35.refs_3_.f5_hbm) | copy-start | bytes 3145732
  192.4 15.2 %collective-permute-start = (bf16[24,32,128]{2,1,0:T(8,128)(2,1)S(1)}, bf16[24,32,128]{2,1,0:T(8,128)(2,1)S(1)}, u32[]{:S(2)}, u32[]{:S(2)}) collective-permute-start(bf16[24,32,128]{2,1,0:T(8,128)(2,1)S(1)} %get-tuple-element.39), channel_id=1, source_target_pairs={{0,64},{64,128},{128,192},{192,0},{1,65},{65,129},{129,193},{193,1... | collective-permute-start | bytes 589832 | tf_op jit(solution)/shard_map/ppermute | solution.py:317
  194.0 13.6 %collective-permute-start.1 = (bf16[24,32,128]{2,1,0:T(8,128)(2,1)S(1)}, bf16[24,32,128]{2,1,0:T(8,128)(2,1)S(1)}, u32[]{:S(2)}, u32[]{:S(2)}) collective-permute-start(bf16[24,32,128]{2,1,0:T(8,128)(2,1)S(1)} %get-tuple-element.40), channel_id=1, source_target_pairs={{0,128},{64,192},{128,0},{192,64},{1,129},{65,193},{129,1},{193,65... | collective-permute-start | bytes 589832 | tf_op jit(solution)/shard_map/ppermute | solution.py:317
  197.0 10.7 %collective-permute-start.2 = (bf16[24,32,128]{2,1,0:T(8,128)(2,1)S(1)}, bf16[24,32,128]{2,1,0:T(8,128)(2,1)S(1)}, u32[]{:S(2)}, u32[]{:S(2)}) collective-permute-start(bf16[24,32,128]{2,1,0:T(8,128)(2,1)S(1)} %get-tuple-element.41), channel_id=1, source_target_pairs={{0,192},{64,0},{128,64},{192,128},{1,193},{65,1},{129,65},{193,129... | collective-permute-start | bytes 589832 | tf_op jit(solution)/shard_map/ppermute | solution.py:317
  202.3 13.0 %collective-permute-start.5 = (f32[128,128]{1,0:T(8,128)S(1)}, f32[128,128]{1,0:T(8,128)S(1)}, u32[]{:S(2)}, u32[]{:S(2)}) collective-permute-start(f32[128,128]{1,0:T(8,128)S(1)} %get-tuple-element.42), channel_id=1, source_target_pairs={{1,0},{2,1},{3,2},{4,3},{5,4},{6,5},{7,6},{9,8},{10,9},{11,10},{12... | collective-permute-start | bytes 196616 | tf_op jit(solution)/shard_map/ppermute | solution.py:431
  205.5 9.8 %collective-permute-start.6 = (f32[128,128]{1,0:T(8,128)S(1)}, f32[128,128]{1,0:T(8,128)S(1)}, u32[]{:S(2)}, u32[]{:S(2)}) collective-permute-start(f32[128,128]{1,0:T(8,128)S(1)} %get-tuple-element.43), channel_id=1, source_target_pairs={{0,1},{1,2},{2,3},{3,4},{4,5},{5,6},{6,7},{8,9},{9,10},{10,11},{11... | collective-permute-start | bytes 196616 | tf_op jit(solution)/shard_map/ppermute | solution.py:432
  216.6 24.3 %copy-start.10 = (s32[127,2]{0,1:T(2,128)S(1)}, s32[127,2]{0,1:T(2,128)}, u32[]{:S(2)}) copy-start(s32[127,2]{0,1:T(2,128)} %param.6) | copy-start | bytes 3052
  225.5 8.2 %collective-permute-start.7 = (bf16[24,32,128]{2,1,0:T(8,128)(2,1)}, bf16[24,32,128]{2,1,0:T(8,128)(2,1)S(1)}, u32[]{:S(2)}, u32[]{:S(2)}) collective-permute-start(bf16[24,32,128]{2,1,0:T(8,128)(2,1)} %get-tuple-element.50), channel_id=1, source_target_pairs={{0,64},{64,128},{128,192},{192,0},{1,65},{65,129},{129,193},{193,1... | collective-permute-start | bytes 589832 | tf_op jit(solution)/shard_map/ppermute | solution.py:317
  227.1 10.9 %collective-permute-start.8 = (bf16[24,32,128]{2,1,0:T(8,128)(2,1)}, bf16[24,32,128]{2,1,0:T(8,128)(2,1)S(1)}, u32[]{:S(2)}, u32[]{:S(2)}) collective-permute-start(bf16[24,32,128]{2,1,0:T(8,128)(2,1)} %get-tuple-element.51), channel_id=1, source_target_pairs={{0,128},{64,192},{128,0},{192,64},{1,129},{65,193},{129,1},{193,65... | collective-permute-start | bytes 589832 | tf_op jit(solution)/shard_map/ppermute | solution.py:317
  230.0 8.0 %collective-permute-start.9 = (bf16[24,32,128]{2,1,0:T(8,128)(2,1)}, bf16[24,32,128]{2,1,0:T(8,128)(2,1)S(1)}, u32[]{:S(2)}, u32[]{:S(2)}) collective-permute-start(bf16[24,32,128]{2,1,0:T(8,128)(2,1)} %get-tuple-element.52), channel_id=1, source_target_pairs={{0,192},{64,0},{128,64},{192,128},{1,193},{65,1},{129,65},{193,129... | collective-permute-start | bytes 589832 | tf_op jit(solution)/shard_map/ppermute | solution.py:317
  239.2 5.8 %collective-permute-start.10 = (bf16[24,32,128]{2,1,0:T(8,128)(2,1)S(1)}, bf16[24,32,128]{2,1,0:T(8,128)(2,1)S(1)}, u32[]{:S(2)}, u32[]{:S(2)}) collective-permute-start(bf16[24,32,128]{2,1,0:T(8,128)(2,1)S(1)} %get-tuple-element.54), channel_id=1, source_target_pairs={{0,8},{1,9},{2,10},{3,11},{4,12},{5,13},{6,14},{7,15},{8,0},{9,1},... | collective-permute-start | bytes 589832 | tf_op jit(solution)/shard_map/ppermute | solution.py:437
  245.0 9.1 %collective-permute-start.13 = (f32[32,640]{1,0:T(8,128)S(1)}, f32[32,640]{1,0:T(8,128)S(1)}, u32[]{:S(2)}, u32[]{:S(2)}) collective-permute-start(f32[32,640]{1,0:T(8,128)S(1)} %get-tuple-element.58), channel_id=1, source_target_pairs={{0,48},{1,49},{2,50},{3,51},{4,52},{5,53},{6,54},{7,55},{8,56},{9,... | collective-permute-start | bytes 245768 | tf_op jit(solution)/shard_map/ppermute | solution.py:440
  246.2 9.3 %collective-permute-start.12 = (f32[32,640]{1,0:T(8,128)S(1)}, f32[32,640]{1,0:T(8,128)S(1)}, u32[]{:S(2)}, u32[]{:S(2)}) collective-permute-start(f32[32,640]{1,0:T(8,128)S(1)} %get-tuple-element.57), channel_id=1, source_target_pairs={{0,32},{1,33},{2,34},{3,35},{4,36},{5,37},{6,38},{7,39},{8,40},{9,... | collective-permute-start | bytes 245768 | tf_op jit(solution)/shard_map/ppermute | solution.py:440
  249.1 7.5 %collective-permute-start.11 = (f32[32,640]{1,0:T(8,128)S(1)}, f32[32,640]{1,0:T(8,128)S(1)}, u32[]{:S(2)}, u32[]{:S(2)}) collective-permute-start(f32[32,640]{1,0:T(8,128)S(1)} %get-tuple-element.56), channel_id=1, source_target_pairs={{0,16},{1,17},{2,18},{3,19},{4,20},{5,21},{6,22},{7,23},{8,24},{9,... | collective-permute-start | bytes 245768 | tf_op jit(solution)/shard_map/ppermute | solution.py:440
  256.6 12.6 %collective-permute-start.14 = (f32[32,640]{1,0:T(8,128)S(1)}, f32[32,640]{1,0:T(8,128)S(1)}, u32[]{:S(2)}, u32[]{:S(2)}) collective-permute-start(f32[32,640]{1,0:T(8,128)S(1)} %add_add_fusion), channel_id=1, source_target_pairs={{0,0},{1,8},{2,16},{3,24},{4,32},{5,40},{6,48},{7,56},{8,1},{9,9},... | collective-permute-start | bytes 245768 | tf_op jit(solution)/shard_map/ppermute | solution.py:441
  (6 other events, 16.6 us)

commit v4 on v3

--- a/solution.py
+++ b/solution.py
@@ -47,8 +47,19 @@
     return off + [k for k in slots if k[1] == 0], len(off)
 
 
+def of_parity(slots, odd):
+    return ordered([k for k in slots if k[0] % 2 == odd])[0]
+
+
 EARLY, EARLY_OFF = ordered(EARLY_TILES)
-LATE, LATE_OFF = ordered(STRANGE + tuple(LATE_TILES))
+EARLY_BY = [of_parity(EARLY, odd) for odd in range(2)]
+LATE_ALL = STRANGE + tuple(LATE_TILES)
+LATE_BY = [of_parity(LATE_ALL, odd) for odd in range(2)]
+EARLY_HALF = len(EARLY_BY[0])
+LATE_HALF = len(LATE_BY[0])
+LATE_DIAGONALS = 1
+EARLY_DIAGONALS = 3
+AXES = ("aux", "blk")
 
 
 def sent_slots(slots, off):
@@ -165,6 +176,18 @@
     )(rows, perm, metric, mask)
 
 
+def quarter(tile_ref, row, col, which):
+    at = pl.multiple_of(row * BS + lax.rem(which, NY) * PART, PART)
+    return tile_ref[pl.ds(at, PART), col * BS : (col + 1) * BS]
+
+
+def put_sent(out_ref, n, low_at, value):
+    high = value.astype(jnp.bfloat16)
+    out_ref[n] = high
+    if low_at is not None:
+        out_ref[low_at] = (value - high.astype(jnp.float32)).astype(jnp.bfloat16)
+
+
 def put_slot(tile_ref, row, col, n, diagonal, slots, off, y, own_ref, out_refs):
     for d in range(NY):
         at = pl.multiple_of(row * BS + lax.rem(y + d, NY) * PART, PART)
@@ -235,7 +258,8 @@
     )(below, f0, f1, f6, f7, above)
 
 
-def late_kernel(y_ref, mask_ref, rows_hbm, f1_hbm, f2_hbm, f5_hbm, f6_hbm, perm_ref, metric_ref, from_below, from_above, edges, own_ref, o1, o2, o3, rows_ref, turned_ref, left_ref, right_ref, tiles_ref, flip_ref, row_sems, sems):
+def late_kernel(y_ref, mask_ref, rows_hbm, f1_hbm, f2_hbm, f5_hbm, f6_hbm, perm_ref, metric_ref, from_below, from_above, edges, own_ref, *rest):
+    outs, (rows_ref, turned_ref, left_ref, right_ref, tiles_ref, flip_ref, row_sems, sems) = rest[:7], rest[7:]
     feeds = []
     for n in range(4):
         piece = pl.ds(n * 1024, 1024)
@@ -260,10 +284,29 @@
     f1, f2, f5, f6 = [right_ref[n] for n in range(4)]
     right = jnp.concatenate([f1, f2, left_ref[...], f5, f6], axis=1)
     tiles_ref[...] = jnp.dot(left_ref[...].T, right, preferred_element_type=jnp.float32)
-    y = y_ref[0]
-    for tile_ref, (r, e) in zip((from_below, from_above, *(edges.at[k] for k in range(4))), STRANGE):
-        put_slot(tile_ref, 0, 0, LATE.index((r, e)), False, LATE, LATE_OFF, y, own_ref, (o1, o2, o3))
-    put_tiles(LATE_TILES, (tiles_ref,), flip_ref, LATE, LATE_OFF, y, own_ref, (o1, o2, o3))
+    at = {(0, -2): (from_below, 0, 0), (7, 2): (from_above, 0, 0)}
+    for n, slot in enumerate(STRANGE[2:]):
+        at[slot] = (edges.at[n], 0, 0)
+    flips = 0
+    for slot, (_, s, t, turned) in LATE_TILES.items():
+        if turned:
+            flip_ref[flips] = tiles_ref[s * BS : (s + 1) * BS, t * BS : (t + 1) * BS].T
+            at[slot] = (flip_ref.at[flips], 0, 0)
+            flips += 1
+        else:
+            at[slot] = (tiles_ref, s, t)
+    y, odd = y_ref[0], y_ref[1]
+    for n in range(LATE_HALF):
+        for d in range(NY):
+            even_piece, odd_piece = [quarter(*at[LATE_BY[k][n]], y + d) for k in range(2)]
+            mine = jnp.where(odd == 0, even_piece, odd_piece)
+            theirs = jnp.where(odd == 0, odd_piece, even_piece)
+            low_at = n + LATE_DIAGONALS if n >= LATE_HALF - LATE_DIAGONALS else None
+            if d == 0:
+                own_ref[n] = mine
+            else:
+                put_sent(outs[d - 1], n, low_at, mine)
+            put_sent(outs[3 + d], n, low_at, theirs)
 
 
 def exchange_shapes(slots, off):
@@ -292,11 +335,12 @@
 def late_tiles(y, mask, rows, f1, f2, f5, f6, perm, metric, from_below, from_above, edges):
     return pl.pallas_call(
         late_kernel,
-        out_shape=exchange_shapes(LATE, LATE_OFF),
+        out_shape=[jax.ShapeDtypeStruct((LATE_HALF, PART, BS), jnp.float32)]
+        + [jax.ShapeDtypeStruct((LATE_HALF + LATE_DIAGONALS, PART, BS), jnp.bfloat16)] * 7,
         in_specs=[pl.BlockSpec(memory_space=SMEM)] * 2
         + [pl.BlockSpec(memory_space=pl.ANY)] * 5
         + [pl.BlockSpec(memory_space=VMEM)] * 5,
-        out_specs=[pl.BlockSpec(memory_space=VMEM)] * 4,
+        out_specs=[pl.BlockSpec(memory_space=VMEM)] * 8,
         scratch_shapes=[
             pltpu.VMEM((4096, PAIR), jnp.bfloat16),
             pltpu.VMEM((8, 512, PAIR), jnp.bfloat16),
@@ -307,7 +351,7 @@
             pltpu.SemaphoreType.DMA((4,)),
             pltpu.SemaphoreType.DMA((4,)),
         ],
-        compiler_params=pltpu.CompilerParams(vmem_limit_bytes=60 << 20),
+        compiler_params=pltpu.CompilerParams(vmem_limit_bytes=52 << 20),
         cost_estimate=pl.CostEstimate(flops=2 * 4096 * 256 * 1536, bytes_accessed=8 << 20, transcendentals=0),
         name="late_tiles",
     )(y, mask, rows, f1, f2, f5, f6, perm, metric, from_below, from_above, edges)
@@ -317,87 +361,104 @@
     return [lax.ppermute(s, "aux", [(a, (a + d) % NY) for a in range(NY)]) for d, s in enumerate(sent, 1)]
 
 
-def gathered(own_ref, got_refs, n, e, slots, off):
+def gathered(own_ref, got_refs, n, low_at):
     value = own_ref[n]
     for got in got_refs:
         value = value + got[n].astype(jnp.float32)
-        if e == 0:
-            value = value + got[n + len(slots) - off].astype(jnp.float32)
+        if low_at is not None:
+            value = value + got[low_at].astype(jnp.float32)
     return value
 
 
-def early_sum_kernel(own_ref, g1, g2, g3, out_ref):
-    for n, (r, e) in enumerate(EARLY):
-        out_ref[n] = gathered(own_ref, (g1, g2, g3), n, e, EARLY, EARLY_OFF)
-
-
-def early_sum(own, got):
+def early_sum_kernel(odd_ref, own_ref, g1, g2, g3, mine_ref, theirs_ref):
+    odd = odd_ref[0]
+    for n in range(EARLY_HALF):
+        pair = []
+        for k in range(2):
+            r, e = EARLY_BY[k][n]
+            m = EARLY.index((r, e))
+            pair.append(gathered(own_ref, (g1, g2, g3), m, m + len(EARLY) - EARLY_OFF if e == 0 else None))
+        low_at = n + EARLY_DIAGONALS if n >= EARLY_HALF - EARLY_DIAGONALS else None
+        mine_ref[n] = jnp.where(odd == 0, pair[0], pair[1])
+        put_sent(theirs_ref, n, low_at, jnp.where(odd == 0, pair[1], pair[0]))
+
+
+def early_sum(odd, own, got):
     return pl.pallas_call(
         early_sum_kernel,
-        out_shape=jax.ShapeDtypeStruct(own.shape, jnp.float32),
+        out_shape=[
+            jax.ShapeDtypeStruct((EARLY_HALF, PART, BS), jnp.float32),
+            jax.ShapeDtypeStruct((EARLY_HALF + EARLY_DIAGONALS, PART, BS), jnp.bfloat16),
+        ],
+        in_specs=[pl.BlockSpec(memory_space=SMEM)] + [pl.BlockSpec(memory_space=VMEM)] * 4,
+        out_specs=[pl.BlockSpec(memory_space=VMEM)] * 2,
+        compiler_params=pltpu.CompilerParams(vmem_limit_bytes=16 << 20),
+        name="early_sum",
+    )(odd, own, *got)
+
+
+def settle_kernel(z_ref, early_ref, early_got, late_ref, *rest):
+    late_got, (own_ref, o1, o2, o3, band_ref) = rest[:7], rest[7:]
+    odd, half = lax.rem(z_ref[0], 2), lax.div(z_ref[0], 2)
+
+    def place(by, n, value):
+        (r0, e0), (r1, e1) = by[0][n], by[1][n]
+        band_ref[jnp.where(odd == 0, r0 // 2, r1 // 2), jnp.where(odd == 0, e0 + 2, e1 + 2)] = value
+
+    for n in range(EARLY_HALF):
+        low_at = n + EARLY_DIAGONALS if n >= EARLY_HALF - EARLY_DIAGONALS else None
+        place(EARLY_BY, n, gathered(early_ref, (early_got,), n, low_at))
+    for n in range(LATE_HALF):
+        low_at = n + LATE_DIAGONALS if n >= LATE_HALF - LATE_DIAGONALS else None
+        place(LATE_BY, n, gathered(late_ref, late_got, n, low_at))
+    for j, out in enumerate((own_ref, o1, o2, o3)):
+        k = lax.rem(half + j, 4)
+        for slot in range(BAND):
+            if j == 0:
+                out[:, slot * BS : (slot + 1) * BS] = band_ref[k, slot]
+            else:
+                put_sent(out, slot, BAND if slot == 2 else None, band_ref[k, slot])
+
+
+def settle(z, early, early_got, late, late_got):
+    return pl.pallas_call(
+        settle_kernel,
+        out_shape=[jax.ShapeDtypeStruct((PART, BAND * BS), jnp.float32)]
+        + [jax.ShapeDtypeStruct((BAND + 1, PART, BS), jnp.bfloat16)] * 3,
+        in_specs=[pl.BlockSpec(memory_space=SMEM)] + [pl.BlockSpec(memory_space=VMEM)] * 10,
+        out_specs=[pl.BlockSpec(memory_space=VMEM)] * 4,
+        scratch_shapes=[pltpu.VMEM((4, BAND, PART, BS), jnp.float32)],
+        compiler_params=pltpu.CompilerParams(vmem_limit_bytes=16 << 20),
+        name="settle",
+    )(z, early, early_got, late, *late_got)
+
+
+def finish_kernel(own_ref, g1, g2, g3, out_ref):
+    for slot in range(BAND):
+        value = own_ref[:, slot * BS : (slot + 1) * BS]
+        for got in (g1, g2, g3):
+            value = value + got[slot].astype(jnp.float32)
+            if slot == 2:
+                value = value + got[BAND].astype(jnp.float32)
+        out_ref[:, slot * BS : (slot + 1) * BS] = value
+
+
+def finish(own, got):
+    return pl.pallas_call(
+        finish_kernel,
+        out_shape=jax.ShapeDtypeStruct((PART, BAND * BS), jnp.float32),
         in_specs=[pl.BlockSpec(memory_space=VMEM)] * 4,
         out_specs=pl.BlockSpec(memory_space=VMEM),
         compiler_params=pltpu.CompilerParams(vmem_limit_bytes=16 << 20),
-        name="early_sum",
+        name="finish",
     )(own, *got)
-
-
-def merge_kernel(odd_ref, early_ref, late_ref, g1, g2, g3, own_ref, out_ref, band_ref):
-    for n, (r, e) in enumerate(EARLY):
-        band_ref[r, e + 2] = early_ref[n]
-    for n, (r, e) in enumerate(LATE):
-        band_ref[r, e + 2] = gathered(late_ref, (g1, g2, g3), n, e, LATE, LATE_OFF)
-    odd = odd_ref[0]
-    for k in range(4):
-        for slot in range(BAND):
-            own_ref[k, slot] = band_ref[2 * k + odd, slot]
-            value = band_ref[2 * k + 1 - odd, slot]
-            high = value.astype(jnp.bfloat16)
-            out_ref[k * 6 + slot] = high
-            if slot == 2:
-                out_ref[k * 6 + 5] = (value - high.astype(jnp.float32)).astype(jnp.bfloat16)
-
-
-def merge(odd, early, late, got):
-    return pl.pallas_call(
-        merge_kernel,
-        out_shape=[
-            jax.ShapeDtypeStruct((4, BAND, PART, BS), jnp.float32),
-            jax.ShapeDtypeStruct((24, PART, BS), jnp.bfloat16),
-        ],
-        in_specs=[pl.BlockSpec(memory_space=SMEM)] + [pl.BlockSpec(memory_space=VMEM)] * 5,
-        out_specs=[pl.BlockSpec(memory_space=VMEM)] * 2,
-        scratch_shapes=[pltpu.VMEM((NC, BAND, PART, BS), jnp.float32)],
-        compiler_params=pltpu.CompilerParams(vmem_limit_bytes=16 << 20),
-        name="merge",
-    )(odd, early, late, *got)
-
-
-def settle_kernel(half_ref, own_ref, got_ref, o0, o1, o2, o3):
-    for j, out in enumerate((o0, o1, o2, o3)):
-        k = lax.rem(half_ref[0] + j, 4)
-        for slot in range(BAND):
-            value = own_ref[k, slot] + got_ref[k * 6 + slot].astype(jnp.float32)
-            if slot == 2:
-                value = value + got_ref[k * 6 + 5].astype(jnp.float32)
-            out[:, slot * BS : (slot + 1) * BS] = value
-
-
-def settle(half, own, got):
-    return pl.pallas_call(
-        settle_kernel,
-        out_shape=[jax.ShapeDtypeStruct((PART, BAND * BS), jnp.float32)] * 4,
-        in_specs=[pl.BlockSpec(memory_space=SMEM)] + [pl.BlockSpec(memory_space=VMEM)] * 2,
-        out_specs=[pl.BlockSpec(memory_space=VMEM)] * 4,
-        compiler_params=pltpu.CompilerParams(vmem_limit_bytes=16 << 20),
-        name="settle",
-    )(half, own, got)
 
 
 def local(integrals, metric, pair_list, aux_mask):
     blk = lax.axis_index("blk")
-    y = jnp.full((1,), lax.axis_index("aux"), jnp.int32)
     z, c = blk // NC, blk % NC
+    y = jnp.stack([lax.axis_index("aux"), z % 2]).astype(jnp.int32)
+    at_z = jnp.full((1,), z, jnp.int32)
     grid = [(k // NC, k % NC) for k in range(NZ * NC)]
     up = [(zz * NC + cc, zz * NC + cc + 1) for zz, cc in grid if cc < NC - 1]
     down = [(b, a) for a, b in up]
@@ -426,19 +487,29 @@
     f5, f6 = fit_chunk(rows, 2, perm, metric, mask_of(5, 6))
 
     early, *sent = early_tiles(y, (f0, f1, f2, f5, f6, f7))
-    early = early_sum(early, over_domains(sent))
+    early, early_sent = early_sum(jnp.full((1,), z % 2, jnp.int32), early, over_domains(sent))
     to_below, to_above, edges = edge_tiles(below, f0, f1, f6, f7, above)
     from_above = lax.ppermute(to_below, "blk", down)
     from_below = lax.ppermute(to_above, "blk", up)
-    early, from_above, from_below, last = lax.optimization_barrier((early, from_above, from_below, last))
+    early_sent, from_above, from_below, last = lax.optimization_barrier((early_sent, from_above, from_below, last))
 
     late, *sent = late_tiles(y, mask_of(3, 4), last, f1, f2, f5, f6, perm, metric, from_below, from_above, edges)
-    own, sent = merge(jnp.full((1,), z % 2, jnp.int32), early, late, over_domains(sent))
-    got = lax.ppermute(sent, "blk", [(zz * NC + cc, (zz ^ 1) * NC + cc) for zz, cc in grid])
-    total, *sent = settle(jnp.full((1,), z // 2, jnp.int32), own, got)
-    for j, s in enumerate(sent, 1):
-        total = total + lax.ppermute(s, "blk", [(zz * NC + cc, (zz + 2 * j) % NZ * NC + cc) for zz, cc in grid])
-    total = lax.ppermute(total, "blk", [(zz * NC + cc, cc * NC + zz) for zz, cc in grid])
+    whole_grid = [(a, zz, cc) for a in range(NY) for zz, cc in grid]
+
+    def move(array, d, flip):
+        pairs = [
+            (a * NZ * NC + zz * NC + cc, (a + d) % NY * NZ * NC + (zz ^ flip) * NC + cc) for a, zz, cc in whole_grid
+        ]
+        return lax.ppermute(array, AXES, pairs)
+
+    early_got = move(early_sent, 0, 1)
+    late_got = [move(s, d, 0) for d, s in enumerate(sent[:3], 1)] + [move(s, d, 1) for d, s in enumerate(sent[3:])]
+    own, *sent = settle(at_z, early, early_got, late, late_got)
+    got = [
+        lax.ppermute(s, "blk", [(zz * NC + cc, (zz + 2 * j) % NZ * NC + cc) for zz, cc in grid])
+        for j, s in enumerate(sent, 1)
+    ]
+    total = lax.ppermute(finish(own, got), "blk", [(zz * NC + cc, cc * NC + zz) for zz, cc in grid])
     return (total * scale[None, :])[None]
 
 

time: 271 us -> 264 us (0.974)
  Pallas kernels: 41.6 us -> 36.3 us
  local copies, waits for them, and re-layouts: 3.79 us -> 0.26 us
    ppermute x2 -> x9, starting transfers between devices: 10 us -> 18.2 us  [the longest x8 11.9 us: move(): return lax.ppermute(array, AXES, pairs)]
    ppermute x6 -> x3, waiting for transfers between devices: 6.68 us -> 0.01 us  [over_domains(): lax.ppermute(s, 'aux', [(a, (a + d) % NY) for a in range(NY)])]
    ppermute x6 -> x3, starting transfers between devices: 11.8 us -> 5.92 us  [over_domains(): lax.ppermute(s, 'aux', [(a, (a + d) % NY) for a in range(NY)])]
    all_to_all x2, waiting for transfers between devices: 146 us -> 150 us  [spread(): lax.all_to_all(cut_chunk(source, blocks), 'blk', split_axis=0, concat_axi...]
    unnamed x26 -> x14, local copies, waits for them, and re-layouts: 3.04 us -> 0.04 us
    ppermute x2 -> x9, waiting for transfers between devices: 8.31 us -> 11 us  [the longest x1 6.25 us: local(): lax.ppermute(finish(own, got), 'blk', [(zz * NC + cc, cc * NC + zz) for z...]
  transfers between devices with their start and end apart: 17 -> 21, of which waited for: 9 -> 10; matrix products, arithmetic and copies ran while one was open for 1% -> 0% of each run, Pallas kernels for 10% -> 12%
where the time goes in v4:
time: 264 us; the launch traced here: 261 us
  waiting for transfers between devices  165 us (62%)
  starting transfers between devices  58.7 us (22%)
  Pallas kernels  36.3 us (14%)
    all_to_all x2, waiting for transfers between devices, spread(): lax.all_to_all(cut_chunk(source, blocks), 'blk', split_axis=0, concat_axi...  150 us
    all_to_all x2, starting transfers between devices, spread(): lax.all_to_all(cut_chunk(source, blocks), 'blk', split_axis=0, concat_axi...  18 us
    pallas_call x3, Pallas kernels, fit_chunk(): pl.pallas_call(fit_kernel, grid=(1,), out_shape=[jax.ShapeDtypeStruct((40...  14.8 us
    ppermute x8, starting transfers between devices, move(): return lax.ppermute(array, AXES, pairs)  11.9 us
    pallas_call x2, Pallas kernels, cut_chunk(): pl.pallas_call(lambda *refs: cut_kernel(*refs, blocks=blocks), out_shape=...  7.74 us
    pallas_call x1, Pallas kernels, late_tiles(): pl.pallas_call(late_kernel, out_shape=[jax.ShapeDtypeStruct((LATE_HALF, P...  7.29 us
    ppermute x1, starting transfers between devices, local(): lax.ppermute(finish(own, got), 'blk', [(zz * NC + cc, cc * NC + zz) for z...  6.32 us
    ppermute x1, waiting for transfers between devices, local(): lax.ppermute(finish(own, got), 'blk', [(zz * NC + cc, cc * NC + zz) for z...  6.25 us
  transfers between devices with their start and end apart: 21, of which 10 were waited for; matrix products, arithmetic and copies ran while one was open for 0% of the time, Pallas kernels for 12%

profile of v4, /device:TPU:4, one launch (start us, length us, event | category | flops | bytes accessed | tf_op | source)
XLA Modules:
  0.0 261.5 jit_solution(3378839587739979659)
XLA Ops:
  0.0 4.9 %cut_chunk.2 = bf16[64,8,8,768]{3,2,1,0:T(8,128)(2,1)} custom-call(bf16[8,8,8,8192]{3,2,1,0:T(8,128)(2,1)} %bitcast.14), custom_call_target="tpu_custom_call" | custom-call | bytes 12582912 | tf_op jit(solution)/shard_map/cut_chunk/pallas_call | solution.py:110
  4.9 12.2 %all-to-all-start = ((bf16[64,8,8,768]{3,2,1,0:T(8,128)(2,1)}), bf16[64,8,8,768]{3,2,1,0:T(8,128)(2,1)}, u32[]{:S(2)}, u32[]{:S(2)}) async-start(bf16[64,8,8,768]{3,2,1,0:T(8,128)(2,1)} %cut_chunk.2), calls=%async_computation | async-start | bytes 12582912 | tf_op jit(solution)/shard_map/all_to_all | solution.py:478
  17.1 2.8 %cut_chunk.3 = bf16[64,8,8,256]{3,2,1,0:T(8,128)(2,1)} custom-call(bf16[8,8,8,8192]{3,2,1,0:T(8,128)(2,1)} %bitcast.15), custom_call_target="tpu_custom_call" | custom-call | bytes 4194304 | tf_op jit(solution)/shard_map/cut_chunk/pallas_call | solution.py:110
  20.0 138.4 %all-to-all-done = bf16[64,8,8,768]{3,2,1,0:T(8,128)(2,1)} async-done(((bf16[64,8,8,768]{3,2,1,0:T(8,128)(2,1)}), bf16[64,8,8,768]{3,2,1,0:T(8,128)(2,1)}, u32[]{:S(2)}, u32[]{:S(2)}) %all-to-all-start) | async-done | bytes 6291488 | tf_op jit(solution)/shard_map/all_to_all | solution.py:478
  158.3 5.8 %all-to-all-start.1 = ((bf16[64,8,8,256]{3,2,1,0:T(8,128)(2,1)}), bf16[64,8,8,256]{3,2,1,0:T(8,128)(2,1)}, u32[]{:S(2)}, u32[]{:S(2)}) async-start(bf16[64,8,8,256]{3,2,1,0:T(8,128)(2,1)} %cut_chunk.3), calls=%async_computation.1 | async-start | bytes 4194304 | tf_op jit(solution)/shard_map/all_to_all | solution.py:478
  164.8 4.7 %fit_chunk.3 = (bf16[4096,128]{1,0:T(8,128)(2,1)S(1)}, bf16[4096,128]{1,0:T(8,128)(2,1)S(1)}) custom-call(bf16[4096,768]{1,0:T(8,128)(2,1)} %bitcast.4.rows_ref, bf16[256,256]{1,0:T(8,128)(2,1)S(1)} %fusion.1.perm_ref, bf16[512,512]{1,0:T(8,128)(2,1)S(1)} %copy-done, f32[4,2]{1,0:T(4,128)S(1)} %pad_maximum_fusion.mask_ref), custom_call_target="tpu_custom_call" | custom-call | flops 1610612736 | bytes 4194304 | tf_op jit(solution)/shard_map/fit_chunk/pallas_call | solution.py:161
  169.5 2.1 collective-permute-start.3
  171.5 3.5 %collective-permute-start.4 = (bf16[4096,128]{1,0:T(8,128)(2,1)S(1)}, bf16[4096,128]{1,0:T(8,128)(2,1)}, u32[]{:S(2)}, u32[]{:S(2)}) collective-permute-start(bf16[4096,128]{1,0:T(8,128)(2,1)S(1)} %get-tuple-element.36.refs_0_.f0), channel_id=1, source_target_pairs={{1,0},{2,1},{3,2},{4,3},{5,4},{6,5},{7,6},{9,8},{10,9},{11,10},{12... | collective-permute-start | bytes 3145736 | tf_op jit(solution)/shard_map/ppermute | solution.py:484
  175.2 4.7 %fit_chunk.4 = (bf16[4096,128]{1,0:T(8,128)(2,1)S(1)}, bf16[4096,128]{1,0:T(8,128)(2,1)S(1)}) custom-call(bf16[4096,768]{1,0:T(8,128)(2,1)} %bitcast.4.rows_ref, bf16[256,256]{1,0:T(8,128)(2,1)S(1)} %fusion.1.perm_ref, bf16[512,512]{1,0:T(8,128)(2,1)S(1)} %copy-done, f32[4,2]{1,0:T(4,128)S(1)} %get-tuple-element.69.mask_ref), custom_call_target="tpu_custom_call" | custom-call | flops 1610612736 | bytes 4194304 | tf_op jit(solution)/shard_map/fit_chunk/pallas_call | solution.py:161
  179.9 5.4 %fit_chunk.5 = (bf16[4096,128]{1,0:T(8,128)(2,1)S(1)}, bf16[4096,128]{1,0:T(8,128)(2,1)S(1)}) custom-call(bf16[4096,768]{1,0:T(8,128)(2,1)} %bitcast.4.rows_ref, bf16[256,256]{1,0:T(8,128)(2,1)S(1)} %fusion.1.perm_ref, bf16[512,512]{1,0:T(8,128)(2,1)S(1)} %copy-done, f32[4,2]{1,0:T(4,128)S(1)} %get-tuple-element.68.mask_ref), custom_call_target="tpu_custom_call" | custom-call | flops 1610612736 | bytes 4194304 | tf_op jit(solution)/shard_map/fit_chunk/pallas_call | solution.py:161
  185.4 3.6 %early_tiles.1 = (f32[18,32,128]{2,1,0:T(8,128)S(1)}, bf16[24,32,128]{2,1,0:T(8,128)(2,1)S(1)}, bf16[24,32,128]{2,1,0:T(8,128)(2,1)S(1)}, bf16[24,32,128]{2,1,0:T(8,128)(2,1)S(1)}) custom-call(s32[2]{0:T(128)S(1)} %pad_add_fusion.y_ref, bf16[4096,128]{1,0:T(8,128)(2,1)S(1)} %get-tuple-element.36.refs_0_.f0, ...), custom_call_target="tpu_custom_call" | custom-call | flops 2147483648 | bytes 7340032 | tf_op jit(solution)/shard_map/early_tiles/pallas_call | solution.py:318
  190.7 2.9 %collective-permute-start.1 = (bf16[24,32,128]{2,1,0:T(8,128)(2,1)S(1)}, bf16[24,32,128]{2,1,0:T(8,128)(2,1)S(1)}, u32[]{:S(2)}, u32[]{:S(2)}) collective-permute-start(bf16[24,32,128]{2,1,0:T(8,128)(2,1)S(1)} %get-tuple-element.44), channel_id=1, source_target_pairs={{0,128},{64,192},{128,0},{192,64},{1,129},{65,193},{129,1},{193,65... | collective-permute-start | bytes 589832 | tf_op jit(solution)/shard_map/ppermute | solution.py:361
  195.5 2.6 %edge_tiles.1 = (f32[128,128]{1,0:T(8,128)S(1)}, f32[128,128]{1,0:T(8,128)S(1)}, f32[4,128,128]{2,1,0:T(8,128)S(1)}) custom-call(bf16[4096,128]{1,0:T(8,128)(2,1)} %collective-permute-done.3.below, bf16[4096,128]{1,0:T(8,128)(2,1)S(1)} %get-tuple-element.36.refs_0_.f0, bf16[4096,128]{1,0:T(8,128)(2,1)S(1)} %get-tuple-element.37.refs_1_.f1.f1_hbm, ...), custom_call_target="tpu_custom_call" | custom-call | flops 536870912 | bytes 6291456 | tf_op jit(solution)/shard_map/edge_tiles/pallas_call | solution.py:250
  198.2 3.8 %collective-permute-start.5 = (f32[128,128]{1,0:T(8,128)S(1)}, f32[128,128]{1,0:T(8,128)S(1)}, u32[]{:S(2)}, u32[]{:S(2)}) collective-permute-start(f32[128,128]{1,0:T(8,128)S(1)} %get-tuple-element.48), channel_id=1, source_target_pairs={{1,0},{2,1},{3,2},{4,3},{5,4},{6,5},{7,6},{9,8},{10,9},{11,10},{12... | collective-permute-start | bytes 196616 | tf_op jit(solution)/shard_map/ppermute | solution.py:492
  202.0 1.9 collective-permute-start.6
  204.1 11.3 %all-to-all-done.1 = bf16[64,8,8,256]{3,2,1,0:T(8,128)(2,1)} async-done(((bf16[64,8,8,256]{3,2,1,0:T(8,128)(2,1)}), bf16[64,8,8,256]{3,2,1,0:T(8,128)(2,1)}, u32[]{:S(2)}, u32[]{:S(2)}) %all-to-all-start.1) | async-done | bytes 2097184 | tf_op jit(solution)/shard_map/all_to_all | solution.py:478
  216.0 7.3 %late_tiles.1 = (f32[11,32,128]{2,1,0:T(8,128)S(1)}, bf16[12,32,128]{2,1,0:T(8,128)(2,1)S(1)}, bf16[12,32,128]{2,1,0:T(8,128)(2,1)S(1)}, bf16[12,32,128]{2,1,0:T...) custom-call(s32[2]{0:T(128)S(1)} %pad_add_fusion.y_ref, ...), custom_call_target="tpu_custom_call" | custom-call | flops 3221225472 | bytes 8388608 | tf_op jit(solution)/shard_map/late_tiles/pallas_call | solution.py:336
  224.9 2.9 %collective-permute-start.9 = (bf16[12,32,128]{2,1,0:T(8,128)(2,1)S(1)}, bf16[12,32,128]{2,1,0:T(8,128)(2,1)S(1)}, u32[]{:S(2)}, u32[]{:S(2)}) collective-permute-start(bf16[12,32,128]{2,1,0:T(8,128)(2,1)S(1)} %get-tuple-element.57), channel_id=1, source_target_pairs={{0,128},{1,129},{2,130},{3,131},{4,132},{5,133},{6,134},{7,135},{8... | collective-permute-start | bytes 294920 | tf_op jit(solution)/shard_map/ppermute | solution.py:503
  235.0 2.7 %collective-permute-done.12.rest_4_ = bf16[12,32,128]{2,1,0:T(8,128)(2,1)S(1)} collective-permute-done((bf16[12,32,128]{2,1,0:T(8,128)(2,1)S(1)}, bf16[12,32,128]{2,1,0:T(8,128)(2,1)S(1)}, u32[]{:S(2)}, u32[]{:S(2)}) %collective-permute-start.12) | collective-permute-done | bytes 98336 | tf_op jit(solution)/shard_map/ppermute | solution.py:503
  239.5 2.5 collective-permute-start.16
  242.0 2.7 %collective-permute-start.17 = (bf16[6,32,128]{2,1,0:T(8,128)(2,1)S(1)}, bf16[6,32,128]{2,1,0:T(8,128)(2,1)S(1)}, u32[]{:S(2)}, u32[]{:S(2)}) collective-permute-start(bf16[6,32,128]{2,1,0:T(8,128)(2,1)S(1)} %get-tuple-element.66), channel_id=1, source_target_pairs={{0,48},{1,49},{2,50},{3,51},{4,52},{5,53},{6,54},{7,55},{8,56},{9,... | collective-permute-start | bytes 147464 | tf_op jit(solution)/shard_map/ppermute | solution.py:509
  245.7 2.4 collective-permute-done.16.g2
  248.2 6.3 %collective-permute-start.18 = (f32[32,640]{1,0:T(8,128)S(1)}, f32[32,640]{1,0:T(8,128)S(1)}, u32[]{:S(2)}, u32[]{:S(2)}) collective-permute-start(f32[32,640]{1,0:T(8,128)S(1)} %finish.1), channel_id=1, source_target_pairs={{0,0},{1,8},{2,16},{3,24},{4,32},{5,40},{6,48},{7,56},{8,1},{9,9},... | collective-permute-start | bytes 245768 | tf_op jit(solution)/shard_map/ppermute | solution.py:512
  254.6 6.2 %collective-permute-done.18 = f32[32,640]{1,0:T(8,128)S(1)} collective-permute-done((f32[32,640]{1,0:T(8,128)S(1)}, f32[32,640]{1,0:T(8,128)S(1)}, u32[]{:S(2)}, u32[]{:S(2)}) %collective-permute-start.18) | collective-permute-done | bytes 81952 | tf_op jit(solution)/shard_map/ppermute | solution.py:512
  (60 shorter events, 17.4 us)
Async XLA Ops:
  4.9 153.4 %all-to-all-start = ((bf16[64,8,8,768]{3,2,1,0:T(8,128)(2,1)}), bf16[64,8,8,768]{3,2,1,0:T(8,128)(2,1)}, u32[]{:S(2)}, u32[]{:S(2)}) async-start(bf16[64,8,8,768]{3,2,1,0:T(8,128)(2,1)} %cut_chunk.2), calls=%async_computation | async-start | bytes 12582912 | tf_op jit(solution)/shard_map/all_to_all | solution.py:478
  17.1 147.1 %copy-start.5 = (s32[4,64]{1,0:T(4,128)S(1)}, s32[4,64]{1,0:T(4,128)}, u32[]{:S(2)}) copy-start(s32[4,64]{1,0:T(4,128)} %param.7) | copy-start | bytes 3076
  17.1 147.6 %copy-start = (bf16[512,512]{1,0:T(8,128)(2,1)S(1)}, bf16[512,512]{1,0:T(8,128)(2,1)}, u32[]{:S(2)}) copy-start(bf16[512,512]{1,0:T(8,128)(2,1)} %metric_ref.7) | copy-start | bytes 1572868
  158.3 57.0 %all-to-all-start.1 = ((bf16[64,8,8,256]{3,2,1,0:T(8,128)(2,1)}), bf16[64,8,8,256]{3,2,1,0:T(8,128)(2,1)}, u32[]{:S(2)}, u32[]{:S(2)}) async-start(bf16[64,8,8,256]{3,2,1,0:T(8,128)(2,1)} %cut_chunk.3), calls=%async_computation.1 | async-start | bytes 4194304 | tf_op jit(solution)/shard_map/all_to_all | solution.py:478
  169.5 26.1 %collective-permute-start.3 = (bf16[4096,128]{1,0:T(8,128)(2,1)S(1)}, bf16[4096,128]{1,0:T(8,128)(2,1)}, u32[]{:S(2)}, u32[]{:S(2)}) collective-permute-start(bf16[4096,128]{1,0:T(8,128)(2,1)S(1)} %get-tuple-element.41.refs_5_.f7), channel_id=1, source_target_pairs={{0,1},{1,2},{2,3},{3,4},{4,5},{5,6},{6,7},{8,9},{9,10},{10,11},{11... | collective-permute-start | bytes 3145736 | tf_op jit(solution)/shard_map/ppermute | solution.py:485
  171.5 24.0 %collective-permute-start.4 = (bf16[4096,128]{1,0:T(8,128)(2,1)S(1)}, bf16[4096,128]{1,0:T(8,128)(2,1)}, u32[]{:S(2)}, u32[]{:S(2)}) collective-permute-start(bf16[4096,128]{1,0:T(8,128)(2,1)S(1)} %get-tuple-element.36.refs_0_.f0), channel_id=1, source_target_pairs={{1,0},{2,1},{3,2},{4,3},{5,4},{6,5},{7,6},{9,8},{10,9},{11,10},{12... | collective-permute-start | bytes 3145736 | tf_op jit(solution)/shard_map/ppermute | solution.py:484
  189.0 14.9 %collective-permute-start = (bf16[24,32,128]{2,1,0:T(8,128)(2,1)S(1)}, bf16[24,32,128]{2,1,0:T(8,128)(2,1)S(1)}, u32[]{:S(2)}, u32[]{:S(2)}) collective-permute-start(bf16[24,32,128]{2,1,0:T(8,128)(2,1)S(1)} %get-tuple-element.43), channel_id=1, source_target_pairs={{0,64},{64,128},{128,192},{192,0},{1,65},{65,129},{129,193},{193,1... | collective-permute-start | bytes 589832 | tf_op jit(solution)/shard_map/ppermute | solution.py:361
  190.7 13.2 %collective-permute-start.1 = (bf16[24,32,128]{2,1,0:T(8,128)(2,1)S(1)}, bf16[24,32,128]{2,1,0:T(8,128)(2,1)S(1)}, u32[]{:S(2)}, u32[]{:S(2)}) collective-permute-start(bf16[24,32,128]{2,1,0:T(8,128)(2,1)S(1)} %get-tuple-element.44), channel_id=1, source_target_pairs={{0,128},{64,192},{128,0},{192,64},{1,129},{65,193},{129,1},{193,65... | collective-permute-start | bytes 589832 | tf_op jit(solution)/shard_map/ppermute | solution.py:361
  193.6 10.3 %collective-permute-start.2 = (bf16[24,32,128]{2,1,0:T(8,128)(2,1)S(1)}, bf16[24,32,128]{2,1,0:T(8,128)(2,1)S(1)}, u32[]{:S(2)}, u32[]{:S(2)}) collective-permute-start(bf16[24,32,128]{2,1,0:T(8,128)(2,1)S(1)} %get-tuple-element.45), channel_id=1, source_target_pairs={{0,192},{64,0},{128,64},{192,128},{1,193},{65,1},{129,65},{193,129... | collective-permute-start | bytes 589832 | tf_op jit(solution)/shard_map/ppermute | solution.py:361
  198.2 17.2 %collective-permute-start.5 = (f32[128,128]{1,0:T(8,128)S(1)}, f32[128,128]{1,0:T(8,128)S(1)}, u32[]{:S(2)}, u32[]{:S(2)}) collective-permute-start(f32[128,128]{1,0:T(8,128)S(1)} %get-tuple-element.48), channel_id=1, source_target_pairs={{1,0},{2,1},{3,2},{4,3},{5,4},{6,5},{7,6},{9,8},{10,9},{11,10},{12... | collective-permute-start | bytes 196616 | tf_op jit(solution)/shard_map/ppermute | solution.py:492
  202.0 13.4 %collective-permute-start.6 = (f32[128,128]{1,0:T(8,128)S(1)}, f32[128,128]{1,0:T(8,128)S(1)}, u32[]{:S(2)}, u32[]{:S(2)}) collective-permute-start(f32[128,128]{1,0:T(8,128)S(1)} %get-tuple-element.49), channel_id=1, source_target_pairs={{0,1},{1,2},{2,3},{3,4},{4,5},{5,6},{6,7},{8,9},{9,10},{10,11},{11... | collective-permute-start | bytes 196616 | tf_op jit(solution)/shard_map/ppermute | solution.py:493
  203.9 23.9 %copy-start.6 = (s32[127,2]{0,1:T(2,128)S(1)}, s32[127,2]{0,1:T(2,128)}, u32[]{:S(2)}) copy-start(s32[127,2]{0,1:T(2,128)} %param.6) | copy-start | bytes 3052
  215.4 15.2 %collective-permute-start.7 = (bf16[12,32,128]{2,1,0:T(8,128)(2,1)S(1)}, bf16[12,32,128]{2,1,0:T(8,128)(2,1)S(1)}, u32[]{:S(2)}, u32[]{:S(2)}) collective-permute-start(bf16[12,32,128]{2,1,0:T(8,128)(2,1)S(1)} %get-tuple-element.50), channel_id=1, source_target_pairs={{0,8},{1,9},{2,10},{3,11},{4,12},{5,13},{6,14},{7,15},{8,0},{9,1},... | collective-permute-start | bytes 294920 | tf_op jit(solution)/shard_map/ppermute | solution.py:503
  223.3 8.1 %collective-permute-start.8 = (bf16[12,32,128]{2,1,0:T(8,128)(2,1)S(1)}, bf16[12,32,128]{2,1,0:T(8,128)(2,1)S(1)}, u32[]{:S(2)}, u32[]{:S(2)}) collective-permute-start(bf16[12,32,128]{2,1,0:T(8,128)(2,1)S(1)} %get-tuple-element.56), channel_id=1, source_target_pairs={{0,64},{1,65},{2,66},{3,67},{4,68},{5,69},{6,70},{7,71},{8,72},{9,... | collective-permute-start | bytes 294920 | tf_op jit(solution)/shard_map/ppermute | solution.py:503
  224.9 8.6 %collective-permute-start.9 = (bf16[12,32,128]{2,1,0:T(8,128)(2,1)S(1)}, bf16[12,32,128]{2,1,0:T(8,128)(2,1)S(1)}, u32[]{:S(2)}, u32[]{:S(2)}) collective-permute-start(bf16[12,32,128]{2,1,0:T(8,128)(2,1)S(1)} %get-tuple-element.57), channel_id=1, source_target_pairs={{0,128},{1,129},{2,130},{3,131},{4,132},{5,133},{6,134},{7,135},{8... | collective-permute-start | bytes 294920 | tf_op jit(solution)/shard_map/ppermute | solution.py:503
  227.8 7.1 %collective-permute-start.10 = (bf16[12,32,128]{2,1,0:T(8,128)(2,1)S(1)}, bf16[12,32,128]{2,1,0:T(8,128)(2,1)S(1)}, u32[]{:S(2)}, u32[]{:S(2)}) collective-permute-start(bf16[12,32,128]{2,1,0:T(8,128)(2,1)S(1)} %get-tuple-element.58), channel_id=1, source_target_pairs={{0,192},{1,193},{2,194},{3,195},{4,196},{5,197},{6,198},{7,199},{8... | collective-permute-start | bytes 294920 | tf_op jit(solution)/shard_map/ppermute | solution.py:503
  229.2 5.8 %collective-permute-start.11 = (bf16[12,32,128]{2,1,0:T(8,128)(2,1)S(1)}, bf16[12,32,128]{2,1,0:T(8,128)(2,1)S(1)}, u32[]{:S(2)}, u32[]{:S(2)}) collective-permute-start(bf16[12,32,128]{2,1,0:T(8,128)(2,1)S(1)} %get-tuple-element.59), channel_id=1, source_target_pairs={{0,8},{1,9},{2,10},{3,11},{4,12},{5,13},{6,14},{7,15},{8,0},{9,1},... | collective-permute-start | bytes 294920 | tf_op jit(solution)/shard_map/ppermute | solution.py:503
  230.6 7.0 %collective-permute-start.12 = (bf16[12,32,128]{2,1,0:T(8,128)(2,1)S(1)}, bf16[12,32,128]{2,1,0:T(8,128)(2,1)S(1)}, u32[]{:S(2)}, u32[]{:S(2)}) collective-permute-start(bf16[12,32,128]{2,1,0:T(8,128)(2,1)S(1)} %get-tuple-element.60), channel_id=1, source_target_pairs={{0,72},{1,73},{2,74},{3,75},{4,76},{5,77},{6,78},{7,79},{8,64},{9,... | collective-permute-start | bytes 294920 | tf_op jit(solution)/shard_map/ppermute | solution.py:503
  231.3 7.3 %collective-permute-start.13 = (bf16[12,32,128]{2,1,0:T(8,128)(2,1)S(1)}, bf16[12,32,128]{2,1,0:T(8,128)(2,1)S(1)}, u32[]{:S(2)}, u32[]{:S(2)}) collective-permute-start(bf16[12,32,128]{2,1,0:T(8,128)(2,1)S(1)} %get-tuple-element.61), channel_id=1, source_target_pairs={{0,136},{1,137},{2,138},{3,139},{4,140},{5,141},{6,142},{7,143},{8... | collective-permute-start | bytes 294920 | tf_op jit(solution)/shard_map/ppermute | solution.py:503
  233.5 5.8 %collective-permute-start.14 = (bf16[12,32,128]{2,1,0:T(8,128)(2,1)S(1)}, bf16[12,32,128]{2,1,0:T(8,128)(2,1)S(1)}, u32[]{:S(2)}, u32[]{:S(2)}) collective-permute-start(bf16[12,32,128]{2,1,0:T(8,128)(2,1)S(1)} %get-tuple-element.62), channel_id=1, source_target_pairs={{0,200},{1,201},{2,202},{3,203},{4,204},{5,205},{6,206},{7,207},{8... | collective-permute-start | bytes 294920 | tf_op jit(solution)/shard_map/ppermute | solution.py:503
  239.4 6.3 %collective-permute-start.15 = (bf16[6,32,128]{2,1,0:T(8,128)(2,1)S(1)}, bf16[6,32,128]{2,1,0:T(8,128)(2,1)S(1)}, u32[]{:S(2)}, u32[]{:S(2)}) collective-permute-start(bf16[6,32,128]{2,1,0:T(8,128)(2,1)S(1)} %get-tuple-element.64), channel_id=1, source_target_pairs={{0,16},{1,17},{2,18},{3,19},{4,20},{5,21},{6,22},{7,23},{8,24},{9,... | collective-permute-start | bytes 147464 | tf_op jit(solution)/shard_map/ppermute | solution.py:509
  239.5 8.6 %collective-permute-start.16 = (bf16[6,32,128]{2,1,0:T(8,128)(2,1)S(1)}, bf16[6,32,128]{2,1,0:T(8,128)(2,1)S(1)}, u32[]{:S(2)}, u32[]{:S(2)}) collective-permute-start(bf16[6,32,128]{2,1,0:T(8,128)(2,1)S(1)} %get-tuple-element.65), channel_id=1, source_target_pairs={{0,32},{1,33},{2,34},{3,35},{4,36},{5,37},{6,38},{7,39},{8,40},{9,... | collective-permute-start | bytes 147464 | tf_op jit(solution)/shard_map/ppermute | solution.py:509
  242.0 6.1 %collective-permute-start.17 = (bf16[6,32,128]{2,1,0:T(8,128)(2,1)S(1)}, bf16[6,32,128]{2,1,0:T(8,128)(2,1)S(1)}, u32[]{:S(2)}, u32[]{:S(2)}) collective-permute-start(bf16[6,32,128]{2,1,0:T(8,128)(2,1)S(1)} %get-tuple-element.66), channel_id=1, source_target_pairs={{0,48},{1,49},{2,50},{3,51},{4,52},{5,53},{6,54},{7,55},{8,56},{9,... | collective-permute-start | bytes 147464 | tf_op jit(solution)/shard_map/ppermute | solution.py:509
  248.2 12.6 %collective-permute-start.18 = (f32[32,640]{1,0:T(8,128)S(1)}, f32[32,640]{1,0:T(8,128)S(1)}, u32[]{:S(2)}, u32[]{:S(2)}) collective-permute-start(f32[32,640]{1,0:T(8,128)S(1)} %finish.1), channel_id=1, source_target_pairs={{0,0},{1,8},{2,16},{3,24},{4,32},{5,40},{6,48},{7,56},{8,1},{9,9},... | collective-permute-start | bytes 245768 | tf_op jit(solution)/shard_map/ppermute | solution.py:512
  (4 other events, 50.3 us)

commit v5 on v4

--- a/solution.py
+++ b/solution.py
@@ -13,6 +13,7 @@
 PAIR = 2 * BS
 BAND = 5
 PART = BS // NY
+PARTS = 2
 FIRST = (0, 7, 1, 2, 5, 6)
 LAST = (3, 4)
 VMEM = pltpu.MemorySpace.VMEM
@@ -77,11 +78,11 @@
 
 
 def cut_kernel(source, out_ref, held, sems, *, blocks):
-    half = NZ * NC // 2
+    size = NZ * NC // PARTS
 
     def gather(part):
         def one(n, carry):
-            k = part * half + n
+            k = part * size + n
             z, c = k // NC, k % NC
             for start, at, width in runs(blocks):
                 begin = pl.multiple_of(c * 1024 + start, BS)
@@ -90,15 +91,15 @@
                 ).start()
             return carry
 
-        lax.fori_loop(0, half, one, 0)
-
-    gather(0)
-    gather(1)
+        lax.fori_loop(0, size, one, 0)
+
+    for part in range(PARTS):
+        gather(part)
     writes = []
-    for part in range(2):
-        here = held.at[pl.ds(part * half, half)]
+    for part in range(PARTS):
+        here = held.at[pl.ds(part * size, size)]
         pltpu.make_async_copy(here, here, sems.at[part]).wait()
-        write = pltpu.make_async_copy(here, out_ref.at[pl.ds(part * half, half)], sems.at[2 + part])
+        write = pltpu.make_async_copy(here, out_ref.at[pl.ds(part * size, size)], sems.at[PARTS + part])
         write.start()
         writes.append(write)
     for write in writes:
@@ -112,17 +113,18 @@
         out_shape=jax.ShapeDtypeStruct(shape, jnp.bfloat16),
         in_specs=[pl.BlockSpec(memory_space=pl.ANY)],
         out_specs=pl.BlockSpec(memory_space=pl.ANY),
-        scratch_shapes=[pltpu.VMEM(shape, jnp.bfloat16), pltpu.SemaphoreType.DMA((4,))],
+        scratch_shapes=[pltpu.VMEM(shape, jnp.bfloat16), pltpu.SemaphoreType.DMA((2 * PARTS,))],
         compiler_params=pltpu.CompilerParams(vmem_limit_bytes=60 << 20),
         cost_estimate=pl.CostEstimate(flops=0, bytes_accessed=2 * 8192 * shape[3], transcendentals=0),
         name="cut_chunk",
     )(integrals.reshape(8, NZ, 8, NC * 1024))
 
 
-def turn_rows(rows_ref, perm_ref, turned_ref, first, count):
+def turn_rows(rows_refs, perm_ref, turned_ref, first, count):
     def turn(g, carry):
         start = pl.multiple_of(g * 256, 256)
-        turned = jnp.dot(perm_ref[...], rows_ref[pl.ds(start, 256), :], preferred_element_type=jnp.float32)
+        rows = jnp.concatenate([rows_ref[pl.ds(start, 256), :] for rows_ref in rows_refs], axis=1)
+        turned = jnp.dot(perm_ref[...], rows, preferred_element_type=jnp.float32)
         turned = turned.astype(jnp.bfloat16)
         at = pl.multiple_of(g * 32, 32)
         for i in range(8):
@@ -142,8 +144,8 @@
     return out
 
 
-def fit_kernel(rows_ref, perm_ref, metric_ref, mask_ref, out_a, out_b, turned_ref):
-    turn_rows(rows_ref, perm_ref, turned_ref, 0, 16)
+def fit_kernel(rows_a, rows_b, perm_ref, metric_ref, mask_ref, out_a, out_b, turned_ref):
+    turn_rows((rows_a, rows_b), perm_ref, turned_ref, 0, 16)
 
     def fit(i, carry):
         at = pl.multiple_of(i * 512, 512)
@@ -157,13 +159,14 @@
     return pl.BlockSpec(shape, lambda g: at or (0,) * len(shape))
 
 
-def fit_chunk(rows, at, perm, metric, mask):
+def fit_chunk(rows, pair, perm, metric, mask):
     return pl.pallas_call(
         fit_kernel,
         grid=(1,),
         out_shape=[jax.ShapeDtypeStruct((4096, BS), jnp.bfloat16)] * 2,
         in_specs=[
-            whole((4096, PAIR), (0, at)),
+            whole((4096, BS), (0, FIRST.index(pair[0]))),
+            whole((4096, BS), (0, FIRST.index(pair[1]))),
             whole((256, 256)),
             whole((512, 512)),
             pl.BlockSpec(memory_space=SMEM),
@@ -173,7 +176,7 @@
         compiler_params=pltpu.CompilerParams(vmem_limit_bytes=24 << 20),
         cost_estimate=pl.CostEstimate(flops=2 * 4096 * PAIR * 768, bytes_accessed=4 * 4096 * PAIR, transcendentals=0),
         name="fit_chunk",
-    )(rows, perm, metric, mask)
+    )(rows, rows, perm, metric, mask)
 
 
 def quarter(tile_ref, row, col, which):
@@ -271,14 +274,14 @@
         copy.start()
     for n, feed in enumerate(feeds):
         feed.wait()
-        turn_rows(rows_ref, perm_ref, turned_ref, 4 * n, 4)
+        turn_rows((rows_ref,), perm_ref, turned_ref, 4 * n, 4)
 
     def step(i, carry):
         at = pl.ds(pl.multiple_of(i * 512, 512), 512)
         left_ref[at, :BS], left_ref[at, BS:] = fit_one(metric_ref, turned_ref, mask_ref, i)
         return carry
 
-    lax.fori_loop(0, 8, step, 0, unroll=2)
+    lax.fori_loop(0, 8, step, 0, unroll=4)
     for copy in fits:
         copy.wait()
     f1, f2, f5, f6 = [right_ref[n] for n in range(4)]
@@ -414,44 +417,19 @@
     for j, out in enumerate((own_ref, o1, o2, o3)):
         k = lax.rem(half + j, 4)
         for slot in range(BAND):
-            if j == 0:
-                out[:, slot * BS : (slot + 1) * BS] = band_ref[k, slot]
-            else:
-                put_sent(out, slot, BAND if slot == 2 else None, band_ref[k, slot])
+            out[:, slot * BS : (slot + 1) * BS] = band_ref[k, slot]
 
 
 def settle(z, early, early_got, late, late_got):
     return pl.pallas_call(
         settle_kernel,
-        out_shape=[jax.ShapeDtypeStruct((PART, BAND * BS), jnp.float32)]
-        + [jax.ShapeDtypeStruct((BAND + 1, PART, BS), jnp.bfloat16)] * 3,
+        out_shape=[jax.ShapeDtypeStruct((PART, BAND * BS), jnp.float32)] * 4,
         in_specs=[pl.BlockSpec(memory_space=SMEM)] + [pl.BlockSpec(memory_space=VMEM)] * 10,
         out_specs=[pl.BlockSpec(memory_space=VMEM)] * 4,
         scratch_shapes=[pltpu.VMEM((4, BAND, PART, BS), jnp.float32)],
         compiler_params=pltpu.CompilerParams(vmem_limit_bytes=16 << 20),
         name="settle",
     )(z, early, early_got, late, *late_got)
-
-
-def finish_kernel(own_ref, g1, g2, g3, out_ref):
-    for slot in range(BAND):
-        value = own_ref[:, slot * BS : (slot + 1) * BS]
-        for got in (g1, g2, g3):
-            value = value + got[slot].astype(jnp.float32)
-            if slot == 2:
-                value = value + got[BAND].astype(jnp.float32)
-        out_ref[:, slot * BS : (slot + 1) * BS] = value
-
-
-def finish(own, got):
-    return pl.pallas_call(
-        finish_kernel,
-        out_shape=jax.ShapeDtypeStruct((PART, BAND * BS), jnp.float32),
-        in_specs=[pl.BlockSpec(memory_space=VMEM)] * 4,
-        out_specs=pl.BlockSpec(memory_space=VMEM),
-        compiler_params=pltpu.CompilerParams(vmem_limit_bytes=16 << 20),
-        name="finish",
-    )(own, *got)
 
 
 def local(integrals, metric, pair_list, aux_mask):
@@ -470,9 +448,18 @@
     mask_of = lambda *blocks: jnp.stack([own_mask[:, b] for b in blocks], axis=1)
 
     e = jnp.arange(BAND, dtype=jnp.int32) - 2
-    low, high = blk + jnp.minimum(e, 0), blk + jnp.maximum(e, 0)
+    home = c * NC + z
+    low, high = home + jnp.minimum(e, 0), home + jnp.maximum(e, 0)
     hits = (pair_list[:, 0][:, None] == low[None]) & (pair_list[:, 1][:, None] == high[None])
     scale = jnp.repeat(jnp.sum(hits.astype(jnp.float32), axis=0), BS)
+
+    whole_grid = [(a, zz, cc) for a in range(NY) for zz, cc in grid]
+
+    def move(array, d, flip):
+        pairs = [
+            (a * NZ * NC + zz * NC + cc, (a + d) % NY * NZ * NC + (zz ^ flip) * NC + cc) for a, zz, cc in whole_grid
+        ]
+        return lax.ppermute(array, AXES, pairs)
 
     def spread(blocks, source):
         got = lax.all_to_all(cut_chunk(source, blocks), "blk", split_axis=0, concat_axis=0, tiled=True)
@@ -480,37 +467,27 @@
 
     rows = spread(FIRST, integrals)
     last = spread(LAST, integrals)
-    f0, f7 = fit_chunk(rows, 0, perm, metric, mask_of(0, 7))
+    f0, f7 = fit_chunk(rows, (0, 7), perm, metric, mask_of(0, 7))
     above = lax.ppermute(f0, "blk", down)
     below = lax.ppermute(f7, "blk", up)
-    f1, f2 = fit_chunk(rows, 1, perm, metric, mask_of(1, 2))
-    f5, f6 = fit_chunk(rows, 2, perm, metric, mask_of(5, 6))
+    f1, f2 = fit_chunk(rows, (1, 2), perm, metric, mask_of(1, 2))
+    f5, f6 = fit_chunk(rows, (5, 6), perm, metric, mask_of(5, 6))
 
     early, *sent = early_tiles(y, (f0, f1, f2, f5, f6, f7))
     early, early_sent = early_sum(jnp.full((1,), z % 2, jnp.int32), early, over_domains(sent))
     to_below, to_above, edges = edge_tiles(below, f0, f1, f6, f7, above)
     from_above = lax.ppermute(to_below, "blk", down)
     from_below = lax.ppermute(to_above, "blk", up)
-    early_sent, from_above, from_below, last = lax.optimization_barrier((early_sent, from_above, from_below, last))
+    early_got = move(early_sent, 0, 1)
+    early_got, from_above, from_below, last = lax.optimization_barrier((early_got, from_above, from_below, last))
 
     late, *sent = late_tiles(y, mask_of(3, 4), last, f1, f2, f5, f6, perm, metric, from_below, from_above, edges)
-    whole_grid = [(a, zz, cc) for a in range(NY) for zz, cc in grid]
-
-    def move(array, d, flip):
-        pairs = [
-            (a * NZ * NC + zz * NC + cc, (a + d) % NY * NZ * NC + (zz ^ flip) * NC + cc) for a, zz, cc in whole_grid
-        ]
-        return lax.ppermute(array, AXES, pairs)
-
-    early_got = move(early_sent, 0, 1)
     late_got = [move(s, d, 0) for d, s in enumerate(sent[:3], 1)] + [move(s, d, 1) for d, s in enumerate(sent[3:])]
-    own, *sent = settle(at_z, early, early_got, late, late_got)
-    got = [
-        lax.ppermute(s, "blk", [(zz * NC + cc, (zz + 2 * j) % NZ * NC + cc) for zz, cc in grid])
-        for j, s in enumerate(sent, 1)
-    ]
-    total = lax.ppermute(finish(own, got), "blk", [(zz * NC + cc, cc * NC + zz) for zz, cc in grid])
-    return (total * scale[None, :])[None]
+    total, *sent = settle(at_z, early, early_got, late, late_got)
+    for j, s in enumerate(sent, 1):
+        total = total + lax.ppermute(s, "blk", [(zz * NC + cc, (zz + 2 * j) % NZ * NC + cc) for zz, cc in grid])
+    total = (total * scale[None, :])[None]
+    return lax.ppermute(total, "blk", [(zz * NC + cc, cc * NC + zz) for zz, cc in grid])
 
 
 def solution(mesh):

time: 264 us -> 265 us (level)
  waiting for transfers between devices: 165 us -> 169 us
    ppermute x3, waiting for transfers between devices: 0.01 us -> 7.18 us  [over_domains(): lax.ppermute(s, 'aux', [(a, (a + d) % NY) for a in range(NY)])]
    all_to_all x2, waiting for transfers between devices: 150 us -> 143 us  [spread(): lax.all_to_all(cut_chunk(source, blocks), 'blk', split_axis=0, concat_axi...]
    ppermute x3, waiting for transfers between devices: 3.27 us -> 6.41 us  [local(): lax.ppermute(s, 'blk', [(zz * NC + cc, (zz + 2 * j) % NZ * NC + cc) for z...]
  transfers between devices with their start and end apart: 21 -> 21, of which waited for: 10 -> 11; matrix products, arithmetic and copies ran while one was open for 0% -> 0% of each run, Pallas kernels for 12% -> 9%
where the time goes in v5:
time: 265 us; the launch traced here: 264 us
  waiting for transfers between devices  169 us (64%)
  starting transfers between devices  57 us (22%)
  Pallas kernels  35.9 us (14%)
    all_to_all x2, waiting for transfers between devices, spread(): lax.all_to_all(cut_chunk(source, blocks), 'blk', split_axis=0, concat_axi...  143 us
    all_to_all x2, starting transfers between devices, spread(): lax.all_to_all(cut_chunk(source, blocks), 'blk', split_axis=0, concat_axi...  18 us
    pallas_call x3, Pallas kernels, fit_chunk(): pl.pallas_call(fit_kernel, grid=(1,), out_shape=[jax.ShapeDtypeStruct((40...  14.8 us
    ppermute x8, starting transfers between devices, move(): return lax.ppermute(array, AXES, pairs)  12.8 us
    pallas_call x2, Pallas kernels, cut_chunk(): pl.pallas_call(lambda *refs: cut_kernel(*refs, blocks=blocks), out_shape=...  7.74 us
    ppermute x1, waiting for transfers between devices, local(): lax.ppermute(total, 'blk', [(zz * NC + cc, cc * NC + zz) for zz, cc in gr...  7.71 us
    ppermute x3, waiting for transfers between devices, over_domains(): lax.ppermute(s, 'aux', [(a, (a + d) % NY) for a in range(NY)])  7.18 us
    pallas_call x1, Pallas kernels, late_tiles(): pl.pallas_call(late_kernel, out_shape=[jax.ShapeDtypeStruct((LATE_HALF, P...  6.97 us
  transfers between devices with their start and end apart: 21, of which 11 were waited for; matrix products, arithmetic and copies ran while one was open for 0% of the time, Pallas kernels for 9%

profile of v5, /device:TPU:4, one launch (start us, length us, event | category | flops | bytes accessed | tf_op | source)
XLA Modules:
  0.0 263.9 jit_solution(1255660036668189583)
XLA Ops:
  0.0 4.9 %cut_chunk.2 = bf16[64,8,8,768]{3,2,1,0:T(8,128)(2,1)} custom-call(bf16[8,8,8,8192]{3,2,1,0:T(8,128)(2,1)} %bitcast.14), custom_call_target="tpu_custom_call" | custom-call | bytes 12582912 | tf_op jit(solution)/shard_map/cut_chunk/pallas_call | solution.py:111
  4.9 12.2 %all-to-all-start = ((bf16[64,8,8,768]{3,2,1,0:T(8,128)(2,1)}), bf16[64,8,8,768]{3,2,1,0:T(8,128)(2,1)}, u32[]{:S(2)}, u32[]{:S(2)}) async-start(bf16[64,8,8,768]{3,2,1,0:T(8,128)(2,1)} %cut_chunk.2), calls=%async_computation | async-start | bytes 12582912 | tf_op jit(solution)/shard_map/all_to_all | solution.py:465
  17.1 2.8 %cut_chunk.3 = bf16[64,8,8,256]{3,2,1,0:T(8,128)(2,1)} custom-call(bf16[8,8,8,8192]{3,2,1,0:T(8,128)(2,1)} %bitcast.15), custom_call_target="tpu_custom_call" | custom-call | bytes 4194304 | tf_op jit(solution)/shard_map/cut_chunk/pallas_call | solution.py:111
  20.0 138.4 %all-to-all-done = bf16[64,8,8,768]{3,2,1,0:T(8,128)(2,1)} async-done(((bf16[64,8,8,768]{3,2,1,0:T(8,128)(2,1)}), bf16[64,8,8,768]{3,2,1,0:T(8,128)(2,1)}, u32[]{:S(2)}, u32[]{:S(2)}) %all-to-all-start) | async-done | bytes 6291488 | tf_op jit(solution)/shard_map/all_to_all | solution.py:465
  158.3 5.8 %all-to-all-start.1 = ((bf16[64,8,8,256]{3,2,1,0:T(8,128)(2,1)}), bf16[64,8,8,256]{3,2,1,0:T(8,128)(2,1)}, u32[]{:S(2)}, u32[]{:S(2)}) async-start(bf16[64,8,8,256]{3,2,1,0:T(8,128)(2,1)} %cut_chunk.3), calls=%async_computation.1 | async-start | bytes 4194304 | tf_op jit(solution)/shard_map/all_to_all | solution.py:465
  164.8 4.7 %fit_chunk.3 = (bf16[4096,128]{1,0:T(8,128)(2,1)S(1)}, bf16[4096,128]{1,0:T(8,128)(2,1)S(1)}) custom-call(bf16[4096,768]{1,0:T(8,128)(2,1)} %bitcast.4.rows_a.rows_b, bf16[4096,768]{1,0:T(8,128)(2,1)} %bitcast.4.rows_a.rows_b, bf16[256,256]{1,0:T(8,128)(2,1)S(1)} %fusion.1.perm_ref, bf16[512,512]{1,0:T(8,128)(2,1)S(1)} %copy-done, ...), custom_call_target="tpu_custom_call" | custom-call | flops 1610612736 | bytes 4194304 | tf_op jit(solution)/shard_map/fit_chunk/pallas_call | solution.py:163
  171.5 3.5 %collective-permute-start.5 = (bf16[4096,128]{1,0:T(8,128)(2,1)S(1)}, bf16[4096,128]{1,0:T(8,128)(2,1)}, u32[]{:S(2)}, u32[]{:S(2)}) collective-permute-start(bf16[4096,128]{1,0:T(8,128)(2,1)S(1)} %get-tuple-element.36.refs_0_.f0), channel_id=1, source_target_pairs={{1,0},{2,1},{3,2},{4,3},{5,4},{6,5},{7,6},{9,8},{10,9},{11,10},{12... | collective-permute-start | bytes 3145736 | tf_op jit(solution)/shard_map/ppermute | solution.py:471
  175.2 4.7 %fit_chunk.4 = (bf16[4096,128]{1,0:T(8,128)(2,1)S(1)}, bf16[4096,128]{1,0:T(8,128)(2,1)S(1)}) custom-call(bf16[4096,768]{1,0:T(8,128)(2,1)} %bitcast.4.rows_a.rows_b, bf16[4096,768]{1,0:T(8,128)(2,1)} %bitcast.4.rows_a.rows_b, bf16[256,256]{1,0:T(8,128)(2,1)S(1)} %fusion.1.perm_ref, bf16[512,512]{1,0:T(8,128)(2,1)S(1)} %copy-done, ...), custom_call_target="tpu_custom_call" | custom-call | flops 1610612736 | bytes 4194304 | tf_op jit(solution)/shard_map/fit_chunk/pallas_call | solution.py:163
  179.9 5.4 %fit_chunk.5 = (bf16[4096,128]{1,0:T(8,128)(2,1)S(1)}, bf16[4096,128]{1,0:T(8,128)(2,1)S(1)}) custom-call(bf16[4096,768]{1,0:T(8,128)(2,1)} %bitcast.4.rows_a.rows_b, bf16[4096,768]{1,0:T(8,128)(2,1)} %bitcast.4.rows_a.rows_b, bf16[256,256]{1,0:T(8,128)(2,1)S(1)} %fusion.1.perm_ref, bf16[512,512]{1,0:T(8,128)(2,1)S(1)} %copy-done, ...), custom_call_target="tpu_custom_call" | custom-call | flops 1610612736 | bytes 4194304 | tf_op jit(solution)/shard_map/fit_chunk/pallas_call | solution.py:163
  185.4 3.6 %early_tiles.1 = (f32[18,32,128]{2,1,0:T(8,128)S(1)}, bf16[24,32,128]{2,1,0:T(8,128)(2,1)S(1)}, bf16[24,32,128]{2,1,0:T(8,128)(2,1)S(1)}, bf16[24,32,128]{2,1,0:T(8,128)(2,1)S(1)}) custom-call(s32[2]{0:T(128)S(1)} %pad_add_fusion.y_ref, bf16[4096,128]{1,0:T(8,128)(2,1)S(1)} %get-tuple-element.36.refs_0_.f0, ...), custom_call_target="tpu_custom_call" | custom-call | flops 2147483648 | bytes 7340032 | tf_op jit(solution)/shard_map/early_tiles/pallas_call | solution.py:321
  190.6 2.9 %collective-permute-start.1 = (bf16[24,32,128]{2,1,0:T(8,128)(2,1)S(1)}, bf16[24,32,128]{2,1,0:T(8,128)(2,1)S(1)}, u32[]{:S(2)}, u32[]{:S(2)}) collective-permute-start(bf16[24,32,128]{2,1,0:T(8,128)(2,1)S(1)} %get-tuple-element.44), channel_id=1, source_target_pairs={{0,128},{64,192},{128,0},{192,64},{1,129},{65,193},{129,1},{193,65... | collective-permute-start | bytes 589832 | tf_op jit(solution)/shard_map/ppermute | solution.py:364
  194.9 2.1 collective-permute-done.g1
  197.0 5.1 %collective-permute-done.1.g2 = bf16[24,32,128]{2,1,0:T(8,128)(2,1)S(1)} collective-permute-done((bf16[24,32,128]{2,1,0:T(8,128)(2,1)S(1)}, bf16[24,32,128]{2,1,0:T(8,128)(2,1)S(1)}, u32[]{:S(2)}, u32[]{:S(2)}) %collective-permute-start.1) | collective-permute-done | bytes 196640 | tf_op jit(solution)/shard_map/ppermute | solution.py:364
  203.8 2.6 edge_tiles.1
  208.4 2.6 collective-permute-start.7
  211.0 4.7 %all-to-all-done.1 = bf16[64,8,8,256]{3,2,1,0:T(8,128)(2,1)} async-done(((bf16[64,8,8,256]{3,2,1,0:T(8,128)(2,1)}), bf16[64,8,8,256]{3,2,1,0:T(8,128)(2,1)}, u32[]{:S(2)}, u32[]{:S(2)}) %all-to-all-start.1) | async-done | bytes 2097184 | tf_op jit(solution)/shard_map/all_to_all | solution.py:465
  215.7 7.0 %late_tiles.1 = (f32[11,32,128]{2,1,0:T(8,128)S(1)}, bf16[12,32,128]{2,1,0:T(8,128)(2,1)S(1)}, bf16[12,32,128]{2,1,0:T(8,128)(2,1)S(1)}, bf16[12,32,128]{2,1,0:T...) custom-call(s32[2]{0:T(128)S(1)} %pad_add_fusion.y_ref, ...), custom_call_target="tpu_custom_call" | custom-call | flops 3221225472 | bytes 8388608 | tf_op jit(solution)/shard_map/late_tiles/pallas_call | solution.py:339
  224.3 2.9 %collective-permute-start.9 = (bf16[12,32,128]{2,1,0:T(8,128)(2,1)S(1)}, bf16[12,32,128]{2,1,0:T(8,128)(2,1)S(1)}, u32[]{:S(2)}, u32[]{:S(2)}) collective-permute-start(bf16[12,32,128]{2,1,0:T(8,128)(2,1)S(1)} %get-tuple-element.57), channel_id=1, source_target_pairs={{0,128},{1,129},{2,130},{3,131},{4,132},{5,133},{6,134},{7,135},{8... | collective-permute-start | bytes 294920 | tf_op jit(solution)/shard_map/ppermute | solution.py:462
  231.6 2.3 collective-permute-start.14
  234.1 3.0 %collective-permute-done.12.rest_4_ = bf16[12,32,128]{2,1,0:T(8,128)(2,1)S(1)} collective-permute-done((bf16[12,32,128]{2,1,0:T(8,128)(2,1)S(1)}, bf16[12,32,128]{2,1,0:T(8,128)(2,1)S(1)}, u32[]{:S(2)}, u32[]{:S(2)}) %collective-permute-start.12) | collective-permute-done | bytes 98336 | tf_op jit(solution)/shard_map/ppermute | solution.py:462
  239.5 3.3 %collective-permute-start.16 = (f32[32,640]{1,0:T(8,128)S(1)}, f32[32,640]{1,0:T(8,128)S(1)}, u32[]{:S(2)}, u32[]{:S(2)}) collective-permute-start(f32[32,640]{1,0:T(8,128)S(1)} %get-tuple-element.65), channel_id=1, source_target_pairs={{0,32},{1,33},{2,34},{3,35},{4,36},{5,37},{6,38},{7,39},{8,40},{9,... | collective-permute-start | bytes 245768 | tf_op jit(solution)/shard_map/ppermute | solution.py:488
  248.3 2.3 collective-permute-done.15
  250.6 4.9 %collective-permute-start.18 = (f32[1,32,640]{2,1,0:T(8,128)S(1)}, f32[1,32,640]{2,1,0:T(8,128)S(1)}, u32[]{:S(2)}, u32[]{:S(2)}) collective-permute-start(f32[1,32,640]{2,1,0:T(8,128)S(1)} %multiply_bitcast_fusion), channel_id=1, source_target_pairs={{0,0},{1,8},{2,16},{3,24},{4,32},{5,40},{6,48},{7,56},{8,1},{9,9},... | collective-permute-start | bytes 245768 | tf_op jit(solution)/shard_map/ppermute | solution.py:490
  255.6 7.7 %collective-permute-done.18 = f32[1,32,640]{2,1,0:T(8,128)S(1)} collective-permute-done((f32[1,32,640]{2,1,0:T(8,128)S(1)}, f32[1,32,640]{2,1,0:T(8,128)S(1)}, u32[]{:S(2)}, u32[]{:S(2)}) %collective-permute-start.18) | collective-permute-done | bytes 81952 | tf_op jit(solution)/shard_map/ppermute | solution.py:490
  (60 shorter events, 24.2 us)
Async XLA Ops:
  4.9 153.4 %all-to-all-start = ((bf16[64,8,8,768]{3,2,1,0:T(8,128)(2,1)}), bf16[64,8,8,768]{3,2,1,0:T(8,128)(2,1)}, u32[]{:S(2)}, u32[]{:S(2)}) async-start(bf16[64,8,8,768]{3,2,1,0:T(8,128)(2,1)} %cut_chunk.2), calls=%async_computation | async-start | bytes 12582912 | tf_op jit(solution)/shard_map/all_to_all | solution.py:465
  17.1 147.1 %copy-start.5 = (s32[4,64]{1,0:T(4,128)S(1)}, s32[4,64]{1,0:T(4,128)}, u32[]{:S(2)}) copy-start(s32[4,64]{1,0:T(4,128)} %param.7) | copy-start | bytes 3076
  17.1 147.6 %copy-start = (bf16[512,512]{1,0:T(8,128)(2,1)S(1)}, bf16[512,512]{1,0:T(8,128)(2,1)}, u32[]{:S(2)}) copy-start(bf16[512,512]{1,0:T(8,128)(2,1)} %metric_ref.7) | copy-start | bytes 1572868
  158.3 57.4 %all-to-all-start.1 = ((bf16[64,8,8,256]{3,2,1,0:T(8,128)(2,1)}), bf16[64,8,8,256]{3,2,1,0:T(8,128)(2,1)}, u32[]{:S(2)}, u32[]{:S(2)}) async-start(bf16[64,8,8,256]{3,2,1,0:T(8,128)(2,1)} %cut_chunk.3), calls=%async_computation.1 | async-start | bytes 4194304 | tf_op jit(solution)/shard_map/all_to_all | solution.py:465
  169.4 34.3 %collective-permute-start.4 = (bf16[4096,128]{1,0:T(8,128)(2,1)S(1)}, bf16[4096,128]{1,0:T(8,128)(2,1)}, u32[]{:S(2)}, u32[]{:S(2)}) collective-permute-start(bf16[4096,128]{1,0:T(8,128)(2,1)S(1)} %get-tuple-element.41.refs_5_.f7), channel_id=1, source_target_pairs={{0,1},{1,2},{2,3},{3,4},{4,5},{5,6},{6,7},{8,9},{9,10},{10,11},{11... | collective-permute-start | bytes 3145736 | tf_op jit(solution)/shard_map/ppermute | solution.py:472
  171.5 32.3 %collective-permute-start.5 = (bf16[4096,128]{1,0:T(8,128)(2,1)S(1)}, bf16[4096,128]{1,0:T(8,128)(2,1)}, u32[]{:S(2)}, u32[]{:S(2)}) collective-permute-start(bf16[4096,128]{1,0:T(8,128)(2,1)S(1)} %get-tuple-element.36.refs_0_.f0), channel_id=1, source_target_pairs={{1,0},{2,1},{3,2},{4,3},{5,4},{6,5},{7,6},{9,8},{10,9},{11,10},{12... | collective-permute-start | bytes 3145736 | tf_op jit(solution)/shard_map/ppermute | solution.py:471
  185.4 25.6 %copy-start.6 = (s32[127,2]{0,1:T(2,128)S(1)}, s32[127,2]{0,1:T(2,128)}, u32[]{:S(2)}) copy-start(s32[127,2]{0,1:T(2,128)} %param.6) | copy-start | bytes 3052
  189.0 8.0 %collective-permute-start = (bf16[24,32,128]{2,1,0:T(8,128)(2,1)S(1)}, bf16[24,32,128]{2,1,0:T(8,128)(2,1)S(1)}, u32[]{:S(2)}, u32[]{:S(2)}) collective-permute-start(bf16[24,32,128]{2,1,0:T(8,128)(2,1)S(1)} %get-tuple-element.43), channel_id=1, source_target_pairs={{0,64},{64,128},{128,192},{192,0},{1,65},{65,129},{129,193},{193,1... | collective-permute-start | bytes 589832 | tf_op jit(solution)/shard_map/ppermute | solution.py:364
  190.6 11.5 %collective-permute-start.1 = (bf16[24,32,128]{2,1,0:T(8,128)(2,1)S(1)}, bf16[24,32,128]{2,1,0:T(8,128)(2,1)S(1)}, u32[]{:S(2)}, u32[]{:S(2)}) collective-permute-start(bf16[24,32,128]{2,1,0:T(8,128)(2,1)S(1)} %get-tuple-element.44), channel_id=1, source_target_pairs={{0,128},{64,192},{128,0},{192,64},{1,129},{65,193},{129,1},{193,65... | collective-permute-start | bytes 589832 | tf_op jit(solution)/shard_map/ppermute | solution.py:364
  193.6 8.5 %collective-permute-start.2 = (bf16[24,32,128]{2,1,0:T(8,128)(2,1)S(1)}, bf16[24,32,128]{2,1,0:T(8,128)(2,1)S(1)}, u32[]{:S(2)}, u32[]{:S(2)}) collective-permute-start(bf16[24,32,128]{2,1,0:T(8,128)(2,1)S(1)} %get-tuple-element.45), channel_id=1, source_target_pairs={{0,192},{64,0},{128,64},{192,128},{1,193},{65,1},{129,65},{193,129... | collective-permute-start | bytes 589832 | tf_op jit(solution)/shard_map/ppermute | solution.py:364
  202.2 13.5 %collective-permute-start.3 = (bf16[12,32,128]{2,1,0:T(8,128)(2,1)S(1)}, bf16[12,32,128]{2,1,0:T(8,128)(2,1)S(1)}, u32[]{:S(2)}, u32[]{:S(2)}) collective-permute-start(bf16[12,32,128]{2,1,0:T(8,128)(2,1)S(1)} %get-tuple-element.47), channel_id=1, source_target_pairs={{0,8},{1,9},{2,10},{3,11},{4,12},{5,13},{6,14},{7,15},{8,0},{9,1},... | collective-permute-start | bytes 294920 | tf_op jit(solution)/shard_map/ppermute | solution.py:462
  206.4 9.2 %collective-permute-start.6 = (f32[128,128]{1,0:T(8,128)S(1)}, f32[128,128]{1,0:T(8,128)S(1)}, u32[]{:S(2)}, u32[]{:S(2)}) collective-permute-start(f32[128,128]{1,0:T(8,128)S(1)} %get-tuple-element.48), channel_id=1, source_target_pairs={{1,0},{2,1},{3,2},{4,3},{5,4},{6,5},{7,6},{9,8},{10,9},{11,10},{12... | collective-permute-start | bytes 196616 | tf_op jit(solution)/shard_map/ppermute | solution.py:479
  208.4 7.3 %collective-permute-start.7 = (f32[128,128]{1,0:T(8,128)S(1)}, f32[128,128]{1,0:T(8,128)S(1)}, u32[]{:S(2)}, u32[]{:S(2)}) collective-permute-start(f32[128,128]{1,0:T(8,128)S(1)} %get-tuple-element.49), channel_id=1, source_target_pairs={{0,1},{1,2},{2,3},{3,4},{4,5},{5,6},{6,7},{8,9},{9,10},{10,11},{11... | collective-permute-start | bytes 196616 | tf_op jit(solution)/shard_map/ppermute | solution.py:480
  222.7 8.1 %collective-permute-start.8 = (bf16[12,32,128]{2,1,0:T(8,128)(2,1)S(1)}, bf16[12,32,128]{2,1,0:T(8,128)(2,1)S(1)}, u32[]{:S(2)}, u32[]{:S(2)}) collective-permute-start(bf16[12,32,128]{2,1,0:T(8,128)(2,1)S(1)} %get-tuple-element.56), channel_id=1, source_target_pairs={{0,64},{1,65},{2,66},{3,67},{4,68},{5,69},{6,70},{7,71},{8,72},{9,... | collective-permute-start | bytes 294920 | tf_op jit(solution)/shard_map/ppermute | solution.py:462
  224.3 7.3 %collective-permute-start.9 = (bf16[12,32,128]{2,1,0:T(8,128)(2,1)S(1)}, bf16[12,32,128]{2,1,0:T(8,128)(2,1)S(1)}, u32[]{:S(2)}, u32[]{:S(2)}) collective-permute-start(bf16[12,32,128]{2,1,0:T(8,128)(2,1)S(1)} %get-tuple-element.57), channel_id=1, source_target_pairs={{0,128},{1,129},{2,130},{3,131},{4,132},{5,133},{6,134},{7,135},{8... | collective-permute-start | bytes 294920 | tf_op jit(solution)/shard_map/ppermute | solution.py:462
  227.2 6.9 %collective-permute-start.10 = (bf16[12,32,128]{2,1,0:T(8,128)(2,1)S(1)}, bf16[12,32,128]{2,1,0:T(8,128)(2,1)S(1)}, u32[]{:S(2)}, u32[]{:S(2)}) collective-permute-start(bf16[12,32,128]{2,1,0:T(8,128)(2,1)S(1)} %get-tuple-element.58), channel_id=1, source_target_pairs={{0,192},{1,193},{2,194},{3,195},{4,196},{5,197},{6,198},{7,199},{8... | collective-permute-start | bytes 294920 | tf_op jit(solution)/shard_map/ppermute | solution.py:462
  228.6 5.5 %collective-permute-start.11 = (bf16[12,32,128]{2,1,0:T(8,128)(2,1)S(1)}, bf16[12,32,128]{2,1,0:T(8,128)(2,1)S(1)}, u32[]{:S(2)}, u32[]{:S(2)}) collective-permute-start(bf16[12,32,128]{2,1,0:T(8,128)(2,1)S(1)} %get-tuple-element.59), channel_id=1, source_target_pairs={{0,8},{1,9},{2,10},{3,11},{4,12},{5,13},{6,14},{7,15},{8,0},{9,1},... | collective-permute-start | bytes 294920 | tf_op jit(solution)/shard_map/ppermute | solution.py:462
  229.2 7.9 %collective-permute-start.12 = (bf16[12,32,128]{2,1,0:T(8,128)(2,1)S(1)}, bf16[12,32,128]{2,1,0:T(8,128)(2,1)S(1)}, u32[]{:S(2)}, u32[]{:S(2)}) collective-permute-start(bf16[12,32,128]{2,1,0:T(8,128)(2,1)S(1)} %get-tuple-element.60), channel_id=1, source_target_pairs={{0,72},{1,73},{2,74},{3,75},{4,76},{5,77},{6,78},{7,79},{8,64},{9,... | collective-permute-start | bytes 294920 | tf_op jit(solution)/shard_map/ppermute | solution.py:462
  230.7 7.2 %collective-permute-start.13 = (bf16[12,32,128]{2,1,0:T(8,128)(2,1)S(1)}, bf16[12,32,128]{2,1,0:T(8,128)(2,1)S(1)}, u32[]{:S(2)}, u32[]{:S(2)}) collective-permute-start(bf16[12,32,128]{2,1,0:T(8,128)(2,1)S(1)} %get-tuple-element.61), channel_id=1, source_target_pairs={{0,136},{1,137},{2,138},{3,139},{4,140},{5,141},{6,142},{7,143},{8... | collective-permute-start | bytes 294920 | tf_op jit(solution)/shard_map/ppermute | solution.py:462
  231.6 7.1 %collective-permute-start.14 = (bf16[12,32,128]{2,1,0:T(8,128)(2,1)S(1)}, bf16[12,32,128]{2,1,0:T(8,128)(2,1)S(1)}, u32[]{:S(2)}, u32[]{:S(2)}) collective-permute-start(bf16[12,32,128]{2,1,0:T(8,128)(2,1)S(1)} %get-tuple-element.62), channel_id=1, source_target_pairs={{0,200},{1,201},{2,202},{3,203},{4,204},{5,205},{6,206},{7,207},{8... | collective-permute-start | bytes 294920 | tf_op jit(solution)/shard_map/ppermute | solution.py:462
  238.8 7.5 %collective-permute-start.17 = (f32[32,640]{1,0:T(8,128)S(1)}, f32[32,640]{1,0:T(8,128)S(1)}, u32[]{:S(2)}, u32[]{:S(2)}) collective-permute-start(f32[32,640]{1,0:T(8,128)S(1)} %get-tuple-element.66), channel_id=1, source_target_pairs={{0,48},{1,49},{2,50},{3,51},{4,52},{5,53},{6,54},{7,55},{8,56},{9,... | collective-permute-start | bytes 245768 | tf_op jit(solution)/shard_map/ppermute | solution.py:488
  239.5 8.8 %collective-permute-start.16 = (f32[32,640]{1,0:T(8,128)S(1)}, f32[32,640]{1,0:T(8,128)S(1)}, u32[]{:S(2)}, u32[]{:S(2)}) collective-permute-start(f32[32,640]{1,0:T(8,128)S(1)} %get-tuple-element.65), channel_id=1, source_target_pairs={{0,32},{1,33},{2,34},{3,35},{4,36},{5,37},{6,38},{7,39},{8,40},{9,... | collective-permute-start | bytes 245768 | tf_op jit(solution)/shard_map/ppermute | solution.py:488
  242.8 7.8 %collective-permute-start.15 = (f32[32,640]{1,0:T(8,128)S(1)}, f32[32,640]{1,0:T(8,128)S(1)}, u32[]{:S(2)}, u32[]{:S(2)}) collective-permute-start(f32[32,640]{1,0:T(8,128)S(1)} %get-tuple-element.64), channel_id=1, source_target_pairs={{0,16},{1,17},{2,18},{3,19},{4,20},{5,21},{6,22},{7,23},{8,24},{9,... | collective-permute-start | bytes 245768 | tf_op jit(solution)/shard_map/ppermute | solution.py:488
  250.6 12.6 %collective-permute-start.18 = (f32[1,32,640]{2,1,0:T(8,128)S(1)}, f32[1,32,640]{2,1,0:T(8,128)S(1)}, u32[]{:S(2)}, u32[]{:S(2)}) collective-permute-start(f32[1,32,640]{2,1,0:T(8,128)S(1)} %multiply_bitcast_fusion), channel_id=1, source_target_pairs={{0,0},{1,8},{2,16},{3,24},{4,32},{5,40},{6,48},{7,56},{8,1},{9,9},... | collective-permute-start | bytes 245768 | tf_op jit(solution)/shard_map/ppermute | solution.py:490
  (4 other events, 71.6 us)

commit v6 on v5

--- a/solution.py
+++ b/solution.py
@@ -131,7 +131,7 @@
             turned_ref[i, pl.ds(at, 32), :] = turned[i * 32 : (i + 1) * 32]
         return carry
 
-    lax.fori_loop(first, first + count, turn, 0, unroll=4)
+    lax.fori_loop(first, first + count, turn, 0, unroll=min(count, 8))
 
 
 def fit_one(metric_ref, turned_ref, mask_ref, i):
@@ -152,7 +152,7 @@
         out_a[pl.ds(at, 512), :], out_b[pl.ds(at, 512), :] = fit_one(metric_ref, turned_ref, mask_ref, i)
         return carry
 
-    lax.fori_loop(0, 8, fit, 0, unroll=2)
+    lax.fori_loop(0, 8, fit, 0, unroll=4)
 
 
 def whole(shape, at=None):

time: 265 us -> 265 us (level)
  transfers between devices with their start and end apart: 21 -> 21, of which waited for: 11 -> 11; matrix products, arithmetic and copies ran while one was open for 0% -> 0% of each run, Pallas kernels for 9% -> 8%
where the time goes in v6:
time: 265 us; the launch traced here: 264 us
  waiting for transfers between devices  171 us (65%)
  starting transfers between devices  57 us (22%)
  Pallas kernels  33.9 us (13%)
    all_to_all x2, waiting for transfers between devices, spread(): lax.all_to_all(cut_chunk(source, blocks), 'blk', split_axis=0, concat_axi...  145 us
    all_to_all x2, starting transfers between devices, spread(): lax.all_to_all(cut_chunk(source, blocks), 'blk', split_axis=0, concat_axi...  18 us
    ppermute x8, starting transfers between devices, move(): return lax.ppermute(array, AXES, pairs)  13 us
    pallas_call x3, Pallas kernels, fit_chunk(): pl.pallas_call(fit_kernel, grid=(1,), out_shape=[jax.ShapeDtypeStruct((40...  12.7 us
    pallas_call x2, Pallas kernels, cut_chunk(): pl.pallas_call(lambda *refs: cut_kernel(*refs, blocks=blocks), out_shape=...  7.74 us
    ppermute x1, waiting for transfers between devices, local(): lax.ppermute(total, 'blk', [(zz * NC + cc, cc * NC + zz) for zz, cc in gr...  7.71 us
    ppermute x3, waiting for transfers between devices, over_domains(): lax.ppermute(s, 'aux', [(a, (a + d) % NY) for a in range(NY)])  7.21 us
    pallas_call x1, Pallas kernels, late_tiles(): pl.pallas_call(late_kernel, out_shape=[jax.ShapeDtypeStruct((LATE_HALF, P...  6.97 us
  transfers between devices with their start and end apart: 21, of which 11 were waited for; matrix products, arithmetic and copies ran while one was open for 0% of the time, Pallas kernels for 8%

profile of v6, /device:TPU:4, one launch (start us, length us, event | category | flops | bytes accessed | tf_op | source)
XLA Modules:
  0.0 263.9 jit_solution(2233748914632563401)
XLA Ops:
  0.0 4.9 %cut_chunk.2 = bf16[64,8,8,768]{3,2,1,0:T(8,128)(2,1)} custom-call(bf16[8,8,8,8192]{3,2,1,0:T(8,128)(2,1)} %bitcast.14), custom_call_target="tpu_custom_call" | custom-call | bytes 12582912 | tf_op jit(solution)/shard_map/cut_chunk/pallas_call | solution.py:111
  4.9 12.2 %all-to-all-start = ((bf16[64,8,8,768]{3,2,1,0:T(8,128)(2,1)}), bf16[64,8,8,768]{3,2,1,0:T(8,128)(2,1)}, u32[]{:S(2)}, u32[]{:S(2)}) async-start(bf16[64,8,8,768]{3,2,1,0:T(8,128)(2,1)} %cut_chunk.2), calls=%async_computation | async-start | bytes 12582912 | tf_op jit(solution)/shard_map/all_to_all | solution.py:465
  17.1 2.8 %cut_chunk.3 = bf16[64,8,8,256]{3,2,1,0:T(8,128)(2,1)} custom-call(bf16[8,8,8,8192]{3,2,1,0:T(8,128)(2,1)} %bitcast.15), custom_call_target="tpu_custom_call" | custom-call | bytes 4194304 | tf_op jit(solution)/shard_map/cut_chunk/pallas_call | solution.py:111
  20.0 138.4 %all-to-all-done = bf16[64,8,8,768]{3,2,1,0:T(8,128)(2,1)} async-done(((bf16[64,8,8,768]{3,2,1,0:T(8,128)(2,1)}), bf16[64,8,8,768]{3,2,1,0:T(8,128)(2,1)}, u32[]{:S(2)}, u32[]{:S(2)}) %all-to-all-start) | async-done | bytes 6291488 | tf_op jit(solution)/shard_map/all_to_all | solution.py:465
  158.3 5.8 %all-to-all-start.1 = ((bf16[64,8,8,256]{3,2,1,0:T(8,128)(2,1)}), bf16[64,8,8,256]{3,2,1,0:T(8,128)(2,1)}, u32[]{:S(2)}, u32[]{:S(2)}) async-start(bf16[64,8,8,256]{3,2,1,0:T(8,128)(2,1)} %cut_chunk.3), calls=%async_computation.1 | async-start | bytes 4194304 | tf_op jit(solution)/shard_map/all_to_all | solution.py:465
  164.8 4.0 %fit_chunk.3 = (bf16[4096,128]{1,0:T(8,128)(2,1)S(1)}, bf16[4096,128]{1,0:T(8,128)(2,1)S(1)}) custom-call(bf16[4096,768]{1,0:T(8,128)(2,1)} %bitcast.4.rows_a.rows_b, bf16[4096,768]{1,0:T(8,128)(2,1)} %bitcast.4.rows_a.rows_b, bf16[256,256]{1,0:T(8,128)(2,1)S(1)} %fusion.1.perm_ref, bf16[512,512]{1,0:T(8,128)(2,1)S(1)} %copy-done, ...), custom_call_target="tpu_custom_call" | custom-call | flops 1610612736 | bytes 4194304 | tf_op jit(solution)/shard_map/fit_chunk/pallas_call | solution.py:163
  170.8 3.5 %collective-permute-start.5 = (bf16[4096,128]{1,0:T(8,128)(2,1)S(1)}, bf16[4096,128]{1,0:T(8,128)(2,1)}, u32[]{:S(2)}, u32[]{:S(2)}) collective-permute-start(bf16[4096,128]{1,0:T(8,128)(2,1)S(1)} %get-tuple-element.36.refs_0_.f0), channel_id=1, source_target_pairs={{1,0},{2,1},{3,2},{4,3},{5,4},{6,5},{7,6},{9,8},{10,9},{11,10},{12... | collective-permute-start | bytes 3145736 | tf_op jit(solution)/shard_map/ppermute | solution.py:471
  174.5 4.0 %fit_chunk.4 = (bf16[4096,128]{1,0:T(8,128)(2,1)S(1)}, bf16[4096,128]{1,0:T(8,128)(2,1)S(1)}) custom-call(bf16[4096,768]{1,0:T(8,128)(2,1)} %bitcast.4.rows_a.rows_b, bf16[4096,768]{1,0:T(8,128)(2,1)} %bitcast.4.rows_a.rows_b, bf16[256,256]{1,0:T(8,128)(2,1)S(1)} %fusion.1.perm_ref, bf16[512,512]{1,0:T(8,128)(2,1)S(1)} %copy-done, ...), custom_call_target="tpu_custom_call" | custom-call | flops 1610612736 | bytes 4194304 | tf_op jit(solution)/shard_map/fit_chunk/pallas_call | solution.py:163
  178.5 4.7 %fit_chunk.5 = (bf16[4096,128]{1,0:T(8,128)(2,1)S(1)}, bf16[4096,128]{1,0:T(8,128)(2,1)S(1)}) custom-call(bf16[4096,768]{1,0:T(8,128)(2,1)} %bitcast.4.rows_a.rows_b, bf16[4096,768]{1,0:T(8,128)(2,1)} %bitcast.4.rows_a.rows_b, bf16[256,256]{1,0:T(8,128)(2,1)S(1)} %fusion.1.perm_ref, bf16[512,512]{1,0:T(8,128)(2,1)S(1)} %copy-done, ...), custom_call_target="tpu_custom_call" | custom-call | flops 1610612736 | bytes 4194304 | tf_op jit(solution)/shard_map/fit_chunk/pallas_call | solution.py:163
  183.3 3.6 %early_tiles.1 = (f32[18,32,128]{2,1,0:T(8,128)S(1)}, bf16[24,32,128]{2,1,0:T(8,128)(2,1)S(1)}, bf16[24,32,128]{2,1,0:T(8,128)(2,1)S(1)}, bf16[24,32,128]{2,1,0:T(8,128)(2,1)S(1)}) custom-call(s32[2]{0:T(128)S(1)} %pad_add_fusion.y_ref, bf16[4096,128]{1,0:T(8,128)(2,1)S(1)} %get-tuple-element.36.refs_0_.f0, ...), custom_call_target="tpu_custom_call" | custom-call | flops 2147483648 | bytes 7340032 | tf_op jit(solution)/shard_map/early_tiles/pallas_call | solution.py:321
  188.6 2.9 %collective-permute-start.1 = (bf16[24,32,128]{2,1,0:T(8,128)(2,1)S(1)}, bf16[24,32,128]{2,1,0:T(8,128)(2,1)S(1)}, u32[]{:S(2)}, u32[]{:S(2)}) collective-permute-start(bf16[24,32,128]{2,1,0:T(8,128)(2,1)S(1)} %get-tuple-element.44), channel_id=1, source_target_pairs={{0,128},{64,192},{128,0},{192,64},{1,129},{65,193},{129,1},{193,65... | collective-permute-start | bytes 589832 | tf_op jit(solution)/shard_map/ppermute | solution.py:364
  192.9 2.1 collective-permute-done.g1
  195.0 5.1 %collective-permute-done.1.g2 = bf16[24,32,128]{2,1,0:T(8,128)(2,1)S(1)} collective-permute-done((bf16[24,32,128]{2,1,0:T(8,128)(2,1)S(1)}, bf16[24,32,128]{2,1,0:T(8,128)(2,1)S(1)}, u32[]{:S(2)}, u32[]{:S(2)}) %collective-permute-start.1) | collective-permute-done | bytes 196640 | tf_op jit(solution)/shard_map/ppermute | solution.py:364
  201.9 2.6 edge_tiles.1
  206.5 2.4 collective-permute-start.7
  208.9 6.7 %all-to-all-done.1 = bf16[64,8,8,256]{3,2,1,0:T(8,128)(2,1)} async-done(((bf16[64,8,8,256]{3,2,1,0:T(8,128)(2,1)}), bf16[64,8,8,256]{3,2,1,0:T(8,128)(2,1)}, u32[]{:S(2)}, u32[]{:S(2)}) %all-to-all-start.1) | async-done | bytes 2097184 | tf_op jit(solution)/shard_map/all_to_all | solution.py:465
  215.7 7.0 %late_tiles.1 = (f32[11,32,128]{2,1,0:T(8,128)S(1)}, bf16[12,32,128]{2,1,0:T(8,128)(2,1)S(1)}, bf16[12,32,128]{2,1,0:T(8,128)(2,1)S(1)}, bf16[12,32,128]{2,1,0:T...) custom-call(s32[2]{0:T(128)S(1)} %pad_add_fusion.y_ref, ...), custom_call_target="tpu_custom_call" | custom-call | flops 3221225472 | bytes 8388608 | tf_op jit(solution)/shard_map/late_tiles/pallas_call | solution.py:339
  224.3 2.9 %collective-permute-start.9 = (bf16[12,32,128]{2,1,0:T(8,128)(2,1)S(1)}, bf16[12,32,128]{2,1,0:T(8,128)(2,1)S(1)}, u32[]{:S(2)}, u32[]{:S(2)}) collective-permute-start(bf16[12,32,128]{2,1,0:T(8,128)(2,1)S(1)} %get-tuple-element.57), channel_id=1, source_target_pairs={{0,128},{1,129},{2,130},{3,131},{4,132},{5,133},{6,134},{7,135},{8... | collective-permute-start | bytes 294920 | tf_op jit(solution)/shard_map/ppermute | solution.py:462
  231.6 2.3 collective-permute-start.14
  234.1 3.0 %collective-permute-done.12.rest_4_ = bf16[12,32,128]{2,1,0:T(8,128)(2,1)S(1)} collective-permute-done((bf16[12,32,128]{2,1,0:T(8,128)(2,1)S(1)}, bf16[12,32,128]{2,1,0:T(8,128)(2,1)S(1)}, u32[]{:S(2)}, u32[]{:S(2)}) %collective-permute-start.12) | collective-permute-done | bytes 98336 | tf_op jit(solution)/shard_map/ppermute | solution.py:462
  239.4 3.4 %collective-permute-start.16 = (f32[32,640]{1,0:T(8,128)S(1)}, f32[32,640]{1,0:T(8,128)S(1)}, u32[]{:S(2)}, u32[]{:S(2)}) collective-permute-start(f32[32,640]{1,0:T(8,128)S(1)} %get-tuple-element.65), channel_id=1, source_target_pairs={{0,32},{1,33},{2,34},{3,35},{4,36},{5,37},{6,38},{7,39},{8,40},{9,... | collective-permute-start | bytes 245768 | tf_op jit(solution)/shard_map/ppermute | solution.py:488
  248.3 2.3 collective-permute-done.15
  250.6 4.9 %collective-permute-start.18 = (f32[1,32,640]{2,1,0:T(8,128)S(1)}, f32[1,32,640]{2,1,0:T(8,128)S(1)}, u32[]{:S(2)}, u32[]{:S(2)}) collective-permute-start(f32[1,32,640]{2,1,0:T(8,128)S(1)} %multiply_bitcast_fusion), channel_id=1, source_target_pairs={{0,0},{1,8},{2,16},{3,24},{4,32},{5,40},{6,48},{7,56},{8,1},{9,9},... | collective-permute-start | bytes 245768 | tf_op jit(solution)/shard_map/ppermute | solution.py:490
  255.6 7.7 %collective-permute-done.18 = f32[1,32,640]{2,1,0:T(8,128)S(1)} collective-permute-done((f32[1,32,640]{2,1,0:T(8,128)S(1)}, f32[1,32,640]{2,1,0:T(8,128)S(1)}, u32[]{:S(2)}, u32[]{:S(2)}) %collective-permute-start.18) | collective-permute-done | bytes 81952 | tf_op jit(solution)/shard_map/ppermute | solution.py:490
  (60 shorter events, 24.3 us)
Async XLA Ops:
  4.9 153.4 %all-to-all-start = ((bf16[64,8,8,768]{3,2,1,0:T(8,128)(2,1)}), bf16[64,8,8,768]{3,2,1,0:T(8,128)(2,1)}, u32[]{:S(2)}, u32[]{:S(2)}) async-start(bf16[64,8,8,768]{3,2,1,0:T(8,128)(2,1)} %cut_chunk.2), calls=%async_computation | async-start | bytes 12582912 | tf_op jit(solution)/shard_map/all_to_all | solution.py:465
  17.1 147.1 %copy-start.5 = (s32[4,64]{1,0:T(4,128)S(1)}, s32[4,64]{1,0:T(4,128)}, u32[]{:S(2)}) copy-start(s32[4,64]{1,0:T(4,128)} %param.7) | copy-start | bytes 3076
  17.1 147.6 %copy-start = (bf16[512,512]{1,0:T(8,128)(2,1)S(1)}, bf16[512,512]{1,0:T(8,128)(2,1)}, u32[]{:S(2)}) copy-start(bf16[512,512]{1,0:T(8,128)(2,1)} %metric_ref.7) | copy-start | bytes 1572868
  158.3 57.4 %all-to-all-start.1 = ((bf16[64,8,8,256]{3,2,1,0:T(8,128)(2,1)}), bf16[64,8,8,256]{3,2,1,0:T(8,128)(2,1)}, u32[]{:S(2)}, u32[]{:S(2)}) async-start(bf16[64,8,8,256]{3,2,1,0:T(8,128)(2,1)} %cut_chunk.3), calls=%async_computation.1 | async-start | bytes 4194304 | tf_op jit(solution)/shard_map/all_to_all | solution.py:465
  168.8 33.2 %collective-permute-start.4 = (bf16[4096,128]{1,0:T(8,128)(2,1)S(1)}, bf16[4096,128]{1,0:T(8,128)(2,1)}, u32[]{:S(2)}, u32[]{:S(2)}) collective-permute-start(bf16[4096,128]{1,0:T(8,128)(2,1)S(1)} %get-tuple-element.41.refs_5_.f7), channel_id=1, source_target_pairs={{0,1},{1,2},{2,3},{3,4},{4,5},{5,6},{6,7},{8,9},{9,10},{10,11},{11... | collective-permute-start | bytes 3145736 | tf_op jit(solution)/shard_map/ppermute | solution.py:472
  170.8 31.1 %collective-permute-start.5 = (bf16[4096,128]{1,0:T(8,128)(2,1)S(1)}, bf16[4096,128]{1,0:T(8,128)(2,1)}, u32[]{:S(2)}, u32[]{:S(2)}) collective-permute-start(bf16[4096,128]{1,0:T(8,128)(2,1)S(1)} %get-tuple-element.36.refs_0_.f0), channel_id=1, source_target_pairs={{1,0},{2,1},{3,2},{4,3},{5,4},{6,5},{7,6},{9,8},{10,9},{11,10},{12... | collective-permute-start | bytes 3145736 | tf_op jit(solution)/shard_map/ppermute | solution.py:471
  183.3 25.6 %copy-start.6 = (s32[127,2]{0,1:T(2,128)S(1)}, s32[127,2]{0,1:T(2,128)}, u32[]{:S(2)}) copy-start(s32[127,2]{0,1:T(2,128)} %param.6) | copy-start | bytes 3052
  187.0 8.0 %collective-permute-start = (bf16[24,32,128]{2,1,0:T(8,128)(2,1)S(1)}, bf16[24,32,128]{2,1,0:T(8,128)(2,1)S(1)}, u32[]{:S(2)}, u32[]{:S(2)}) collective-permute-start(bf16[24,32,128]{2,1,0:T(8,128)(2,1)S(1)} %get-tuple-element.43), channel_id=1, source_target_pairs={{0,64},{64,128},{128,192},{192,0},{1,65},{65,129},{129,193},{193,1... | collective-permute-start | bytes 589832 | tf_op jit(solution)/shard_map/ppermute | solution.py:364
  188.6 11.5 %collective-permute-start.1 = (bf16[24,32,128]{2,1,0:T(8,128)(2,1)S(1)}, bf16[24,32,128]{2,1,0:T(8,128)(2,1)S(1)}, u32[]{:S(2)}, u32[]{:S(2)}) collective-permute-start(bf16[24,32,128]{2,1,0:T(8,128)(2,1)S(1)} %get-tuple-element.44), channel_id=1, source_target_pairs={{0,128},{64,192},{128,0},{192,64},{1,129},{65,193},{129,1},{193,65... | collective-permute-start | bytes 589832 | tf_op jit(solution)/shard_map/ppermute | solution.py:364
  191.5 8.6 %collective-permute-start.2 = (bf16[24,32,128]{2,1,0:T(8,128)(2,1)S(1)}, bf16[24,32,128]{2,1,0:T(8,128)(2,1)S(1)}, u32[]{:S(2)}, u32[]{:S(2)}) collective-permute-start(bf16[24,32,128]{2,1,0:T(8,128)(2,1)S(1)} %get-tuple-element.45), channel_id=1, source_target_pairs={{0,192},{64,0},{128,64},{192,128},{1,193},{65,1},{129,65},{193,129... | collective-permute-start | bytes 589832 | tf_op jit(solution)/shard_map/ppermute | solution.py:364
  200.2 15.5 %collective-permute-start.3 = (bf16[12,32,128]{2,1,0:T(8,128)(2,1)S(1)}, bf16[12,32,128]{2,1,0:T(8,128)(2,1)S(1)}, u32[]{:S(2)}, u32[]{:S(2)}) collective-permute-start(bf16[12,32,128]{2,1,0:T(8,128)(2,1)S(1)} %get-tuple-element.47), channel_id=1, source_target_pairs={{0,8},{1,9},{2,10},{3,11},{4,12},{5,13},{6,14},{7,15},{8,0},{9,1},... | collective-permute-start | bytes 294920 | tf_op jit(solution)/shard_map/ppermute | solution.py:462
  204.6 11.1 %collective-permute-start.6 = (f32[128,128]{1,0:T(8,128)S(1)}, f32[128,128]{1,0:T(8,128)S(1)}, u32[]{:S(2)}, u32[]{:S(2)}) collective-permute-start(f32[128,128]{1,0:T(8,128)S(1)} %get-tuple-element.48), channel_id=1, source_target_pairs={{1,0},{2,1},{3,2},{4,3},{5,4},{6,5},{7,6},{9,8},{10,9},{11,10},{12... | collective-permute-start | bytes 196616 | tf_op jit(solution)/shard_map/ppermute | solution.py:479
  206.5 9.2 %collective-permute-start.7 = (f32[128,128]{1,0:T(8,128)S(1)}, f32[128,128]{1,0:T(8,128)S(1)}, u32[]{:S(2)}, u32[]{:S(2)}) collective-permute-start(f32[128,128]{1,0:T(8,128)S(1)} %get-tuple-element.49), channel_id=1, source_target_pairs={{0,1},{1,2},{2,3},{3,4},{4,5},{5,6},{6,7},{8,9},{9,10},{10,11},{11... | collective-permute-start | bytes 196616 | tf_op jit(solution)/shard_map/ppermute | solution.py:480
  222.7 8.1 %collective-permute-start.8 = (bf16[12,32,128]{2,1,0:T(8,128)(2,1)S(1)}, bf16[12,32,128]{2,1,0:T(8,128)(2,1)S(1)}, u32[]{:S(2)}, u32[]{:S(2)}) collective-permute-start(bf16[12,32,128]{2,1,0:T(8,128)(2,1)S(1)} %get-tuple-element.56), channel_id=1, source_target_pairs={{0,64},{1,65},{2,66},{3,67},{4,68},{5,69},{6,70},{7,71},{8,72},{9,... | collective-permute-start | bytes 294920 | tf_op jit(solution)/shard_map/ppermute | solution.py:462
  224.3 7.3 %collective-permute-start.9 = (bf16[12,32,128]{2,1,0:T(8,128)(2,1)S(1)}, bf16[12,32,128]{2,1,0:T(8,128)(2,1)S(1)}, u32[]{:S(2)}, u32[]{:S(2)}) collective-permute-start(bf16[12,32,128]{2,1,0:T(8,128)(2,1)S(1)} %get-tuple-element.57), channel_id=1, source_target_pairs={{0,128},{1,129},{2,130},{3,131},{4,132},{5,133},{6,134},{7,135},{8... | collective-permute-start | bytes 294920 | tf_op jit(solution)/shard_map/ppermute | solution.py:462
  227.2 6.9 %collective-permute-start.10 = (bf16[12,32,128]{2,1,0:T(8,128)(2,1)S(1)}, bf16[12,32,128]{2,1,0:T(8,128)(2,1)S(1)}, u32[]{:S(2)}, u32[]{:S(2)}) collective-permute-start(bf16[12,32,128]{2,1,0:T(8,128)(2,1)S(1)} %get-tuple-element.58), channel_id=1, source_target_pairs={{0,192},{1,193},{2,194},{3,195},{4,196},{5,197},{6,198},{7,199},{8... | collective-permute-start | bytes 294920 | tf_op jit(solution)/shard_map/ppermute | solution.py:462
  228.6 5.5 %collective-permute-start.11 = (bf16[12,32,128]{2,1,0:T(8,128)(2,1)S(1)}, bf16[12,32,128]{2,1,0:T(8,128)(2,1)S(1)}, u32[]{:S(2)}, u32[]{:S(2)}) collective-permute-start(bf16[12,32,128]{2,1,0:T(8,128)(2,1)S(1)} %get-tuple-element.59), channel_id=1, source_target_pairs={{0,8},{1,9},{2,10},{3,11},{4,12},{5,13},{6,14},{7,15},{8,0},{9,1},... | collective-permute-start | bytes 294920 | tf_op jit(solution)/shard_map/ppermute | solution.py:462
  229.2 7.9 %collective-permute-start.12 = (bf16[12,32,128]{2,1,0:T(8,128)(2,1)S(1)}, bf16[12,32,128]{2,1,0:T(8,128)(2,1)S(1)}, u32[]{:S(2)}, u32[]{:S(2)}) collective-permute-start(bf16[12,32,128]{2,1,0:T(8,128)(2,1)S(1)} %get-tuple-element.60), channel_id=1, source_target_pairs={{0,72},{1,73},{2,74},{3,75},{4,76},{5,77},{6,78},{7,79},{8,64},{9,... | collective-permute-start | bytes 294920 | tf_op jit(solution)/shard_map/ppermute | solution.py:462
  230.7 7.2 %collective-permute-start.13 = (bf16[12,32,128]{2,1,0:T(8,128)(2,1)S(1)}, bf16[12,32,128]{2,1,0:T(8,128)(2,1)S(1)}, u32[]{:S(2)}, u32[]{:S(2)}) collective-permute-start(bf16[12,32,128]{2,1,0:T(8,128)(2,1)S(1)} %get-tuple-element.61), channel_id=1, source_target_pairs={{0,136},{1,137},{2,138},{3,139},{4,140},{5,141},{6,142},{7,143},{8... | collective-permute-start | bytes 294920 | tf_op jit(solution)/shard_map/ppermute | solution.py:462
  231.6 7.1 %collective-permute-start.14 = (bf16[12,32,128]{2,1,0:T(8,128)(2,1)S(1)}, bf16[12,32,128]{2,1,0:T(8,128)(2,1)S(1)}, u32[]{:S(2)}, u32[]{:S(2)}) collective-permute-start(bf16[12,32,128]{2,1,0:T(8,128)(2,1)S(1)} %get-tuple-element.62), channel_id=1, source_target_pairs={{0,200},{1,201},{2,202},{3,203},{4,204},{5,205},{6,206},{7,207},{8... | collective-permute-start | bytes 294920 | tf_op jit(solution)/shard_map/ppermute | solution.py:462
  238.8 7.5 %collective-permute-start.17 = (f32[32,640]{1,0:T(8,128)S(1)}, f32[32,640]{1,0:T(8,128)S(1)}, u32[]{:S(2)}, u32[]{:S(2)}) collective-permute-start(f32[32,640]{1,0:T(8,128)S(1)} %get-tuple-element.66), channel_id=1, source_target_pairs={{0,48},{1,49},{2,50},{3,51},{4,52},{5,53},{6,54},{7,55},{8,56},{9,... | collective-permute-start | bytes 245768 | tf_op jit(solution)/shard_map/ppermute | solution.py:488
  239.4 8.9 %collective-permute-start.16 = (f32[32,640]{1,0:T(8,128)S(1)}, f32[32,640]{1,0:T(8,128)S(1)}, u32[]{:S(2)}, u32[]{:S(2)}) collective-permute-start(f32[32,640]{1,0:T(8,128)S(1)} %get-tuple-element.65), channel_id=1, source_target_pairs={{0,32},{1,33},{2,34},{3,35},{4,36},{5,37},{6,38},{7,39},{8,40},{9,... | collective-permute-start | bytes 245768 | tf_op jit(solution)/shard_map/ppermute | solution.py:488
  242.8 7.8 %collective-permute-start.15 = (f32[32,640]{1,0:T(8,128)S(1)}, f32[32,640]{1,0:T(8,128)S(1)}, u32[]{:S(2)}, u32[]{:S(2)}) collective-permute-start(f32[32,640]{1,0:T(8,128)S(1)} %get-tuple-element.64), channel_id=1, source_target_pairs={{0,16},{1,17},{2,18},{3,19},{4,20},{5,21},{6,22},{7,23},{8,24},{9,... | collective-permute-start | bytes 245768 | tf_op jit(solution)/shard_map/ppermute | solution.py:488
  250.6 12.6 %collective-permute-start.18 = (f32[1,32,640]{2,1,0:T(8,128)S(1)}, f32[1,32,640]{2,1,0:T(8,128)S(1)}, u32[]{:S(2)}, u32[]{:S(2)}) collective-permute-start(f32[1,32,640]{2,1,0:T(8,128)S(1)} %multiply_bitcast_fusion), channel_id=1, source_target_pairs={{0,0},{1,8},{2,16},{3,24},{4,32},{5,40},{6,48},{7,56},{8,1},{9,9},... | collective-permute-start | bytes 245768 | tf_op jit(solution)/shard_map/ppermute | solution.py:490
  (4 other events, 70.7 us)

commit v7 on v5

--- a/solution.py
+++ b/solution.py
@@ -131,7 +131,7 @@
             turned_ref[i, pl.ds(at, 32), :] = turned[i * 32 : (i + 1) * 32]
         return carry
 
-    lax.fori_loop(first, first + count, turn, 0, unroll=4)
+    lax.fori_loop(first, first + count, turn, 0, unroll=8)
 
 
 def fit_one(metric_ref, turned_ref, mask_ref, i):
@@ -264,8 +264,8 @@
 def late_kernel(y_ref, mask_ref, rows_hbm, f1_hbm, f2_hbm, f5_hbm, f6_hbm, perm_ref, metric_ref, from_below, from_above, edges, own_ref, *rest):
     outs, (rows_ref, turned_ref, left_ref, right_ref, tiles_ref, flip_ref, row_sems, sems) = rest[:7], rest[7:]
     feeds = []
-    for n in range(4):
-        piece = pl.ds(n * 1024, 1024)
+    for n in range(2):
+        piece = pl.ds(n * 2048, 2048)
         feeds.append(pltpu.make_async_copy(rows_hbm.at[piece], rows_ref.at[piece], row_sems.at[n]))
     fits = [
         pltpu.make_async_copy(f, right_ref.at[n], sems.at[n]) for n, f in enumerate((f1_hbm, f2_hbm, f5_hbm, f6_hbm))
@@ -274,7 +274,7 @@
         copy.start()
     for n, feed in enumerate(feeds):
         feed.wait()
-        turn_rows((rows_ref,), perm_ref, turned_ref, 4 * n, 4)
+        turn_rows((rows_ref,), perm_ref, turned_ref, 8 * n, 8)
 
     def step(i, carry):
         at = pl.ds(pl.multiple_of(i * 512, 512), 512)

time: 265 us -> 265 us (level)
  no operation moved by 1% of the time
where the time goes in v7:
time: 265 us; the launch traced here: 264 us
  waiting for transfers between devices  170 us (64%)
  starting transfers between devices  57 us (22%)
  Pallas kernels  35 us (13%)
    all_to_all x2, waiting for transfers between devices, spread(): lax.all_to_all(cut_chunk(source, blocks), 'blk', split_axis=0, concat_axi...  144 us
    all_to_all x2, starting transfers between devices, spread(): lax.all_to_all(cut_chunk(source, blocks), 'blk', split_axis=0, concat_axi...  18 us
    pallas_call x3, Pallas kernels, fit_chunk(): pl.pallas_call(fit_kernel, grid=(1,), out_shape=[jax.ShapeDtypeStruct((40...  13.7 us
    ppermute x8, starting transfers between devices, move(): return lax.ppermute(array, AXES, pairs)  12.8 us
    pallas_call x2, Pallas kernels, cut_chunk(): pl.pallas_call(lambda *refs: cut_kernel(*refs, blocks=blocks), out_shape=...  7.74 us
    ppermute x1, waiting for transfers between devices, local(): lax.ppermute(total, 'blk', [(zz * NC + cc, cc * NC + zz) for zz, cc in gr...  7.71 us
    ppermute x3, waiting for transfers between devices, over_domains(): lax.ppermute(s, 'aux', [(a, (a + d) % NY) for a in range(NY)])  7.2 us
    pallas_call x1, Pallas kernels, late_tiles(): pl.pallas_call(late_kernel, out_shape=[jax.ShapeDtypeStruct((LATE_HALF, P...  7.13 us
  transfers between devices with their start and end apart: 21, of which 11 were waited for; matrix products, arithmetic and copies ran while one was open for 0% of the time, Pallas kernels for 9%

profile of v7, /device:TPU:4, one launch (start us, length us, event | category | flops | bytes accessed | tf_op | source)
XLA Modules:
  0.0 264.1 jit_solution(5367398708249810855)
XLA Ops:
  0.0 4.9 %cut_chunk.2 = bf16[64,8,8,768]{3,2,1,0:T(8,128)(2,1)} custom-call(bf16[8,8,8,8192]{3,2,1,0:T(8,128)(2,1)} %bitcast.14), custom_call_target="tpu_custom_call" | custom-call | bytes 12582912 | tf_op jit(solution)/shard_map/cut_chunk/pallas_call | solution.py:111
  4.9 12.2 %all-to-all-start = ((bf16[64,8,8,768]{3,2,1,0:T(8,128)(2,1)}), bf16[64,8,8,768]{3,2,1,0:T(8,128)(2,1)}, u32[]{:S(2)}, u32[]{:S(2)}) async-start(bf16[64,8,8,768]{3,2,1,0:T(8,128)(2,1)} %cut_chunk.2), calls=%async_computation | async-start | bytes 12582912 | tf_op jit(solution)/shard_map/all_to_all | solution.py:465
  17.1 2.8 %cut_chunk.3 = bf16[64,8,8,256]{3,2,1,0:T(8,128)(2,1)} custom-call(bf16[8,8,8,8192]{3,2,1,0:T(8,128)(2,1)} %bitcast.15), custom_call_target="tpu_custom_call" | custom-call | bytes 4194304 | tf_op jit(solution)/shard_map/cut_chunk/pallas_call | solution.py:111
  20.0 138.4 %all-to-all-done = bf16[64,8,8,768]{3,2,1,0:T(8,128)(2,1)} async-done(((bf16[64,8,8,768]{3,2,1,0:T(8,128)(2,1)}), bf16[64,8,8,768]{3,2,1,0:T(8,128)(2,1)}, u32[]{:S(2)}, u32[]{:S(2)}) %all-to-all-start) | async-done | bytes 6291488 | tf_op jit(solution)/shard_map/all_to_all | solution.py:465
  158.3 5.8 %all-to-all-start.1 = ((bf16[64,8,8,256]{3,2,1,0:T(8,128)(2,1)}), bf16[64,8,8,256]{3,2,1,0:T(8,128)(2,1)}, u32[]{:S(2)}, u32[]{:S(2)}) async-start(bf16[64,8,8,256]{3,2,1,0:T(8,128)(2,1)} %cut_chunk.3), calls=%async_computation.1 | async-start | bytes 4194304 | tf_op jit(solution)/shard_map/all_to_all | solution.py:465
  164.8 4.3 %fit_chunk.3 = (bf16[4096,128]{1,0:T(8,128)(2,1)S(1)}, bf16[4096,128]{1,0:T(8,128)(2,1)S(1)}) custom-call(bf16[4096,768]{1,0:T(8,128)(2,1)} %bitcast.4.rows_a.rows_b, bf16[4096,768]{1,0:T(8,128)(2,1)} %bitcast.4.rows_a.rows_b, bf16[256,256]{1,0:T(8,128)(2,1)S(1)} %fusion.1.perm_ref, bf16[512,512]{1,0:T(8,128)(2,1)S(1)} %copy-done, ...), custom_call_target="tpu_custom_call" | custom-call | flops 1610612736 | bytes 4194304 | tf_op jit(solution)/shard_map/fit_chunk/pallas_call | solution.py:163
  171.2 3.5 %collective-permute-start.5 = (bf16[4096,128]{1,0:T(8,128)(2,1)S(1)}, bf16[4096,128]{1,0:T(8,128)(2,1)}, u32[]{:S(2)}, u32[]{:S(2)}) collective-permute-start(bf16[4096,128]{1,0:T(8,128)(2,1)S(1)} %get-tuple-element.36.refs_0_.f0), channel_id=1, source_target_pairs={{1,0},{2,1},{3,2},{4,3},{5,4},{6,5},{7,6},{9,8},{10,9},{11,10},{12... | collective-permute-start | bytes 3145736 | tf_op jit(solution)/shard_map/ppermute | solution.py:471
  174.9 4.3 %fit_chunk.4 = (bf16[4096,128]{1,0:T(8,128)(2,1)S(1)}, bf16[4096,128]{1,0:T(8,128)(2,1)S(1)}) custom-call(bf16[4096,768]{1,0:T(8,128)(2,1)} %bitcast.4.rows_a.rows_b, bf16[4096,768]{1,0:T(8,128)(2,1)} %bitcast.4.rows_a.rows_b, bf16[256,256]{1,0:T(8,128)(2,1)S(1)} %fusion.1.perm_ref, bf16[512,512]{1,0:T(8,128)(2,1)S(1)} %copy-done, ...), custom_call_target="tpu_custom_call" | custom-call | flops 1610612736 | bytes 4194304 | tf_op jit(solution)/shard_map/fit_chunk/pallas_call | solution.py:163
  179.2 5.1 %fit_chunk.5 = (bf16[4096,128]{1,0:T(8,128)(2,1)S(1)}, bf16[4096,128]{1,0:T(8,128)(2,1)S(1)}) custom-call(bf16[4096,768]{1,0:T(8,128)(2,1)} %bitcast.4.rows_a.rows_b, bf16[4096,768]{1,0:T(8,128)(2,1)} %bitcast.4.rows_a.rows_b, bf16[256,256]{1,0:T(8,128)(2,1)S(1)} %fusion.1.perm_ref, bf16[512,512]{1,0:T(8,128)(2,1)S(1)} %copy-done, ...), custom_call_target="tpu_custom_call" | custom-call | flops 1610612736 | bytes 4194304 | tf_op jit(solution)/shard_map/fit_chunk/pallas_call | solution.py:163
  184.3 3.6 %early_tiles.1 = (f32[18,32,128]{2,1,0:T(8,128)S(1)}, bf16[24,32,128]{2,1,0:T(8,128)(2,1)S(1)}, bf16[24,32,128]{2,1,0:T(8,128)(2,1)S(1)}, bf16[24,32,128]{2,1,0:T(8,128)(2,1)S(1)}) custom-call(s32[2]{0:T(128)S(1)} %pad_add_fusion.y_ref, bf16[4096,128]{1,0:T(8,128)(2,1)S(1)} %get-tuple-element.36.refs_0_.f0, ...), custom_call_target="tpu_custom_call" | custom-call | flops 2147483648 | bytes 7340032 | tf_op jit(solution)/shard_map/early_tiles/pallas_call | solution.py:321
  189.6 2.9 %collective-permute-start.1 = (bf16[24,32,128]{2,1,0:T(8,128)(2,1)S(1)}, bf16[24,32,128]{2,1,0:T(8,128)(2,1)S(1)}, u32[]{:S(2)}, u32[]{:S(2)}) collective-permute-start(bf16[24,32,128]{2,1,0:T(8,128)(2,1)S(1)} %get-tuple-element.44), channel_id=1, source_target_pairs={{0,128},{64,192},{128,0},{192,64},{1,129},{65,193},{129,1},{193,65... | collective-permute-start | bytes 589832 | tf_op jit(solution)/shard_map/ppermute | solution.py:364
  193.9 2.1 collective-permute-done.g1
  196.0 5.1 %collective-permute-done.1.g2 = bf16[24,32,128]{2,1,0:T(8,128)(2,1)S(1)} collective-permute-done((bf16[24,32,128]{2,1,0:T(8,128)(2,1)S(1)}, bf16[24,32,128]{2,1,0:T(8,128)(2,1)S(1)}, u32[]{:S(2)}, u32[]{:S(2)}) %collective-permute-start.1) | collective-permute-done | bytes 196640 | tf_op jit(solution)/shard_map/ppermute | solution.py:364
  202.8 2.6 edge_tiles.1
  207.3 2.6 collective-permute-start.7
  209.9 5.7 %all-to-all-done.1 = bf16[64,8,8,256]{3,2,1,0:T(8,128)(2,1)} async-done(((bf16[64,8,8,256]{3,2,1,0:T(8,128)(2,1)}), bf16[64,8,8,256]{3,2,1,0:T(8,128)(2,1)}, u32[]{:S(2)}, u32[]{:S(2)}) %all-to-all-start.1) | async-done | bytes 2097184 | tf_op jit(solution)/shard_map/all_to_all | solution.py:465
  215.7 7.1 %late_tiles.1 = (f32[11,32,128]{2,1,0:T(8,128)S(1)}, bf16[12,32,128]{2,1,0:T(8,128)(2,1)S(1)}, bf16[12,32,128]{2,1,0:T(8,128)(2,1)S(1)}, bf16[12,32,128]{2,1,0:T...) custom-call(s32[2]{0:T(128)S(1)} %pad_add_fusion.y_ref, ...), custom_call_target="tpu_custom_call" | custom-call | flops 3221225472 | bytes 8388608 | tf_op jit(solution)/shard_map/late_tiles/pallas_call | solution.py:339
  224.5 2.9 %collective-permute-start.9 = (bf16[12,32,128]{2,1,0:T(8,128)(2,1)S(1)}, bf16[12,32,128]{2,1,0:T(8,128)(2,1)S(1)}, u32[]{:S(2)}, u32[]{:S(2)}) collective-permute-start(bf16[12,32,128]{2,1,0:T(8,128)(2,1)S(1)} %get-tuple-element.57), channel_id=1, source_target_pairs={{0,128},{1,129},{2,130},{3,131},{4,132},{5,133},{6,134},{7,135},{8... | collective-permute-start | bytes 294920 | tf_op jit(solution)/shard_map/ppermute | solution.py:462
  231.8 2.3 collective-permute-start.14
  234.3 3.0 %collective-permute-done.12.rest_4_ = bf16[12,32,128]{2,1,0:T(8,128)(2,1)S(1)} collective-permute-done((bf16[12,32,128]{2,1,0:T(8,128)(2,1)S(1)}, bf16[12,32,128]{2,1,0:T(8,128)(2,1)S(1)}, u32[]{:S(2)}, u32[]{:S(2)}) %collective-permute-start.12) | collective-permute-done | bytes 98336 | tf_op jit(solution)/shard_map/ppermute | solution.py:462
  239.5 3.4 %collective-permute-start.16 = (f32[32,640]{1,0:T(8,128)S(1)}, f32[32,640]{1,0:T(8,128)S(1)}, u32[]{:S(2)}, u32[]{:S(2)}) collective-permute-start(f32[32,640]{1,0:T(8,128)S(1)} %get-tuple-element.65), channel_id=1, source_target_pairs={{0,32},{1,33},{2,34},{3,35},{4,36},{5,37},{6,38},{7,39},{8,40},{9,... | collective-permute-start | bytes 245768 | tf_op jit(solution)/shard_map/ppermute | solution.py:488
  248.5 2.3 collective-permute-done.15
  250.8 4.9 %collective-permute-start.18 = (f32[1,32,640]{2,1,0:T(8,128)S(1)}, f32[1,32,640]{2,1,0:T(8,128)S(1)}, u32[]{:S(2)}, u32[]{:S(2)}) collective-permute-start(f32[1,32,640]{2,1,0:T(8,128)S(1)} %multiply_bitcast_fusion), channel_id=1, source_target_pairs={{0,0},{1,8},{2,16},{3,24},{4,32},{5,40},{6,48},{7,56},{8,1},{9,9},... | collective-permute-start | bytes 245768 | tf_op jit(solution)/shard_map/ppermute | solution.py:490
  255.7 7.7 %collective-permute-done.18 = f32[1,32,640]{2,1,0:T(8,128)S(1)} collective-permute-done((f32[1,32,640]{2,1,0:T(8,128)S(1)}, f32[1,32,640]{2,1,0:T(8,128)S(1)}, u32[]{:S(2)}, u32[]{:S(2)}) %collective-permute-start.18) | collective-permute-done | bytes 81952 | tf_op jit(solution)/shard_map/ppermute | solution.py:490
  (60 shorter events, 24.1 us)
Async XLA Ops:
  4.9 153.4 %all-to-all-start = ((bf16[64,8,8,768]{3,2,1,0:T(8,128)(2,1)}), bf16[64,8,8,768]{3,2,1,0:T(8,128)(2,1)}, u32[]{:S(2)}, u32[]{:S(2)}) async-start(bf16[64,8,8,768]{3,2,1,0:T(8,128)(2,1)} %cut_chunk.2), calls=%async_computation | async-start | bytes 12582912 | tf_op jit(solution)/shard_map/all_to_all | solution.py:465
  17.1 147.1 %copy-start.5 = (s32[4,64]{1,0:T(4,128)S(1)}, s32[4,64]{1,0:T(4,128)}, u32[]{:S(2)}) copy-start(s32[4,64]{1,0:T(4,128)} %param.7) | copy-start | bytes 3076
  17.1 147.6 %copy-start = (bf16[512,512]{1,0:T(8,128)(2,1)S(1)}, bf16[512,512]{1,0:T(8,128)(2,1)}, u32[]{:S(2)}) copy-start(bf16[512,512]{1,0:T(8,128)(2,1)} %metric_ref.7) | copy-start | bytes 1572868
  158.3 57.4 %all-to-all-start.1 = ((bf16[64,8,8,256]{3,2,1,0:T(8,128)(2,1)}), bf16[64,8,8,256]{3,2,1,0:T(8,128)(2,1)}, u32[]{:S(2)}, u32[]{:S(2)}) async-start(bf16[64,8,8,256]{3,2,1,0:T(8,128)(2,1)} %cut_chunk.3), calls=%async_computation.1 | async-start | bytes 4194304 | tf_op jit(solution)/shard_map/all_to_all | solution.py:465
  169.1 33.6 %collective-permute-start.4 = (bf16[4096,128]{1,0:T(8,128)(2,1)S(1)}, bf16[4096,128]{1,0:T(8,128)(2,1)}, u32[]{:S(2)}, u32[]{:S(2)}) collective-permute-start(bf16[4096,128]{1,0:T(8,128)(2,1)S(1)} %get-tuple-element.41.refs_5_.f7), channel_id=1, source_target_pairs={{0,1},{1,2},{2,3},{3,4},{4,5},{5,6},{6,7},{8,9},{9,10},{10,11},{11... | collective-permute-start | bytes 3145736 | tf_op jit(solution)/shard_map/ppermute | solution.py:472
  171.2 31.6 %collective-permute-start.5 = (bf16[4096,128]{1,0:T(8,128)(2,1)S(1)}, bf16[4096,128]{1,0:T(8,128)(2,1)}, u32[]{:S(2)}, u32[]{:S(2)}) collective-permute-start(bf16[4096,128]{1,0:T(8,128)(2,1)S(1)} %get-tuple-element.36.refs_0_.f0), channel_id=1, source_target_pairs={{1,0},{2,1},{3,2},{4,3},{5,4},{6,5},{7,6},{9,8},{10,9},{11,10},{12... | collective-permute-start | bytes 3145736 | tf_op jit(solution)/shard_map/ppermute | solution.py:471
  184.3 25.6 %copy-start.6 = (s32[127,2]{0,1:T(2,128)S(1)}, s32[127,2]{0,1:T(2,128)}, u32[]{:S(2)}) copy-start(s32[127,2]{0,1:T(2,128)} %param.6) | copy-start | bytes 3052
  188.0 8.0 %collective-permute-start = (bf16[24,32,128]{2,1,0:T(8,128)(2,1)S(1)}, bf16[24,32,128]{2,1,0:T(8,128)(2,1)S(1)}, u32[]{:S(2)}, u32[]{:S(2)}) collective-permute-start(bf16[24,32,128]{2,1,0:T(8,128)(2,1)S(1)} %get-tuple-element.43), channel_id=1, source_target_pairs={{0,64},{64,128},{128,192},{192,0},{1,65},{65,129},{129,193},{193,1... | collective-permute-start | bytes 589832 | tf_op jit(solution)/shard_map/ppermute | solution.py:364
  189.6 11.5 %collective-permute-start.1 = (bf16[24,32,128]{2,1,0:T(8,128)(2,1)S(1)}, bf16[24,32,128]{2,1,0:T(8,128)(2,1)S(1)}, u32[]{:S(2)}, u32[]{:S(2)}) collective-permute-start(bf16[24,32,128]{2,1,0:T(8,128)(2,1)S(1)} %get-tuple-element.44), channel_id=1, source_target_pairs={{0,128},{64,192},{128,0},{192,64},{1,129},{65,193},{129,1},{193,65... | collective-permute-start | bytes 589832 | tf_op jit(solution)/shard_map/ppermute | solution.py:364
  192.5 8.5 %collective-permute-start.2 = (bf16[24,32,128]{2,1,0:T(8,128)(2,1)S(1)}, bf16[24,32,128]{2,1,0:T(8,128)(2,1)S(1)}, u32[]{:S(2)}, u32[]{:S(2)}) collective-permute-start(bf16[24,32,128]{2,1,0:T(8,128)(2,1)S(1)} %get-tuple-element.45), channel_id=1, source_target_pairs={{0,192},{64,0},{128,64},{192,128},{1,193},{65,1},{129,65},{193,129... | collective-permute-start | bytes 589832 | tf_op jit(solution)/shard_map/ppermute | solution.py:364
  201.2 14.5 %collective-permute-start.3 = (bf16[12,32,128]{2,1,0:T(8,128)(2,1)S(1)}, bf16[12,32,128]{2,1,0:T(8,128)(2,1)S(1)}, u32[]{:S(2)}, u32[]{:S(2)}) collective-permute-start(bf16[12,32,128]{2,1,0:T(8,128)(2,1)S(1)} %get-tuple-element.47), channel_id=1, source_target_pairs={{0,8},{1,9},{2,10},{3,11},{4,12},{5,13},{6,14},{7,15},{8,0},{9,1},... | collective-permute-start | bytes 294920 | tf_op jit(solution)/shard_map/ppermute | solution.py:462
  205.4 10.3 %collective-permute-start.6 = (f32[128,128]{1,0:T(8,128)S(1)}, f32[128,128]{1,0:T(8,128)S(1)}, u32[]{:S(2)}, u32[]{:S(2)}) collective-permute-start(f32[128,128]{1,0:T(8,128)S(1)} %get-tuple-element.48), channel_id=1, source_target_pairs={{1,0},{2,1},{3,2},{4,3},{5,4},{6,5},{7,6},{9,8},{10,9},{11,10},{12... | collective-permute-start | bytes 196616 | tf_op jit(solution)/shard_map/ppermute | solution.py:479
  207.3 8.4 %collective-permute-start.7 = (f32[128,128]{1,0:T(8,128)S(1)}, f32[128,128]{1,0:T(8,128)S(1)}, u32[]{:S(2)}, u32[]{:S(2)}) collective-permute-start(f32[128,128]{1,0:T(8,128)S(1)} %get-tuple-element.49), channel_id=1, source_target_pairs={{0,1},{1,2},{2,3},{3,4},{4,5},{5,6},{6,7},{8,9},{9,10},{10,11},{11... | collective-permute-start | bytes 196616 | tf_op jit(solution)/shard_map/ppermute | solution.py:480
  222.8 8.1 %collective-permute-start.8 = (bf16[12,32,128]{2,1,0:T(8,128)(2,1)S(1)}, bf16[12,32,128]{2,1,0:T(8,128)(2,1)S(1)}, u32[]{:S(2)}, u32[]{:S(2)}) collective-permute-start(bf16[12,32,128]{2,1,0:T(8,128)(2,1)S(1)} %get-tuple-element.56), channel_id=1, source_target_pairs={{0,64},{1,65},{2,66},{3,67},{4,68},{5,69},{6,70},{7,71},{8,72},{9,... | collective-permute-start | bytes 294920 | tf_op jit(solution)/shard_map/ppermute | solution.py:462
  224.5 7.3 %collective-permute-start.9 = (bf16[12,32,128]{2,1,0:T(8,128)(2,1)S(1)}, bf16[12,32,128]{2,1,0:T(8,128)(2,1)S(1)}, u32[]{:S(2)}, u32[]{:S(2)}) collective-permute-start(bf16[12,32,128]{2,1,0:T(8,128)(2,1)S(1)} %get-tuple-element.57), channel_id=1, source_target_pairs={{0,128},{1,129},{2,130},{3,131},{4,132},{5,133},{6,134},{7,135},{8... | collective-permute-start | bytes 294920 | tf_op jit(solution)/shard_map/ppermute | solution.py:462
  227.4 6.9 %collective-permute-start.10 = (bf16[12,32,128]{2,1,0:T(8,128)(2,1)S(1)}, bf16[12,32,128]{2,1,0:T(8,128)(2,1)S(1)}, u32[]{:S(2)}, u32[]{:S(2)}) collective-permute-start(bf16[12,32,128]{2,1,0:T(8,128)(2,1)S(1)} %get-tuple-element.58), channel_id=1, source_target_pairs={{0,192},{1,193},{2,194},{3,195},{4,196},{5,197},{6,198},{7,199},{8... | collective-permute-start | bytes 294920 | tf_op jit(solution)/shard_map/ppermute | solution.py:462
  228.7 5.5 %collective-permute-start.11 = (bf16[12,32,128]{2,1,0:T(8,128)(2,1)S(1)}, bf16[12,32,128]{2,1,0:T(8,128)(2,1)S(1)}, u32[]{:S(2)}, u32[]{:S(2)}) collective-permute-start(bf16[12,32,128]{2,1,0:T(8,128)(2,1)S(1)} %get-tuple-element.59), channel_id=1, source_target_pairs={{0,8},{1,9},{2,10},{3,11},{4,12},{5,13},{6,14},{7,15},{8,0},{9,1},... | collective-permute-start | bytes 294920 | tf_op jit(solution)/shard_map/ppermute | solution.py:462
  229.3 7.9 %collective-permute-start.12 = (bf16[12,32,128]{2,1,0:T(8,128)(2,1)S(1)}, bf16[12,32,128]{2,1,0:T(8,128)(2,1)S(1)}, u32[]{:S(2)}, u32[]{:S(2)}) collective-permute-start(bf16[12,32,128]{2,1,0:T(8,128)(2,1)S(1)} %get-tuple-element.60), channel_id=1, source_target_pairs={{0,72},{1,73},{2,74},{3,75},{4,76},{5,77},{6,78},{7,79},{8,64},{9,... | collective-permute-start | bytes 294920 | tf_op jit(solution)/shard_map/ppermute | solution.py:462
  230.9 7.2 %collective-permute-start.13 = (bf16[12,32,128]{2,1,0:T(8,128)(2,1)S(1)}, bf16[12,32,128]{2,1,0:T(8,128)(2,1)S(1)}, u32[]{:S(2)}, u32[]{:S(2)}) collective-permute-start(bf16[12,32,128]{2,1,0:T(8,128)(2,1)S(1)} %get-tuple-element.61), channel_id=1, source_target_pairs={{0,136},{1,137},{2,138},{3,139},{4,140},{5,141},{6,142},{7,143},{8... | collective-permute-start | bytes 294920 | tf_op jit(solution)/shard_map/ppermute | solution.py:462
  231.8 7.1 %collective-permute-start.14 = (bf16[12,32,128]{2,1,0:T(8,128)(2,1)S(1)}, bf16[12,32,128]{2,1,0:T(8,128)(2,1)S(1)}, u32[]{:S(2)}, u32[]{:S(2)}) collective-permute-start(bf16[12,32,128]{2,1,0:T(8,128)(2,1)S(1)} %get-tuple-element.62), channel_id=1, source_target_pairs={{0,200},{1,201},{2,202},{3,203},{4,204},{5,205},{6,206},{7,207},{8... | collective-permute-start | bytes 294920 | tf_op jit(solution)/shard_map/ppermute | solution.py:462
  239.0 7.5 %collective-permute-start.17 = (f32[32,640]{1,0:T(8,128)S(1)}, f32[32,640]{1,0:T(8,128)S(1)}, u32[]{:S(2)}, u32[]{:S(2)}) collective-permute-start(f32[32,640]{1,0:T(8,128)S(1)} %get-tuple-element.66), channel_id=1, source_target_pairs={{0,48},{1,49},{2,50},{3,51},{4,52},{5,53},{6,54},{7,55},{8,56},{9,... | collective-permute-start | bytes 245768 | tf_op jit(solution)/shard_map/ppermute | solution.py:488
  239.5 8.9 %collective-permute-start.16 = (f32[32,640]{1,0:T(8,128)S(1)}, f32[32,640]{1,0:T(8,128)S(1)}, u32[]{:S(2)}, u32[]{:S(2)}) collective-permute-start(f32[32,640]{1,0:T(8,128)S(1)} %get-tuple-element.65), channel_id=1, source_target_pairs={{0,32},{1,33},{2,34},{3,35},{4,36},{5,37},{6,38},{7,39},{8,40},{9,... | collective-permute-start | bytes 245768 | tf_op jit(solution)/shard_map/ppermute | solution.py:488
  242.9 7.8 %collective-permute-start.15 = (f32[32,640]{1,0:T(8,128)S(1)}, f32[32,640]{1,0:T(8,128)S(1)}, u32[]{:S(2)}, u32[]{:S(2)}) collective-permute-start(f32[32,640]{1,0:T(8,128)S(1)} %get-tuple-element.64), channel_id=1, source_target_pairs={{0,16},{1,17},{2,18},{3,19},{4,20},{5,21},{6,22},{7,23},{8,24},{9,... | collective-permute-start | bytes 245768 | tf_op jit(solution)/shard_map/ppermute | solution.py:488
  250.8 12.6 %collective-permute-start.18 = (f32[1,32,640]{2,1,0:T(8,128)S(1)}, f32[1,32,640]{2,1,0:T(8,128)S(1)}, u32[]{:S(2)}, u32[]{:S(2)}) collective-permute-start(f32[1,32,640]{2,1,0:T(8,128)S(1)} %multiply_bitcast_fusion), channel_id=1, source_target_pairs={{0,0},{1,8},{2,16},{3,24},{4,32},{5,40},{6,48},{7,56},{8,1},{9,9},... | collective-permute-start | bytes 245768 | tf_op jit(solution)/shard_map/ppermute | solution.py:490
  (4 other events, 70.9 us)
